TPU v7x, 32 devices: a whole 2x2x4 slice. The times are simulated.
32 devices in a mesh: dp: 32 (over z, y, x, core).
Axes of the slice: x: 2, y: 2, z: 4, core: 2. Of those that a mesh axis runs over, the one named last changes fastest.
Arguments:
- tokens: bfloat16 [65536, 512], P('dp'), may hold values from -6 to 6
- segment: int32 [65536], P('dp'), may hold values from 0 to 2, as said below
- counts: int32 [32], P('dp'), may hold values from 1024 to 2048, as said below
- memory: bfloat16 [20, 512], P(None, 'dp'), may hold values from -6 to 6
- w_query: bfloat16 [512, 512], P('dp'), may hold values from -0.375 to 0.375
- b_query: bfloat16 [512], P('dp'), may hold values from -3 to 3
- w_key: bfloat16 [512, 512], P('dp'), may hold values from -0.25 to 0.25
- w_value: bfloat16 [512, 512], P('dp'), may hold values from -0.25 to 0.25
- b_value: bfloat16 [512], P('dp'), may hold values from -3 to 3
- w_out: bfloat16 [512, 512], P('dp'), may hold values from -1 to 1
- b_out: bfloat16 [512], P('dp'), may hold values from -3 to 3
- gain_attn: bfloat16 [512], P('dp'), may hold values from 0.5 to 1.5
- shift_attn: bfloat16 [512], P('dp'), may hold values from -3 to 3
- w_up: bfloat16 [512, 2048], P('dp'), may hold values from -0.25 to 0.25
- b_up: bfloat16 [2048], P('dp'), may hold values from -3 to 3
- w_down: bfloat16 [2048, 512], P('dp'), may hold values from -0.125 to 0.125
- b_down: bfloat16 [512], P('dp'), may hold values from -3 to 3
- gain_ffn: bfloat16 [512], P('dp'), may hold values from 0.5 to 1.5
- shift_ffn: bfloat16 [512], P('dp'), may hold values from -3 to 3
- cotangent: bfloat16 [65536, 512], P('dp'), may hold values from -6 to 6
Outputs:
- output: bfloat16 [65536, 512], P('dp')
- grad_tokens: float32 [65536, 512], P('dp')
- grad_memory: float32 [20, 512], P(None, 'dp')
- grad_w_query: float32 [512, 512], P('dp')
- grad_b_query: float32 [512], P('dp')
- grad_w_key: float32 [512, 512], P('dp')
- grad_w_value: float32 [512, 512], P('dp')
- grad_b_value: float32 [512], P('dp')
- grad_w_out: float32 [512, 512], P('dp')
- grad_b_out: float32 [512], P('dp')
- grad_gain_attn: float32 [512], P('dp')
- grad_shift_attn: float32 [512], P('dp')
- grad_w_up: float32 [512, 2048], P('dp')
- grad_b_up: float32 [2048], P('dp')
- grad_w_down: float32 [2048, 512], P('dp')
- grad_b_down: float32 [512], P('dp')
- grad_gain_ffn: float32 [512], P('dp')
- grad_shift_ffn: float32 [512], P('dp')
Inputs may be any that keep to these rules, and one draw needn't show every extreme that they name: `segment`: within each device's 2048 slots the ids never fall and each id marks one sequence; every used sequence has 128 to 1024 slots; in every draw some device holds a used sequence of exactly 1024 tokens. Ids past a device's used count carry no meaning. `counts`: slots are used from the start of each device and end where a sequence ends; in every draw some device uses all 2048 and some device uses 1024.
All inputs are finite; a program needn't handle non-finite values.
Results may differ from a plain program's by a relative error of at most 0.015.
The roundings to bfloat16 on the way count: a program that leaves them out, or rounds other values in their place, can miss the bound.
Values may be sent and summed in bfloat16 or wider, within the bound.
A program may use at most 320 MiB of HBM per device.

v0:
```python
import jax
import jax.numpy as jnp
from jax import lax
from jax.sharding import PartitionSpec as P

H = 8
HD = 64
QB = 512


EPS = 1e-05
NEG = -1e30


def normalize(value, gain):
    mean = jnp.mean(value, axis=-1, keepdims=True)
    centred = value - mean
    spread = jnp.mean(centred * centred, axis=-1, keepdims=True)
    return centred * lax.rsqrt(spread + EPS) * gain


def smooth(value):
    return jax.nn.gelu(value, approximate=False)


def matmul(left, right):
    return jnp.dot(left, right, preferred_element_type=jnp.float32)


def grad_weight(left, right):
    return lax.dot_general(
        left, right, (((0,), (0,)), ((), ())), preferred_element_type=jnp.float32
    )


def grad_input(left, right):
    return lax.dot_general(
        left, right, (((1,), (1,)), ((), ())), preferred_element_type=jnp.float32
    )


def column_sum(value):
    return jnp.sum(value.astype(jnp.float32), axis=0)


def shards(
    tokens,
    segment,
    counts,
    memory,
    w_query,
    b_query,
    w_key,
    w_value,
    b_value,
    w_out,
    b_out,
    gain_attn,
    shift_attn,
    w_up,
    b_up,
    w_down,
    b_down,
    gain_ffn,
    shift_ffn,
    cotangent,
):
    full = (
        lax.all_gather(memory, "dp", axis=1, tiled=True),
        lax.all_gather(w_query, "dp", axis=0, tiled=True),
        lax.all_gather(b_query, "dp", axis=0, tiled=True),
        lax.all_gather(w_key, "dp", axis=0, tiled=True),
        lax.all_gather(w_value, "dp", axis=0, tiled=True),
        lax.all_gather(b_value, "dp", axis=0, tiled=True),
        lax.all_gather(w_out, "dp", axis=0, tiled=True),
        lax.all_gather(b_out, "dp", axis=0, tiled=True),
        lax.all_gather(gain_attn, "dp", axis=0, tiled=True),
        lax.all_gather(shift_attn, "dp", axis=0, tiled=True),
        lax.all_gather(w_up, "dp", axis=0, tiled=True),
        lax.all_gather(b_up, "dp", axis=0, tiled=True),
        lax.all_gather(w_down, "dp", axis=0, tiled=True),
        lax.all_gather(b_down, "dp", axis=0, tiled=True),
        lax.all_gather(gain_ffn, "dp", axis=0, tiled=True),
        lax.all_gather(shift_ffn, "dp", axis=0, tiled=True),
    )
    (
        memory_full,
        query_weight,
        query_bias,
        key_weight,
        value_weight,
        value_bias,
        out_weight,
        out_bias,
        gain_one,
        shift_one,
        up_weight,
        up_bias,
        down_weight,
        down_bias,
        gain_two,
        shift_two,
    ) = full
    slots = tokens.shape[0]
    width = tokens.shape[1]
    memory_rows = memory_full.shape[0]
    blocks = slots // QB
    scale = HD ** (-0.5)
    valid = jnp.arange(slots) < counts[0]
    key_seg = jnp.where(valid, segment, -1)
    queries = (matmul(tokens, query_weight) + query_bias.astype(jnp.float32)).astype(jnp.bfloat16)
    keys_tok = matmul(tokens, key_weight).astype(jnp.bfloat16)
    keys_mem = matmul(memory_full, key_weight).astype(jnp.bfloat16)
    values_tok = (matmul(tokens, value_weight) + value_bias.astype(jnp.float32)).astype(
        jnp.bfloat16
    )
    values_mem = (matmul(memory_full, value_weight) + value_bias.astype(jnp.float32)).astype(
        jnp.bfloat16
    )
    key_heads = keys_tok.reshape(slots, H, HD)
    key_mem_heads = keys_mem.reshape(memory_rows, H, HD)
    value_heads = values_tok.reshape(slots, H, HD)
    value_mem_heads = values_mem.reshape(memory_rows, H, HD)
    query_blocks = queries.reshape(blocks, QB, H, HD)
    seg_blocks = segment.reshape(blocks, QB)

    def score_block(query_block, seg_block):
        tok_scores = (
            jnp.einsum("qhd,khd->hqk", query_block, key_heads, preferred_element_type=jnp.float32)
            * scale
        )
        mem_scores = (
            jnp.einsum(
                "qhd,khd->hqk", query_block, key_mem_heads, preferred_element_type=jnp.float32
            )
            * scale
        )
        allowed = key_seg[None, :] == seg_block[:, None]
        return (jnp.where(allowed[None], tok_scores, NEG), mem_scores)

    def forward_block(item):
        query_block, seg_block = item
        tok_scores, mem_scores = score_block(query_block, seg_block)
        top = jnp.maximum(jnp.max(tok_scores, axis=-1), jnp.max(mem_scores, axis=-1))
        tok_exp = jnp.exp(tok_scores - top[..., None])
        mem_exp = jnp.exp(mem_scores - top[..., None])
        total = jnp.sum(tok_exp, axis=-1) + jnp.sum(mem_exp, axis=-1)
        tok_weights = (tok_exp / total[..., None]).astype(jnp.bfloat16)
        mem_weights = (mem_exp / total[..., None]).astype(jnp.bfloat16)
        mixed_block = jnp.einsum(
            "hqk,khd->qhd", tok_weights, value_heads, preferred_element_type=jnp.float32
        )
        mixed_block = mixed_block + jnp.einsum(
            "hqk,khd->qhd", mem_weights, value_mem_heads, preferred_element_type=jnp.float32
        )
        return (mixed_block.astype(jnp.bfloat16), top + jnp.log(total))

    mixed_blocks, log_totals = lax.map(forward_block, (query_blocks, seg_blocks))
    mixed = mixed_blocks.reshape(slots, width)
    attention = matmul(mixed, out_weight) + out_bias.astype(jnp.float32)
    first_sum = tokens.astype(jnp.float32) + attention
    first = normalize(first_sum, gain_one.astype(jnp.float32)) + shift_one.astype(jnp.float32)
    first_low = first.astype(jnp.bfloat16)
    hidden = matmul(first_low, up_weight) + up_bias.astype(jnp.float32)
    active = smooth(hidden).astype(jnp.bfloat16)
    branch = matmul(active, down_weight) + down_bias.astype(jnp.float32)
    second_sum = first + branch
    result = normalize(second_sum, gain_two.astype(jnp.float32)) + shift_two.astype(jnp.float32)
    output = jnp.where(valid[:, None], result, 0.0).astype(jnp.bfloat16)
    again = (
        lax.all_gather(memory, "dp", axis=1, tiled=True),
        lax.all_gather(w_query, "dp", axis=0, tiled=True),
        lax.all_gather(w_key, "dp", axis=0, tiled=True),
        lax.all_gather(w_value, "dp", axis=0, tiled=True),
        lax.all_gather(w_out, "dp", axis=0, tiled=True),
        lax.all_gather(w_up, "dp", axis=0, tiled=True),
        lax.all_gather(w_down, "dp", axis=0, tiled=True),
        lax.all_gather(gain_attn, "dp", axis=0, tiled=True),
        lax.all_gather(gain_ffn, "dp", axis=0, tiled=True),
    )
    (
        memory_back,
        query_back,
        key_back,
        value_back,
        out_back,
        up_back,
        down_back,
        gain_one_back,
        gain_two_back,
    ) = again
    seed_grad = jnp.where(valid[:, None], cotangent.astype(jnp.float32), 0.0)
    unused_two, second_back = jax.vjp(normalize, second_sum, gain_two_back.astype(jnp.float32))
    grad_second, grad_gain_two = second_back(seed_grad)
    grad_shift_two = jnp.sum(seed_grad, axis=0)
    branch_grad = grad_second.astype(jnp.bfloat16)
    grad_down = grad_weight(active, branch_grad)
    grad_down_bias = column_sum(branch_grad)
    active_grad = grad_input(branch_grad, down_back)
    unused_hidden, smooth_back = jax.vjp(smooth, hidden)
    hidden_grad = smooth_back(active_grad)[0].astype(jnp.bfloat16)
    grad_up = grad_weight(first_low, hidden_grad)
    grad_up_bias = column_sum(hidden_grad)
    first_grad = grad_second + grad_input(hidden_grad, up_back)
    unused_one, first_back = jax.vjp(normalize, first_sum, gain_one_back.astype(jnp.float32))
    grad_first_sum, grad_gain_one = first_back(first_grad)
    grad_shift_one = jnp.sum(first_grad, axis=0)
    attention_grad = grad_first_sum.astype(jnp.bfloat16)
    grad_out = grad_weight(mixed, attention_grad)
    grad_out_bias = column_sum(attention_grad)
    mixed_grad = grad_input(attention_grad, out_back).astype(jnp.bfloat16)
    grad_blocks = mixed_grad.reshape(blocks, QB, H, HD)

    def backward_block(carry, item):
        key_tok_acc, value_tok_acc, key_mem_acc, value_mem_acc = carry
        query_block, grad_block, total_block, seg_block = item
        tok_scores, mem_scores = score_block(query_block, seg_block)
        tok_probs = jnp.exp(tok_scores - total_block[..., None])
        mem_probs = jnp.exp(mem_scores - total_block[..., None])
        tok_dprobs = jnp.einsum(
            "qhd,khd->hqk", grad_block, value_heads, preferred_element_type=jnp.float32
        )
        mem_dprobs = jnp.einsum(
            "qhd,khd->hqk", grad_block, value_mem_heads, preferred_element_type=jnp.float32
        )
        centre = jnp.sum(tok_probs * tok_dprobs, axis=-1) + jnp.sum(mem_probs * mem_dprobs, axis=-1)
        tok_sgrad = (tok_probs * (tok_dprobs - centre[..., None])).astype(jnp.bfloat16)
        mem_sgrad = (mem_probs * (mem_dprobs - centre[..., None])).astype(jnp.bfloat16)
        query_part = jnp.einsum(
            "hqk,khd->qhd", tok_sgrad, key_heads, preferred_element_type=jnp.float32
        )
        query_part = (
            query_part
            + jnp.einsum(
                "hqk,khd->qhd", mem_sgrad, key_mem_heads, preferred_element_type=jnp.float32
            )
        ) * scale
        key_tok_acc = (
            key_tok_acc
            + jnp.einsum("hqk,qhd->khd", tok_sgrad, query_block, preferred_element_type=jnp.float32)
            * scale
        )
        key_mem_acc = (
            key_mem_acc
            + jnp.einsum("hqk,qhd->khd", mem_sgrad, query_block, preferred_element_type=jnp.float32)
            * scale
        )
        value_tok_acc = value_tok_acc + jnp.einsum(
            "hqk,qhd->khd",
            tok_probs.astype(jnp.bfloat16),
            grad_block,
            preferred_element_type=jnp.float32,
        )
        value_mem_acc = value_mem_acc + jnp.einsum(
            "hqk,qhd->khd",
            mem_probs.astype(jnp.bfloat16),
            grad_block,
            preferred_element_type=jnp.float32,
        )
        return (
            (key_tok_acc, value_tok_acc, key_mem_acc, value_mem_acc),
            query_part.astype(jnp.bfloat16),
        )

    start = (
        jnp.zeros((slots, H, HD), jnp.float32),
        jnp.zeros((slots, H, HD), jnp.float32),
        jnp.zeros((memory_rows, H, HD), jnp.float32),
        jnp.zeros((memory_rows, H, HD), jnp.float32),
    )
    sums, query_parts = lax.scan(
        backward_block, start, (query_blocks, grad_blocks, log_totals, seg_blocks)
    )
    key_tok_grad = sums[0].reshape(slots, width).astype(jnp.bfloat16)
    value_tok_grad = sums[1].reshape(slots, width).astype(jnp.bfloat16)
    key_mem_grad = sums[2].reshape(memory_rows, width).astype(jnp.bfloat16)
    value_mem_grad = sums[3].reshape(memory_rows, width).astype(jnp.bfloat16)
    query_grad = query_parts.reshape(slots, width)
    grad_query = grad_weight(tokens, query_grad)
    grad_query_bias = column_sum(query_grad)
    grad_key = grad_weight(tokens, key_tok_grad) + grad_weight(memory_back, key_mem_grad)
    grad_value = grad_weight(tokens, value_tok_grad) + grad_weight(memory_back, value_mem_grad)
    grad_value_bias = column_sum(value_tok_grad) + column_sum(value_mem_grad)
    grad_memory = grad_input(key_mem_grad, key_back) + grad_input(value_mem_grad, value_back)
    grad_tokens = grad_first_sum + grad_input(query_grad, query_back)
    grad_tokens = (
        grad_tokens + grad_input(key_tok_grad, key_back) + grad_input(value_tok_grad, value_back)
    )
    owned = (
        lax.psum_scatter(grad_memory, "dp", scatter_dimension=1, tiled=True),
        lax.psum_scatter(grad_query, "dp", scatter_dimension=0, tiled=True),
        lax.psum_scatter(grad_query_bias, "dp", scatter_dimension=0, tiled=True),
        lax.psum_scatter(grad_key, "dp", scatter_dimension=0, tiled=True),
        lax.psum_scatter(grad_value, "dp", scatter_dimension=0, tiled=True),
        lax.psum_scatter(grad_value_bias, "dp", scatter_dimension=0, tiled=True),
        lax.psum_scatter(grad_out, "dp", scatter_dimension=0, tiled=True),
        lax.psum_scatter(grad_out_bias, "dp", scatter_dimension=0, tiled=True),
        lax.psum_scatter(grad_gain_one, "dp", scatter_dimension=0, tiled=True),
        lax.psum_scatter(grad_shift_one, "dp", scatter_dimension=0, tiled=True),
        lax.psum_scatter(grad_up, "dp", scatter_dimension=0, tiled=True),
        lax.psum_scatter(grad_up_bias, "dp", scatter_dimension=0, tiled=True),
        lax.psum_scatter(grad_down, "dp", scatter_dimension=0, tiled=True),
        lax.psum_scatter(grad_down_bias, "dp", scatter_dimension=0, tiled=True),
        lax.psum_scatter(grad_gain_two, "dp", scatter_dimension=0, tiled=True),
        lax.psum_scatter(grad_shift_two, "dp", scatter_dimension=0, tiled=True),
    )
    return (
        output,
        grad_tokens,
        owned[0],
        owned[1],
        owned[2],
        owned[3],
        owned[4],
        owned[5],
        owned[6],
        owned[7],
        owned[8],
        owned[9],
        owned[10],
        owned[11],
        owned[12],
        owned[13],
        owned[14],
        owned[15],
    )


def solution(mesh):
    in_specs = (
        P("dp", None),
        P("dp"),
        P("dp"),
        P(None, "dp"),
        P("dp", None),
        P("dp"),
        P("dp", None),
        P("dp", None),
        P("dp"),
        P("dp", None),
        P("dp"),
        P("dp"),
        P("dp"),
        P("dp", None),
        P("dp"),
        P("dp", None),
        P("dp"),
        P("dp"),
        P("dp"),
        P("dp", None),
    )
    out_specs = (
        P("dp", None),
        P("dp", None),
        P(None, "dp"),
        P("dp", None),
        P("dp"),
        P("dp", None),
        P("dp", None),
        P("dp"),
        P("dp", None),
        P("dp"),
        P("dp"),
        P("dp"),
        P("dp", None),
        P("dp"),
        P("dp", None),
        P("dp"),
        P("dp"),
        P("dp"),
    )
    return jax.shard_map(shards, mesh=mesh, in_specs=in_specs, out_specs=out_specs, check_vma=False)
```

profile of v0, /device:TPU:0, one launch (start us, length us, event | category | flops | bytes accessed | tf_op | source)
XLA Modules:
  0.0 2035.3 jit_solution(17654876365592954387)
XLA Ops:
  16.4 42.2 %all-reduce.19 = (bf16[512]{0:T(512)(128)(2,1)S(1)}, bf16[512]{0:T(512)(128)(2,1)S(1)}, bf16[512]{0:T(512)(128)(2,1)S(1)}, bf16[512]{0:T(512)(128)(2,1)S(1)}, bf...) all-reduce(bf16[512]{0:T(512)(128)(2,1)S(1)} %dynamic-update-slice,, ...), channel_id=1, replica_groups=mesh['dp'=32] {'dp'}, use_global_device_ids=true, to_apply=%add | all-reduce | flops 6144 | bytes 24576
  58.6 41.0 %all_gather.60 = bf16[20,512]{0,1:T(8,128)(2,1)S(1)} all-gather(bf16[20,16]{0,1:T(8,128)(2,1)} %param.27), channel_id=1, replica_groups=mesh['dp'=32] {'dp'}, dimensions={1}, use_global_device_ids=true | all-gather | bytes 21120 | tf_op jit(solution)/shard_map/all_gather | solution.py:69
  99.6 38.9 %all_gather.59 = bf16[512,512]{1,0:T(8,128)(2,1)S(1)} all-gather(bf16[16,512]{1,0:T(8,128)(2,1)} %param.30), channel_id=1, replica_groups=mesh['dp'=32] {'dp'}, dimensions={0}, use_global_device_ids=true | all-gather | bytes 540672 | tf_op jit(solution)/shard_map/all_gather | solution.py:72
  138.5 39.5 %all_gather.61 = bf16[512,512]{1,0:T(8,128)(2,1)S(1)} all-gather(bf16[16,512]{1,0:T(8,128)(2,1)} %param.31), channel_id=1, replica_groups=mesh['dp'=32] {'dp'}, dimensions={0}, use_global_device_ids=true | all-gather | bytes 540672 | tf_op jit(solution)/shard_map/all_gather | solution.py:73
  196.1 38.2 %all_gather.57 = bf16[512,512]{1,0:T(8,128)(2,1)S(1)} all-gather(bf16[16,512]{1,0:T(8,128)(2,1)S(1)} %copy-done.48), channel_id=1, replica_groups=mesh['dp'=32] {'dp'}, dimensions={0}, use_global_device_ids=true | all-gather | bytes 540672 | tf_op jit(solution)/shard_map/all_gather | solution.py:70
  234.3 42.2 %all_gather.63 = bf16[512,512]{1,0:T(8,128)(2,1)} all-gather(bf16[16,512]{1,0:T(8,128)(2,1)S(1)} %copy-done.49), channel_id=1, replica_groups=mesh['dp'=32] {'dp'}, dimensions={0}, use_global_device_ids=true | all-gather | bytes 540672 | tf_op jit(solution)/shard_map/all_gather | solution.py:75
  297.7 208.1 %while.31 = (s32[]{:T(128)}, bf16[4,512,8,64]{1,3,2,0:T(8,128)(2,1)}, f32[4,8,512]{2,1,0:T(8,128)}, s32[2048]{0:T(1024)}, s32[4,512]{1,0:T(4,128)}, /*index=5*/b...) while((s32[]{:T(128)}, ...), condition=%wide.region_5.6_spmd, body=%wide.region_0.5_spmd.sunk | while | flops 2271260672 | bytes 114112640 | solution.py:158
  515.2 46.5 %multiply_convert_fusion.2 = (bf16[2048,2048]{1,0:T(8,128)(2,1)}, f32[2048,2048]{1,0:T(8,128)}, f32[2048,2048]{1,0:T(8,128)}) fusion(f32[2048]{0:T(1024)S(1)} %copy-done.56, bf16[512,2048]{1,0:T(8,128)(2,1)} %all-gather.3.cloned.1.call-done, f32[2048,512]{0,1:T(8,128)} %copy-done.10, f32[512]{0:T(512)S(1)} %copy-done.61, f32[512]{0:T(512)S(1)} %copy-done.57, ...), kind=kOutput, calls=%fused_computation.84 | convolution fusion | flops 4577034240 | bytes 48263168 | tf_op jit(solution)/shard_map/dot_general | solution.py:27
  636.2 445.1 %while.32 = (s32[]{:T(128)}, f32[2048,8,64]{0,2,1:T(8,128)}, f32[2048,8,64]{0,2,1:T(8,128)}, f32[20,8,64]{2,0,1:T(8,128)S(1)}, f32[20,8,64]{2,0,1:T(8,128)S(1)},...) while((s32[]{:T(128)}, f32[2048,8,64]{0,2,1:T(8,128)}, ...), condition=%wide.region_17.18_spmd.clone, body=%wide.region_14.17_spmd.clone.sunk | while | flops 5504415744 | bytes 366266624 | solution.py:271
  657.4 24.6 %multiply_reduce_fusion.10 = (f32[8,512]{1,0:T(8,128)S(1)}, f32[8,512,2048]{2,1,0:T(8,128)}) fusion(f32[8,512,2048]{2,1,0:T(8,128)} %fusion.212, f32[8,512]{1,0:T(8,128)S(1)} %dynamic-slice_bitcast_fusion.2, bf16[2048,8,64]{0,2,1:T(8,128)(2,1)S(1)} %get-tuple-element.693, bf16[4,512,8,64]{1,3,2,0:T(8,128)(2,1)} %get-tuple-element.690, ...), kind=kOutput, calls=%fused_computation.29.clone.1 | convolution fusion | flops 1115680768 | bytes 70811648 | tf_op jit(solution)/shard_map/while/body/eval_jaxpr/qhd,khd->hqk/dot_general | solution.py:129
  682.0 27.4 %multiply_convert_fusion.5 = bf16[8,512,2048]{2,1,0:T(8,128)(2,1)} fusion(f32[8,512,2048]{2,1,0:T(8,128)} %get-tuple-element.613, f32[8,512,2048]{2,1,0:T(8,128)} %fusion.212, f32[8,512]{1,0:T(8,128)S(1)} %add.399), kind=kLoop, calls=%fused_computation.28.clone.1 | loop fusion | flops 25165824 | bytes 83902464 | tf_op jit(solution)/shard_map/while/body/eval_jaxpr/convert_element_type | solution.py:227
  766.7 24.7 %multiply_reduce_fusion.10 = (f32[8,512]{1,0:T(8,128)S(1)}, f32[8,512,2048]{2,1,0:T(8,128)}) fusion(f32[8,512,2048]{2,1,0:T(8,128)} %fusion.212, f32[8,512]{1,0:T(8,128)S(1)} %dynamic-slice_bitcast_fusion.2, bf16[2048,8,64]{0,2,1:T(8,128)(2,1)S(1)} %get-tuple-element.693, bf16[4,512,8,64]{1,3,2,0:T(8,128)(2,1)} %get-tuple-element.690, ...), kind=kOutput, calls=%fused_computation.29.clone.1 | convolution fusion | flops 1115680768 | bytes 70811648 | tf_op jit(solution)/shard_map/while/body/eval_jaxpr/qhd,khd->hqk/dot_general | solution.py:129
  791.3 27.4 %multiply_convert_fusion.5 = bf16[8,512,2048]{2,1,0:T(8,128)(2,1)} fusion(f32[8,512,2048]{2,1,0:T(8,128)} %get-tuple-element.613, f32[8,512,2048]{2,1,0:T(8,128)} %fusion.212, f32[8,512]{1,0:T(8,128)S(1)} %add.399), kind=kLoop, calls=%fused_computation.28.clone.1 | loop fusion | flops 25165824 | bytes 83902464 | tf_op jit(solution)/shard_map/while/body/eval_jaxpr/convert_element_type | solution.py:227
  878.5 24.6 %multiply_reduce_fusion.10 = (f32[8,512]{1,0:T(8,128)S(1)}, f32[8,512,2048]{2,1,0:T(8,128)}) fusion(f32[8,512,2048]{2,1,0:T(8,128)} %fusion.212, f32[8,512]{1,0:T(8,128)S(1)} %dynamic-slice_bitcast_fusion.2, bf16[2048,8,64]{0,2,1:T(8,128)(2,1)S(1)} %get-tuple-element.693, bf16[4,512,8,64]{1,3,2,0:T(8,128)(2,1)} %get-tuple-element.690, ...), kind=kOutput, calls=%fused_computation.29.clone.1 | convolution fusion | flops 1115680768 | bytes 70811648 | tf_op jit(solution)/shard_map/while/body/eval_jaxpr/qhd,khd->hqk/dot_general | solution.py:129
  903.1 27.4 %multiply_convert_fusion.5 = bf16[8,512,2048]{2,1,0:T(8,128)(2,1)} fusion(f32[8,512,2048]{2,1,0:T(8,128)} %get-tuple-element.613, f32[8,512,2048]{2,1,0:T(8,128)} %fusion.212, f32[8,512]{1,0:T(8,128)S(1)} %add.399), kind=kLoop, calls=%fused_computation.28.clone.1 | loop fusion | flops 25165824 | bytes 83902464 | tf_op jit(solution)/shard_map/while/body/eval_jaxpr/convert_element_type | solution.py:227
  990.3 24.6 %multiply_reduce_fusion.10 = (f32[8,512]{1,0:T(8,128)S(1)}, f32[8,512,2048]{2,1,0:T(8,128)}) fusion(f32[8,512,2048]{2,1,0:T(8,128)} %fusion.212, f32[8,512]{1,0:T(8,128)S(1)} %dynamic-slice_bitcast_fusion.2, bf16[2048,8,64]{0,2,1:T(8,128)(2,1)S(1)} %get-tuple-element.693, bf16[4,512,8,64]{1,3,2,0:T(8,128)(2,1)} %get-tuple-element.690, ...), kind=kOutput, calls=%fused_computation.29.clone.1 | convolution fusion | flops 1115680768 | bytes 70811648 | tf_op jit(solution)/shard_map/while/body/eval_jaxpr/qhd,khd->hqk/dot_general | solution.py:129
  1014.9 27.4 %multiply_convert_fusion.5 = bf16[8,512,2048]{2,1,0:T(8,128)(2,1)} fusion(f32[8,512,2048]{2,1,0:T(8,128)} %get-tuple-element.613, f32[8,512,2048]{2,1,0:T(8,128)} %fusion.212, f32[8,512]{1,0:T(8,128)S(1)} %add.399), kind=kLoop, calls=%fused_computation.28.clone.1 | loop fusion | flops 25165824 | bytes 83902464 | tf_op jit(solution)/shard_map/while/body/eval_jaxpr/convert_element_type | solution.py:227
  1151.5 37.4 %all-reduce.18 = (f32[512]{0:T(512)S(1)}, f32[512]{0:T(512)S(1)}, f32[512]{0:T(512)S(1)}, f32[512]{0:T(512)S(1)}, f32[512]{0:T(512)S(1)}, /*index=5*/f32[2048]{0...) all-reduce(f32[512]{0:T(512)S(1)} %reduce_sum.215, ...), channel_id=4, replica_groups=mesh['dp'=32] {'dp'}, use_global_device_ids=true, to_apply=%region_21.22.clone | all-reduce | flops 6144 | bytes 49152
  1214.9 133.5 %reduce-scatter.16.cloned.1.call-done = f32[16,512]{1,0:T(8,128)} async-done(((f32[512,512]{1,0:T(8,128)}), f32[16,512]{1,0:T(8,128)}) %reduce-scatter.16.cloned.1.call-update) | async-done | bytes 32784 | tf_op jit(solution)/shard_map/reduce_scatter | solution.py:296
  1348.3 133.4 %reduce-scatter.22.cloned.1.call-done = f32[16,512]{1,0:T(8,128)} async-done(((f32[512,512]{1,0:T(8,128)}), f32[16,512]{1,0:T(8,128)}) %reduce-scatter.22.cloned.1.call-update) | async-done | bytes 32784
  1481.8 133.5 %reduce-scatter.24.cloned.1.call-done = f32[16,512]{1,0:T(8,128)} async-done(((f32[512,512]{1,0:T(8,128)}), f32[16,512]{1,0:T(8,128)}) %reduce-scatter.24.cloned.1.call-update) | async-done | bytes 32784
  1615.3 133.6 %reduce-scatter.26.cloned.1.call-done = f32[16,512]{1,0:T(8,128)} async-done(((f32[512,512]{1,0:T(8,128)}), f32[16,512]{1,0:T(8,128)}) %reduce-scatter.26.cloned.1.call-update) | async-done | bytes 32784
  1748.8 139.7 %reduce-scatter.18.cloned.1.call-done = f32[16,2048]{1,0:T(8,128)} async-done(((f32[512,2048]{1,0:T(8,128)}), f32[16,2048]{1,0:T(8,128)}) %reduce-scatter.18.cloned.1.call-update) | async-done | bytes 131088 | tf_op jit(solution)/shard_map/reduce_scatter | solution.py:300
  1888.5 139.8 %reduce-scatter.20.cloned.1.call-done = f32[64,512]{1,0:T(8,128)} async-done(((f32[2048,512]{1,0:T(8,128)}), f32[64,512]{1,0:T(8,128)}) %reduce-scatter.20.cloned.1.call-update) | async-done | bytes 131088 | tf_op jit(solution)/shard_map/reduce_scatter | solution.py:302
  (378 shorter events, 670.8 us)
Async XLA Ops:
  7.2 508.0 %all-gather.3.cloned.1.call-start = ((), (), s32[]{:S(2)}) async-start(), calls=%async_computation.7 | async-start | bytes 2162688 | tf_op jit(solution)/shard_map/all_gather | solution.py:79
  7.9 553.9 %all-gather.5.cloned.1.call-start = ((), (), s32[]{:S(2)}) async-start(), calls=%async_computation.8 | async-start | bytes 2162688 | tf_op jit(solution)/shard_map/all_gather | solution.py:81
  8.7 1206.2 %reduce-scatter.14.cloned.1.call-start = ((), (), s32[]{:S(2)}) async-start(), calls=%async_computation.9 | async-start | bytes 270336 | tf_op jit(solution)/shard_map/reduce_scatter | solution.py:290
  99.6 78.6 %copy-start.23 = (bf16[20,512]{0,1:T(8,128)(2,1)}, bf16[20,512]{0,1:T(8,128)(2,1)S(1)}, u32[]{:S(2)}) copy-start(bf16[20,512]{0,1:T(8,128)(2,1)S(1)} %all_gather.60) | copy-start | bytes 61444
  138.5 44.3 %copy-start.19 = (bf16[512,512]{1,0:T(8,128)(2,1)}, bf16[512,512]{1,0:T(8,128)(2,1)S(1)}, u32[]{:S(2)}) copy-start(bf16[512,512]{1,0:T(8,128)(2,1)S(1)} %all_gather.59) | copy-start | bytes 1572868
  184.1 12.0 copy-start.48
  184.1 50.1 %copy-start.49 = (bf16[16,512]{1,0:T(8,128)(2,1)S(1)}, bf16[16,512]{1,0:T(8,128)(2,1)}, u32[]{:S(2)}) copy-start(bf16[16,512]{1,0:T(8,128)(2,1)} %param.33) | copy-start | bytes 49156
  234.3 50.3 %copy-start.32 = (bf16[512,512]{1,0:T(8,128)(2,1)}, bf16[512,512]{1,0:T(8,128)(2,1)S(1)}, u32[]{:S(2)}) copy-start(bf16[512,512]{1,0:T(8,128)(2,1)S(1)} %all_gather.57) | copy-start | bytes 1572868
  512.1 106.1 %copy-start.41 = (f32[2048]{0:T(1024)}, f32[2048]{0:T(1024)S(1)}, u32[]{:S(2)}) copy-start(f32[2048]{0:T(1024)S(1)} %broadcast_multiply_fusion.1) | copy-start | bytes 24580
  515.2 103.0 %copy-start.46 = (f32[2048]{0:T(1024)}, f32[2048]{0:T(1024)S(1)}, u32[]{:S(2)}) copy-start(f32[2048]{0:T(1024)S(1)} %fusion.70) | copy-start | bytes 24580
  515.2 46.6 %copy-start.63 = (f32[512]{0:T(512)S(1)}, f32[512]{0:T(512)}, u32[]{:S(2)}) copy-start(f32[512]{0:T(512)} %convert_element_type.163) | copy-start | bytes 6148
  561.8 11.2 copy-start.8
  561.8 11.2 copy-start.43
  561.8 11.2 copy-start.44
  605.2 12.9 copy-start.40
  605.2 13.0 copy-start.11
  726.5 10.9 copy-start
  948.8 10.9 copy-start
  1085.0 263.4 %reduce-scatter.16.cloned.1.call-start = ((), (), s32[]{:S(2)}) async-start(), calls=%async_computation.10 | async-start | bytes 1081344 | tf_op jit(solution)/shard_map/reduce_scatter | solution.py:296
  1089.7 392.1 %reduce-scatter.22.cloned.1.call-start = ((), (), s32[]{:S(2)}) async-start(), calls=%async_computation.13 | async-start | bytes 1081344
  1096.0 519.3 %reduce-scatter.24.cloned.1.call-start = ((), (), s32[]{:S(2)}) async-start(), calls=%async_computation.14 | async-start | bytes 1081344
  1102.9 645.9 %reduce-scatter.26.cloned.1.call-start = ((), (), s32[]{:S(2)}) async-start(), calls=%async_computation.15 | async-start | bytes 1081344
  1109.9 778.6 %reduce-scatter.18.cloned.1.call-start = ((), (), s32[]{:S(2)}) async-start(), calls=%async_computation.11 | async-start | bytes 4325376 | tf_op jit(solution)/shard_map/reduce_scatter | solution.py:300
  1121.2 907.0 %reduce-scatter.20.cloned.1.call-start = ((), (), s32[]{:S(2)}) async-start(), calls=%async_computation.12 | async-start | bytes 4325376 | tf_op jit(solution)/shard_map/reduce_scatter | solution.py:302
  (59 other events, 266.9 us)
Sparse Core Ops, SparseCore 0:
  10.9 59.0 all-gather.2
  72.9 55.6 all-gather.4
  1085.1 129.7 reduce-scatter.13
  1217.6 130.6 reduce-scatter.15
  1351.0 130.7 reduce-scatter.21
  1484.5 130.6 reduce-scatter.23
  1618.1 130.7 reduce-scatter.25
  1751.8 136.6 reduce-scatter.17
  1891.5 136.7 reduce-scatter.19
where the time goes:
time: 2040 us
  waiting for transfers between devices  836 us (41%)
  matrix products  603 us (30%)
  blocking collectives  279 us (14%)
  other arithmetic  207 us (10%)
  local copies, waits for them, and re-layouts  92.5 us (5%)
    unnamed x12, waiting for transfers between devices  402 us
    dot_general x8, matrix products, score_block(): jnp.einsum('qhd,khd->hqk', query_block, key_heads, preferred_element_type...  158 us
    reduce_scatter x1, waiting for transfers between devices, shards(): lax.psum_scatter(grad_down, 'dp', scatter_dimension=0, tiled=True)  140 us
    reduce_scatter x1, waiting for transfers between devices, shards(): lax.psum_scatter(grad_up, 'dp', scatter_dimension=0, tiled=True)  140 us
    reduce_scatter x1, waiting for transfers between devices, shards(): lax.psum_scatter(grad_out, 'dp', scatter_dimension=0, tiled=True)  133 us
    convert_element_type x4, other arithmetic, backward_block(): (tok_probs * (tok_dprobs - centre[..., None])).astype(jnp.bfloat16)  110 us
    unnamed x2, blocking collectives  79.5 us
    dot_general x8, matrix products, matmul(): return jnp.dot(left, right, preferred_element_type=jnp.float32)  69.4 us
  transfers between devices with their start and end apart: 9, of which 7 were waited for; matrix products, arithmetic and copies ran while one was open for 18% of the time, Pallas kernels for 0%

commit v1 on v0

v1 whole, which is shorter than its diff:
```python
import functools
import jax
import jax.numpy as jnp
from jax import lax
from jax.experimental import pallas as pl
from jax.experimental.pallas import tpu as pltpu
from jax.sharding import PartitionSpec as P

H = 8
HD = 64
HA = 80
EPS = 1e-05
BIG = 1e30
PARTS = 32
ROWS = 208
BQ = 256
BK = 256
MP = 32
F32 = jnp.float32
BF16 = jnp.bfloat16
VMEM_LIMIT = 60 << 20

V_BQ, V_BV, V_BO, V_GA, V_SA, V_BD, V_GF, V_SF = range(8)


def dot(left, right, lc, rc):
    return lax.dot_general(left, right, (((lc,), (rc,)), ((), ())), preferred_element_type=F32)


def params(**kw):
    return pltpu.CompilerParams(vmem_limit_bytes=VMEM_LIMIT, **kw)


def qkv_kernel(mem_rows, g_ref, tok_ref, seg_ref, cnt_ref, qa_ref, ka_ref, va_ref, km_ref, vm_ref, wt_ref):
    step = pl.program_id(0)
    rows = tok_ref.shape[0]
    small = g_ref[:, 48:64, :].reshape(512, 512)
    bq = small[:, 128 + V_BQ : 129 + V_BQ].astype(F32)
    bv = small[:, 128 + V_BV : 129 + V_BV].astype(F32)

    @pl.when(step == 0)
    def _():
        for j in range(3):
            wt_ref[512 * j : 512 * j + 512, :] = g_ref[:, 16 * j : 16 * j + 16, :].reshape(512, 512).T
        memt = small[:, 0:128]
        km = dot(wt_ref[512:1024, :], memt, 1, 0).astype(BF16)
        vm = (dot(wt_ref[1024:1536, :], memt, 1, 0) + bv).astype(BF16)
        frow = lax.broadcasted_iota(jnp.int32, (16, 128), 0)
        lane = lax.broadcasted_iota(jnp.int32, (16, 128), 1)
        kf = jnp.where(frow < 3, jnp.where(lane < mem_rows, 0.0, 1.0), jnp.where(frow < 6, 1.0, 0.0)).astype(BF16)
        vf = jnp.where(frow < 3, 1.0, 0.0).astype(BF16)
        for h in range(H):
            km_ref[h, 0:64, :] = km[64 * h : 64 * h + 64, :]
            km_ref[h, 64:80, :] = kf
            vm_ref[h, 0:64, :] = vm[64 * h : 64 * h + 64, :]
            vm_ref[h, 64:80, :] = vf

    tok = tok_ref[...]
    q = ((dot(wt_ref[0:512, :], tok, 1, 1) + bq).astype(BF16) * jnp.asarray(HD ** -0.5, BF16))
    k = dot(wt_ref[512:1024, :], tok, 1, 1).astype(BF16)
    v = (dot(wt_ref[1024:1536, :], tok, 1, 1) + bv).astype(BF16)
    frow = lax.broadcasted_iota(jnp.int32, (16, rows), 0)
    seg = jnp.broadcast_to(seg_ref[...], (16, rows))
    pos = lax.broadcasted_iota(jnp.int32, (16, rows), 1) + step * rows
    valid = pos < cnt_ref[0]
    qf = jnp.where((frow < 3) & (frow != seg), -BIG, 0.0).astype(BF16)
    kf = jnp.where(frow < 3, jnp.where(valid & (frow != seg), 0.0, 1.0), jnp.where(frow < 6, 1.0, 0.0)).astype(BF16)
    vf = jnp.where(frow < 3, 1.0, 0.0).astype(BF16)
    for h in range(H):
        s = slice(64 * h, 64 * h + 64)
        qa_ref[h, 0:64, :] = q[s]
        qa_ref[h, 64:80, :] = qf
        ka_ref[h, 0:64, :] = k[s]
        ka_ref[h, 64:80, :] = kf
        va_ref[h, 0:64, :] = v[s]
        va_ref[h, 64:80, :] = vf


def qkv(g, tokens, segment, counts, mem_rows):
    slots = tokens.shape[0]
    rb = 512
    out = [jax.ShapeDtypeStruct((H, HA, slots), BF16)] * 3 + [jax.ShapeDtypeStruct((H, HA, 128), BF16)] * 2
    blk = pl.BlockSpec((H, HA, rb), lambda i: (0, 0, i))
    mblk = pl.BlockSpec((H, HA, 128), lambda i: (0, 0, 0))
    return pl.pallas_call(
        functools.partial(qkv_kernel, mem_rows),
        grid=(slots // rb,),
        in_specs=[
            pl.BlockSpec((PARTS, 64, 512), lambda i: (0, 0, 0)),
            pl.BlockSpec((rb, 512), lambda i: (i, 0)),
            pl.BlockSpec((1, rb), lambda i: (0, i)),
            pl.BlockSpec(memory_space=pltpu.SMEM),
        ],
        out_specs=[blk, blk, blk, mblk, mblk],
        out_shape=out,
        scratch_shapes=[pltpu.VMEM((1536, 512), BF16)],
        compiler_params=params(),
        name="qkv",
    )(g, tokens, segment.reshape(1, slots), counts)


def key_range(seg, count, first, slots):
    r, c = seg.shape
    pos = lax.broadcasted_iota(jnp.int32, (r, c), 0) * c + lax.broadcasted_iota(jnp.int32, (r, c), 1)
    valid = pos < count
    last = jnp.minimum(first + BQ, count)
    low, high, start = jnp.int32(slots), jnp.int32(0), jnp.int32(0)
    for s in range(3):
        end = jnp.sum(jnp.where(valid & (seg <= s), 1.0, 0.0)).astype(jnp.int32)
        hit = (end > first) & (start < last) & (end > start)
        low = jnp.where(hit, jnp.minimum(low, start), low)
        high = jnp.where(hit, jnp.maximum(high, end), high)
        start = end
    begin = low // 128
    blocks = jnp.where(high > low, (high - begin * 128 + BK - 1) // BK, 0)
    begin = jnp.minimum(begin, slots // 128 - blocks * (BK // 128))
    return begin, blocks


def fwd_kernel(slots, seg_ref, cnt_ref, qa_ref, ka_ref, va_ref, km_ref, vm_ref, mix_ref, lse_ref, acc_ref, m_ref):
    begin, blocks = key_range(seg_ref[...], cnt_ref[0], pl.program_id(0) * BQ, slots)
    for h in range(H):
        s = dot(km_ref[h, :, 0:MP], qa_ref[h], 0, 0)
        top = jnp.max(s, axis=0, keepdims=True)
        p = jnp.exp(s - top).astype(BF16)
        acc_ref[h] = dot(vm_ref[h, :, 0:MP], p, 1, 0)
        m_ref[h : h + 1, :] = top

    @pl.loop(0, blocks)
    def _(j):
        ks = pl.ds(pl.multiple_of((begin + j * (BK // 128)) * 128, 128), BK)
        for h in range(H):
            s = dot(ka_ref[h, :, ks], qa_ref[h], 0, 0)
            old = m_ref[h : h + 1, :]
            top = jnp.maximum(old, jnp.max(s, axis=0, keepdims=True))
            p = jnp.exp(s - top).astype(BF16)
            acc_ref[h] = acc_ref[h] * jnp.exp(old - top) + dot(va_ref[h, :, ks], p, 1, 0)
            m_ref[h : h + 1, :] = top

    for h in range(H):
        total = acc_ref[h, 64:65, :]
        mix_ref[64 * h : 64 * h + 64, :] = (acc_ref[h, 0:64, :] / total).astype(BF16)
        lse_ref[h : h + 1, :] = m_ref[h : h + 1, :] + jnp.log(total)


def attend_forward(seg2, counts, qa, ka, va, km, vm):
    slots = qa.shape[2]
    full = pl.BlockSpec((H, HA, slots), lambda i: (0, 0, 0))
    mfull = pl.BlockSpec((H, HA, 128), lambda i: (0, 0, 0))
    return pl.pallas_call(
        functools.partial(fwd_kernel, slots),
        grid=(slots // BQ,),
        in_specs=[
            pl.BlockSpec(seg2.shape, lambda i: (0, 0)),
            pl.BlockSpec(memory_space=pltpu.SMEM),
            pl.BlockSpec((H, HA, BQ), lambda i: (0, 0, i)),
            full, full, mfull, mfull,
        ],
        out_specs=[pl.BlockSpec((512, BQ), lambda i: (0, i)), pl.BlockSpec((H, BQ), lambda i: (0, i))],
        out_shape=[jax.ShapeDtypeStruct((512, slots), BF16), jax.ShapeDtypeStruct((H, slots), F32)],
        scratch_shapes=[pltpu.VMEM((H, HA, BQ), F32), pltpu.VMEM((H, BQ), F32)],
        compiler_params=params(),
        name="attend_forward",
    )(seg2, counts, qa, ka, va, km, vm)


def norm_parts(value):
    mean = jnp.mean(value, axis=-1, keepdims=True)
    centred = value - mean
    rstd = lax.rsqrt(jnp.mean(centred * centred, axis=-1, keepdims=True) + EPS)
    return centred * rstd, rstd


def norm_grad(grad_hat, hat, rstd):
    return rstd * (
        grad_hat
        - jnp.mean(grad_hat, axis=-1, keepdims=True)
        - hat * jnp.mean(grad_hat * hat, axis=-1, keepdims=True)
    )


def colsum(value):
    return jnp.sum(value, axis=0, keepdims=True)


def mid_kernel(
    rb, cnt_ref, gs_ref, up_ref, dn_ref, wo_ref, mix_ref, tok_ref, cot_ref,
    out_ref, gfirst_ref, mgrad_ref, delta_ref, gw_ref, vec_ref, bup_ref,
    row_ref, rbup_ref, wup_ref, wdn_ref, aup_ref, adn_ref, ao_ref,
):
    step = pl.program_id(0)

    @pl.when(step == 0)
    def _():
        small = gs_ref[...].reshape(512, 512)
        row_ref[...] = small[:, 128:256].astype(F32).T
        bup = jnp.sum(gs_ref[:, 0:8, 256:512].astype(F32), axis=0)
        for v in range(8):
            rbup_ref[0:1, 256 * v : 256 * v + 256] = bup[v : v + 1, :]
        for c in range(4):
            wup_ref[:, 512 * c : 512 * c + 512] = up_ref[:, 16 * c : 16 * c + 16, :].reshape(512, 512)
        wdn_ref[...] = dn_ref[...].reshape(2048, 512)
        aup_ref[...] = jnp.zeros_like(aup_ref)
        adn_ref[...] = jnp.zeros_like(adn_ref)
        ao_ref[...] = jnp.zeros_like(ao_ref)
        vec_ref[...] = jnp.zeros_like(vec_ref)
        bup_ref[...] = jnp.zeros_like(bup_ref)

    wo = wo_ref[...].reshape(512, 512)

    def row(v):
        return row_ref[v : v + 1, :]

    mixt = mix_ref[...]
    attention = dot(mixt, wo, 0, 0) + row(V_BO)
    hat1, rstd1 = norm_parts(tok_ref[...].astype(F32) + attention)
    first = hat1 * row(V_GA) + row(V_SA)
    first_low = first.astype(BF16)
    hidden = dot(first_low, wup_ref[...], 1, 0) + rbup_ref[...]
    cdf = 0.5 + 0.5 * lax.erf(hidden * (2.0 ** -0.5))
    active = (hidden * cdf).astype(BF16)
    slope = cdf + hidden * jnp.exp(hidden * hidden * -0.5) * 0.3989422804014327
    branch = dot(active, wdn_ref[...], 1, 0) + row(V_BD)
    hat2, rstd2 = norm_parts(first + branch)
    valid = lax.broadcasted_iota(jnp.int32, (rb, 1), 0) + step * rb < cnt_ref[0]
    out_ref[...] = jnp.where(valid, hat2 * row(V_GF) + row(V_SF), 0.0).astype(BF16)

    seed = jnp.where(valid, cot_ref[...].astype(F32), 0.0)
    vec_ref[V_GF : V_GF + 1, :] += colsum(seed * hat2)
    vec_ref[V_SF : V_SF + 1, :] += colsum(seed)
    grad_second = norm_grad(seed * row(V_GF), hat2, rstd2)
    branch_grad = grad_second.astype(BF16)
    adn_ref[...] += dot(active, branch_grad, 0, 0)
    vec_ref[V_BD : V_BD + 1, :] += colsum(branch_grad.astype(F32))
    hidden_grad = (dot(branch_grad, wdn_ref[...], 1, 1) * slope).astype(BF16)
    aup_ref[...] += dot(first_low, hidden_grad, 0, 0)
    bup_ref[...] += colsum(hidden_grad.astype(F32))
    first_grad = grad_second + dot(hidden_grad, wup_ref[...], 1, 1)
    vec_ref[V_GA : V_GA + 1, :] += colsum(first_grad * hat1)
    vec_ref[V_SA : V_SA + 1, :] += colsum(first_grad)
    grad_first = norm_grad(first_grad * row(V_GA), hat1, rstd1)
    gfirst_ref[...] = grad_first
    attention_grad = grad_first.astype(BF16)
    vec_ref[V_BO : V_BO + 1, :] += colsum(attention_grad.astype(F32))
    ao_ref[...] += dot(mixt, attention_grad, 1, 0)
    mgrad = dot(wo, attention_grad, 1, 1).astype(BF16)
    mgrad_ref[...] = mgrad
    prod = mgrad.astype(F32) * mixt.astype(F32)
    for h in range(H):
        delta_ref[h : h + 1, :] = jnp.sum(prod[64 * h : 64 * h + 64, :], axis=0, keepdims=True)

    @pl.when(step == pl.num_programs(0) - 1)
    def _():
        gw_ref[:, 0:16, :] = ao_ref[...].astype(gw_ref.dtype).reshape(PARTS, 16, 512)
        for c in range(4):
            gw_ref[:, 16 + 16 * c : 32 + 16 * c, :] = (
                aup_ref[:, 512 * c : 512 * c + 512].astype(gw_ref.dtype).reshape(PARTS, 16, 512)
            )
        gw_ref[:, 80:144, :] = adn_ref[...].astype(gw_ref.dtype).reshape(PARTS, 64, 512)


def middle(g, counts, mixt, tokens, cotangent, rb=256):
    slots = tokens.shape[0]
    rows = pl.BlockSpec((rb, 512), lambda i: (i, 0))
    cols = pl.BlockSpec((512, rb), lambda i: (0, i))
    once = pl.Buffered(1)
    return pl.pallas_call(
        functools.partial(mid_kernel, rb),
        grid=(slots // rb,),
        in_specs=[
            pl.BlockSpec(memory_space=pltpu.SMEM),
            pl.BlockSpec((PARTS, 16, 512), lambda i: (0, 3, 0), pipeline_mode=once),
            pl.BlockSpec((PARTS, 64, 512), lambda i: (0, 1, 0), pipeline_mode=once),
            pl.BlockSpec((PARTS, 64, 512), lambda i: (0, 2, 0), pipeline_mode=once),
            pl.BlockSpec((PARTS, 16, 512), lambda i: (0, 12, 0), pipeline_mode=once),
            cols, rows, rows,
        ],
        out_specs=[
            rows, rows, cols,
            pl.BlockSpec((H, rb), lambda i: (0, i)),
            pl.BlockSpec((PARTS, 144, 512), lambda i: (0, 0, 0), pipeline_mode=once),
            pl.BlockSpec((8, 512), lambda i: (0, 0)),
            pl.BlockSpec((1, 2048), lambda i: (0, 0)),
        ],
        out_shape=[
            jax.ShapeDtypeStruct((slots, 512), BF16),
            jax.ShapeDtypeStruct((slots, 512), F32),
            jax.ShapeDtypeStruct((512, slots), BF16),
            jax.ShapeDtypeStruct((H, slots), F32),
            jax.ShapeDtypeStruct((PARTS, 144, 512), BF16),
            jax.ShapeDtypeStruct((8, 512), F32),
            jax.ShapeDtypeStruct((1, 2048), F32),
        ],
        scratch_shapes=[
            pltpu.VMEM((128, 512), F32),
            pltpu.VMEM((1, 2048), F32),
            pltpu.VMEM((512, 2048), BF16),
            pltpu.VMEM((2048, 512), BF16),
            pltpu.VMEM((512, 2048), F32),
            pltpu.VMEM((2048, 512), F32),
            pltpu.VMEM((512, 512), F32),
        ],
        compiler_params=params(),
        name="middle",
    )(counts, g, g, g, g, mixt, tokens, cotangent)


def split3(value):
    high = value.astype(BF16)
    rest = value - high.astype(F32)
    mid = rest.astype(BF16)
    return high, mid, (rest - mid.astype(F32)).astype(BF16)


def bwd_kernel(
    slots, seg_ref, cnt_ref, qa_ref, ka_ref, va_ref, km_ref, vm_ref, do_ref, lse_ref, delta_ref,
    dq_ref, dk_ref, dv_ref, dkm_ref, dvm_ref, q2_ref, do2_ref, dqa_ref, dka_ref, dva_ref, dkma_ref, dvma_ref,
):
    step = pl.program_id(0)
    begin, blocks = key_range(seg_ref[...], cnt_ref[0], step * BQ, slots)

    @pl.when(step == 0)
    def _():
        dka_ref[...] = jnp.zeros_like(dka_ref)
        dva_ref[...] = jnp.zeros_like(dva_ref)
        dkma_ref[...] = jnp.zeros_like(dkma_ref)
        dvma_ref[...] = jnp.zeros_like(dvma_ref)

    frow = lax.broadcasted_iota(jnp.int32, (16, BQ), 0)

    def feature(value, at):
        high, mid, low = (jnp.broadcast_to(v.astype(F32), (16, BQ)) for v in split3(value))
        return jnp.where(frow == at, high, jnp.where(frow == at + 1, mid, jnp.where(frow == at + 2, low, 0.0)))

    for h in range(H):
        q2_ref[h, 0:64, :] = qa_ref[h, 0:64, :]
        q2_ref[h, 64:80, :] = (qa_ref[h, 64:80, :].astype(F32) + feature(-lse_ref[h : h + 1, :], 3)).astype(BF16)
        do2_ref[h, 0:64, :] = do_ref[64 * h : 64 * h + 64, :]
        do2_ref[h, 64:80, :] = feature(-delta_ref[h : h + 1, :], 0).astype(BF16)

    for h in range(H):
        p = jnp.exp(dot(km_ref[h, :, 0:MP], q2_ref[h], 0, 0))
        ds = (p * dot(vm_ref[h, :, 0:MP], do2_ref[h], 0, 0)).astype(BF16)
        dvma_ref[h, :, 0:MP] += dot(do2_ref[h, 0:64, :], p.astype(BF16), 1, 1)
        dkma_ref[h, :, 0:MP] += dot(q2_ref[h, 0:64, :], ds, 1, 1)
        dqa_ref[h] = dot(km_ref[h, 0:64, 0:MP], ds, 1, 0)

    @pl.loop(0, blocks)
    def _(j):
        ks = pl.ds(pl.multiple_of((begin + j * (BK // 128)) * 128, 128), BK)
        for h in range(H):
            p = jnp.exp(dot(ka_ref[h, :, ks], q2_ref[h], 0, 0))
            ds = (p * dot(va_ref[h, :, ks], do2_ref[h], 0, 0)).astype(BF16)
            dva_ref[h, :, ks] += dot(do2_ref[h, 0:64, :], p.astype(BF16), 1, 1)
            dka_ref[h, :, ks] += dot(q2_ref[h, 0:64, :], ds, 1, 1)
            dqa_ref[h] += dot(ka_ref[h, 0:64, ks], ds, 1, 0)

    for h in range(H):
        dq_ref[64 * h : 64 * h + 64, :] = (dqa_ref[h] * HD ** -0.5).astype(BF16)

    @pl.when(step == pl.num_programs(0) - 1)
    def _():
        for h in range(H):
            s = slice(64 * h, 64 * h + 64)
            dk_ref[s, :] = dka_ref[h].astype(BF16)
            dv_ref[s, :] = dva_ref[h].astype(BF16)
            dkm_ref[s, :] = dkma_ref[h].astype(BF16)
            dvm_ref[s, :] = dvma_ref[h].astype(BF16)


def attend_backward(seg2, counts, qa, ka, va, km, vm, mgrad, lse, delta):
    slots = qa.shape[2]
    once = pl.Buffered(1)
    full = pl.BlockSpec((H, HA, slots), lambda i: (0, 0, 0), pipeline_mode=once)
    mfull = pl.BlockSpec((H, HA, 128), lambda i: (0, 0, 0))
    cols = pl.BlockSpec((512, BQ), lambda i: (0, i))
    stat = pl.BlockSpec((H, BQ), lambda i: (0, i))
    whole = pl.BlockSpec((512, slots), lambda i: (0, 0), pipeline_mode=once)
    mwhole = pl.BlockSpec((512, 128), lambda i: (0, 0))
    return pl.pallas_call(
        functools.partial(bwd_kernel, slots),
        grid=(slots // BQ,),
        in_specs=[
            pl.BlockSpec(seg2.shape, lambda i: (0, 0)),
            pl.BlockSpec(memory_space=pltpu.SMEM),
            pl.BlockSpec((H, HA, BQ), lambda i: (0, 0, i)),
            full, full, mfull, mfull, cols, stat, stat,
        ],
        out_specs=[cols, whole, whole, mwhole, mwhole],
        out_shape=[jax.ShapeDtypeStruct((512, slots), BF16)] * 3 + [jax.ShapeDtypeStruct((512, 128), BF16)] * 2,
        scratch_shapes=[
            pltpu.VMEM((H, HA, BQ), BF16),
            pltpu.VMEM((H, HA, BQ), BF16),
            pltpu.VMEM((H, HD, BQ), F32),
            pltpu.VMEM((H, HD, slots), F32),
            pltpu.VMEM((H, HD, slots), F32),
            pltpu.VMEM((H, HD, 128), F32),
            pltpu.VMEM((H, HD, 128), F32),
        ],
        compiler_params=params(),
        name="attend_backward",
    )(seg2, counts, qa, ka, va, km, vm, mgrad, lse, delta)


def tail_kernel(
    g_ref, tok_ref, dq_ref, dk_ref, dv_ref, dkm_ref, dvm_ref, gfirst_ref, vec_ref, bup_ref,
    gtok_ref, gw_ref, wt_ref, acc_ref, sum_ref,
):
    step = pl.program_id(0)

    @pl.when(step == 0)
    def _():
        for j in range(3):
            wt_ref[512 * j : 512 * j + 512, :] = g_ref[:, 16 * j : 16 * j + 16, :].reshape(512, 512).T
        memt = g_ref[:, 48:64, 0:128].reshape(512, 128)
        acc_ref[0:512, :] = jnp.zeros((512, 512), F32)
        acc_ref[512:1024, :] = dot(dkm_ref[...], memt, 1, 1)
        acc_ref[1024:1536, :] = dot(dvm_ref[...], memt, 1, 1)
        sum_ref[...] = jnp.zeros_like(sum_ref)
        sum_ref[:, 1:2] = jnp.sum(dvm_ref[...].astype(F32), axis=1, keepdims=True)

    tok = tok_ref[...]
    dq, dk, dv = dq_ref[...], dk_ref[...], dv_ref[...]
    acc_ref[0:512, :] += dot(dq, tok, 1, 0)
    acc_ref[512:1024, :] += dot(dk, tok, 1, 0)
    acc_ref[1024:1536, :] += dot(dv, tok, 1, 0)
    sum_ref[:, 0:1] += jnp.sum(dq.astype(F32), axis=1, keepdims=True)
    sum_ref[:, 1:2] += jnp.sum(dv.astype(F32), axis=1, keepdims=True)
    gtok_ref[...] = (
        gfirst_ref[...]
        + dot(dq, wt_ref[0:512, :], 0, 0)
        + dot(dk, wt_ref[512:1024, :], 0, 0)
        + dot(dv, wt_ref[1024:1536, :], 0, 0)
    )

    @pl.when(step == pl.num_programs(0) - 1)
    def _():
        for j in range(3):
            gw_ref[:, 16 * j : 16 * j + 16, :] = (
                acc_ref[512 * j : 512 * j + 512, :].T.astype(gw_ref.dtype).reshape(PARTS, 16, 512)
            )
        gmem = dot(wt_ref[512:1024, :], dkm_ref[...], 0, 0) + dot(wt_ref[1024:1536, :], dvm_ref[...], 0, 0)
        gw_ref[:, 48:64, 0:128] = gmem.astype(gw_ref.dtype).reshape(PARTS, 16, 128)
        lane = lax.broadcasted_iota(jnp.int32, (512, 128), 1)
        vecs = jnp.concatenate([vec_ref[...], jnp.zeros((120, 512), F32)], axis=0).T
        vecs = jnp.where(lane < 2, sum_ref[...], vecs)
        gw_ref[:, 48:64, 128:256] = vecs.astype(gw_ref.dtype).reshape(PARTS, 16, 128)
        rows = jnp.concatenate([bup_ref[0:1, 256 * v : 256 * v + 256] for v in range(8)] + [jnp.zeros((8, 256), F32)], axis=0)
        gw_ref[:, 48:64, 256:512] = jnp.broadcast_to(rows[None].astype(gw_ref.dtype), (PARTS, 16, 256))


def tail(g, tokens, dq, dk, dv, dkm, dvm, gfirst, vec, bup, rb=512):
    slots = tokens.shape[0]
    rows = pl.BlockSpec((rb, 512), lambda i: (i, 0))
    cols = pl.BlockSpec((512, rb), lambda i: (0, i))
    mwhole = pl.BlockSpec((512, 128), lambda i: (0, 0))
    once = pl.Buffered(1)
    return pl.pallas_call(
        tail_kernel,
        grid=(slots // rb,),
        in_specs=[
            pl.BlockSpec((PARTS, 64, 512), lambda i: (0, 0, 0), pipeline_mode=once),
            rows, cols, cols, cols, mwhole, mwhole, rows,
            pl.BlockSpec((8, 512), lambda i: (0, 0)),
            pl.BlockSpec((1, 2048), lambda i: (0, 0)),
        ],
        out_specs=[rows, pl.BlockSpec((PARTS, 64, 512), lambda i: (0, 0, 0), pipeline_mode=once)],
        out_shape=[jax.ShapeDtypeStruct((slots, 512), F32), jax.ShapeDtypeStruct((PARTS, 64, 512), BF16)],
        scratch_shapes=[
            pltpu.VMEM((1536, 512), BF16),
            pltpu.VMEM((1536, 512), F32),
            pltpu.VMEM((512, 128), F32),
        ],
        compiler_params=params(),
        name="tail",
    )(g, tokens, dq, dk, dv, dkm, dvm, gfirst, vec, bup)


NAMES = (
    "memory", "w_query", "b_query", "w_key", "w_value", "b_value", "w_out", "b_out", "gain_attn",
    "shift_attn", "w_up", "b_up", "w_down", "b_down", "gain_ffn", "shift_ffn",
)
VECTORS = ("b_query", "b_value", "b_out", "gain_attn", "shift_attn", "b_down", "gain_ffn", "shift_ffn")


def pad_lanes(value, lanes):
    return jnp.pad(value, ((0, 0), (0, lanes - value.shape[1])))


def pack_part(p, me):
    up = p["w_up"].reshape(16, 4, 512).transpose(1, 0, 2).reshape(64, 512)
    memory = pad_lanes(p["memory"].T, 128)
    vectors = pad_lanes(jnp.stack([p[name] for name in VECTORS], axis=1), 128)
    own = jnp.arange(2048) // 64 == me
    b_up = jnp.where(own, jnp.tile(p["b_up"], PARTS), 0).astype(BF16).reshape(8, 256)
    b_up = jnp.pad(b_up, ((0, 8), (0, 0)))
    small = jnp.concatenate([memory, vectors, b_up], axis=1)
    return jnp.concatenate([p["w_query"], p["w_key"], p["w_value"], small, up, p["w_down"], p["w_out"]], axis=0)


def pack_whole(p):
    parts = []
    for d in range(PARTS):
        mine = {}
        for name in NAMES:
            axis = 1 if name == "memory" else 0
            size = p[name].shape[axis] // PARTS
            mine[name] = lax.slice_in_dim(p[name], d * size, d * size + size, axis=axis)
        parts.append(pack_part(mine, d))
    return jnp.stack(parts)


def unpack_part(early, late, mem_rows, me):
    small = late[48:64]
    vectors = small[:, 128:256]
    b_up = small[0:8, 256:512].reshape(2048)
    out = {
        "memory": small[:, 0:mem_rows].T,
        "w_query": late[0:16],
        "w_key": late[16:32],
        "w_value": late[32:48],
        "w_out": early[0:16],
        "w_up": early[16:80].reshape(4, 16, 512).transpose(1, 0, 2).reshape(16, 2048),
        "w_down": early[80:144],
        "b_up": lax.dynamic_slice_in_dim(b_up, me * 64, 64),
    }
    for index, name in enumerate(VECTORS):
        out[name] = vectors[:, index]
    return out


def shards(n, tokens, segment, counts, *rest):
    p = dict(zip(NAMES, rest[:-1]))
    cotangent = rest[-1]
    slots = tokens.shape[0]
    mem_rows = p["memory"].shape[0]
    me = lax.axis_index("dp")
    if n == PARTS:
        g = lax.all_gather(pack_part(p, me), "dp", axis=0, tiled=False)
    else:
        g = pack_whole(
            {k: lax.all_gather(v, "dp", axis=1 if k == "memory" else 0, tiled=True) for k, v in p.items()}
        )
    seg2 = segment.reshape(slots // 128, 128)
    qa, ka, va, km, vm = qkv(g, tokens, segment, counts, mem_rows)
    mixt, lse = attend_forward(seg2, counts, qa, ka, va, km, vm)
    output, gfirst, mgrad, delta, early, vec, bup = middle(g, counts, mixt, tokens, cotangent)
    dq, dk, dv, dkm, dvm = attend_backward(seg2, counts, qa, ka, va, km, vm, mgrad, lse, delta)
    gtok, late = tail(g, tokens, dq, dk, dv, dkm, dvm, gfirst, vec, bup)
    if n == PARTS:
        early = lax.psum_scatter(early.astype(F32), "dp", scatter_dimension=0)
        late = lax.psum_scatter(late.astype(F32), "dp", scatter_dimension=0)
        grads = unpack_part(early, late, mem_rows, me)
    else:
        parts = [unpack_part(early[d].astype(F32), late[d].astype(F32), mem_rows, d) for d in range(PARTS)]
        grads = {}
        for name in NAMES:
            axis = 1 if name == "memory" else 0
            whole = jnp.concatenate([part[name] for part in parts], axis=axis)
            grads[name] = lax.psum_scatter(whole, "dp", scatter_dimension=axis, tiled=True)
    return (output, gtok) + tuple(grads[name] for name in NAMES)


def solution(mesh):
    n = mesh.shape["dp"]
    row, mat, mem = P("dp"), P("dp", None), P(None, "dp")
    spec = {name: mat if name.startswith("w_") else row for name in NAMES}
    spec["memory"] = mem
    weights = tuple(spec[name] for name in NAMES)
    return jax.shard_map(
        functools.partial(shards, n),
        mesh=mesh,
        in_specs=(mat, row, row) + weights + (mat,),
        out_specs=(mat, mat) + weights,
        check_vma=False,
    )
```

time: 2040 us -> 661 us (0.32)
  matrix products: 603 us -> 0 us
  waiting for transfers between devices: 836 us -> 392 us
  blocking collectives: 279 us -> 0 us
  Pallas kernels: 0 us -> 227 us
  other arithmetic: 207 us -> 12.1 us
  local copies, waits for them, and re-layouts: 92.5 us -> 14 us
    dot_general x80 -> x0, matrix products: 603 us -> none  [the longest x8 158 us: score_block(): jnp.einsum('qhd,khd->hqk', query_block, key_heads, preferred_element_type...]
    unnamed x12 -> x3, waiting for transfers between devices: 402 us -> 0.05 us
    pallas_call x0 -> x5, Pallas kernels: none -> 227 us  [the longest x1 79 us: attend_backward(): pl.pallas_call(functools.partial(bwd_kernel, slots), grid=(slots // BQ,),...]
    all_gather x5 -> x0, blocking collectives: 200 us -> none  [the longest x1 42.2 us: shards(): lax.all_gather(w_out, 'dp', axis=0, tiled=True)]
    reduce_scatter x4 -> x2, waiting for transfers between devices: 434 us -> 318 us  [the longest x1 184 us: shards(): late = lax.psum_scatter(late.astype(F32), 'dp', scatter_dimension=0)]
    convert_element_type x19 -> x2, other arithmetic: 117 us -> 11.4 us  [the longest x1 7.32 us: shards(): early = lax.psum_scatter(early.astype(F32), 'dp', scatter_dimension=0)]
    unnamed x2 -> x0, blocking collectives: 79.5 us -> none
    reduce_sum x17 -> x0, other arithmetic: 75.9 us -> none  [the longest x8 60.4 us: forward_block(): total = jnp.sum(tok_exp, axis=-1) + jnp.sum(mem_exp, axis=-1)]
  transfers between devices with their start and end apart: 9 -> 3, of which waited for: 7 -> 3; matrix products, arithmetic and copies ran while one was open for 18% -> 2% of each run, Pallas kernels for 0% -> 0%
where the time goes in v1:
time: 661 us; the launch traced here: 660 us
  waiting for transfers between devices  392 us (59%)
  Pallas kernels  227 us (34%)
  between operations  14.4 us (2%)
  local copies, waits for them, and re-layouts  14 us (2%)
  other arithmetic  12.1 us (2%)
    reduce_scatter x1, waiting for transfers between devices, shards(): late = lax.psum_scatter(late.astype(F32), 'dp', scatter_dimension=0)  184 us
    reduce_scatter x1, waiting for transfers between devices, shards(): early = lax.psum_scatter(early.astype(F32), 'dp', scatter_dimension=0)  134 us
    pallas_call x1, Pallas kernels, attend_backward(): pl.pallas_call(functools.partial(bwd_kernel, slots), grid=(slots // BQ,),...  79 us
    pallas_call x1, Pallas kernels, attend_forward(): pl.pallas_call(functools.partial(fwd_kernel, slots), grid=(slots // BQ,),...  74.5 us
    all_gather x1, waiting for transfers between devices, shards(): g = lax.all_gather(pack_part(p, me), 'dp', axis=0, tiled=False)  73.6 us
    pallas_call x1, Pallas kernels, middle(): pl.pallas_call(functools.partial(mid_kernel, rb), grid=(slots // rb,), in...  51.5 us
    pallas_call x1, Pallas kernels, tail(): pl.pallas_call(tail_kernel, grid=(slots // rb,), in_specs=[pl.BlockSpec((...  13.7 us
  transfers between devices with their start and end apart: 3, of which 3 were waited for; matrix products, arithmetic and copies ran while one was open for 2% of the time, Pallas kernels for 0%

profile of v1, /device:TPU:0, one launch (start us, length us, event | category | flops | bytes accessed | tf_op | source)
XLA Modules:
  0.0 660.3 jit_solution(16665806534618957335)
XLA Ops:
  8.0 0.8 stack.35
  8.9 0.8 copy.49
  9.7 0.7 constant_dynamic-update-slice_fusion.5
  10.4 0.7 constant_dynamic-update-slice_fusion.4
  11.2 0.7 constant_dynamic-update-slice_fusion.3
  11.9 0.7 fusion.6
  12.6 0.8 constant_dynamic-update-slice_fusion.1
  13.4 0.7 constant_dynamic-update-slice_fusion
  14.2 0.7 copy-done
  15.6 73.6 %all-gather.3.cloned.1.call-done = bf16[6656,512]{1,0:T(8,128)(2,1)} async-done(((bf16[208,512]{1,0:T(8,128)(2,1)}), bf16[6656,512]{1,0:T(8,128)(2,1)}) %all-gather.3.cloned.1.call-update) | async-done | bytes 6815760 | tf_op jit(solution)/shard_map/all_gather | solution.py:539
  89.2 8.7 %qkv.1 = (bf16[8,80,2048]{2,1,0:T(8,128)(2,1)}, bf16[8,80,2048]{2,1,0:T(8,128)(2,1)}, bf16[8,80,2048]{2,1,0:T(8,128)(2,1)}, bf16[8,80,128]{2,1,0:T(8,128)(2,1)}, bf16[8,80,128]{2,1,0:T(8,128)(2,1)}) custom-call(bf16[32,208,512]{2,1,0:T(8,128)(2,1)} %bitcast.41, bf16[2048,512]{1,0:T(8,128)(2,1)} %tok_ref.5, s32[1,2048]{1,0:T(1,128)} %bitcast.50, ...), custom_call_target="tpu_custom_call" | custom-call | tf_op jit(solution)/shard_map/qkv/pallas_call | solution.py:85
  98.0 74.5 %attend_forward.1 = (bf16[512,2048]{1,0:T(8,128)(2,1)}, f32[8,2048]{1,0:T(8,128)}) custom-call(s32[16,128]{1,0:T(8,128)} %bitcast.51, s32[1]{0:T(128)S(6)} %copy.56.cnt_ref, bf16[8,80,2048]{2,1,0:T(8,128)(2,1)} %get-tuple-element.39.qa_ref, bf16[8,80,2048]{2,1,0:T(8,128)(2,1)} %get-tuple-element.40.ka_ref, bf16[8,80,2048]{2,1,0:T(8,128)(2,1)} %get-tuple-element.41.va_ref, ...), custom_call_target="tpu_custom_call" | custom-call | tf_op jit(solution)/shard_map/attend_forward/pallas_call | solution.py:150
  172.5 51.5 %middle.1 = (bf16[2048,512]{1,0:T(8,128)(2,1)}, f32[2048,512]{1,0:T(8,128)}, bf16[512,2048]{1,0:T(8,128)(2,1)}, f32[8,2048]{1,0:T(8,128)}, bf16[32,144,512]{2,1,...) custom-call(s32[1]{0:T(128)S(6)} %copy.56.cnt_ref, bf16[32,208,512]{2,1,0:T(8,128)(2,1)} %bitcast.42, ...), custom_call_target="tpu_custom_call" | custom-call | tf_op jit(solution)/shard_map/middle/pallas_call | solution.py:267
  224.0 79.0 %attend_backward.1 = (bf16[512,2048]{1,0:T(8,128)(2,1)}, bf16[512,2048]{1,0:T(8,128)(2,1)}, bf16[512,2048]{1,0:T(8,128)(2,1)}, bf16[512,128]{1,0:T(8,128)(2,1)}, bf16[512,128]{1,0:T(8,128)(2,1)}) custom-call(s32[16,128]{1,0:T(8,128)} %bitcast.52, s32[1]{0:T(128)S(6)} %copy.56.cnt_ref, bf16[8,80,2048]{2,1,0:T(8,128)(2,1)} %get-tuple-element.39.qa_ref, ...), custom_call_target="tpu_custom_call" | custom-call | tf_op jit(solution)/shard_map/attend_backward/pallas_call | solution.py:380
  303.0 13.7 %tail.1 = (f32[2048,512]{1,0:T(8,128)}, bf16[32,64,512]{2,1,0:T(8,128)(2,1)}) custom-call(bf16[32,208,512]{2,1,0:T(8,128)(2,1)} %bitcast.46, bf16[2048,512]{1,0:T(8,128)(2,1)} %tok_ref.5, bf16[512,2048]{1,0:T(8,128)(2,1)} %get-tuple-element.49.dq_ref, bf16[512,2048]{1,0:T(8,128)(2,1)} %get-tuple-element.50.dk_ref, ...), custom_call_target="tpu_custom_call" | custom-call | tf_op jit(solution)/shard_map/tail/pallas_call | solution.py:458
  316.7 4.1 convert_element_type.14
  320.8 7.3 %convert_element_type.15 = f32[32,144,512]{2,1,0:T(8,128)} convert(bf16[32,144,512]{2,1,0:T(8,128)(2,1)} %get-tuple-element.59) | non-fusion elementwise | flops 2359296 | bytes 14155776 | tf_op jit(solution)/shard_map/convert_element_type | solution.py:551
  328.2 184.4 %reduce-scatter.3.cloned.1.call-done = f32[1,64,512]{2,1,0:T(8,128)} async-done(((f32[32,64,512]{2,1,0:T(8,128)}), f32[1,64,512]{2,1,0:T(8,128)}) %reduce-scatter.3.cloned.1.call-update) | async-done | bytes 131088 | tf_op jit(solution)/shard_map/reduce_scatter | solution.py:552
  512.6 1.4 slice_bitcast_fusion.2
  514.7 0.8 slice_reduce_fusion
  516.1 134.0 %reduce-scatter.5.cloned.1.call-done = f32[1,144,512]{2,1,0:T(8,128)} async-done(((f32[32,144,512]{2,1,0:T(8,128)}), f32[1,144,512]{2,1,0:T(8,128)}) %reduce-scatter.5.cloned.1.call-update) | async-done | bytes 294928 | tf_op jit(solution)/shard_map/reduce_scatter | solution.py:551
  650.1 1.6 slice_bitcast_fusion
  651.7 0.7 copy.46
  652.4 1.4 slice_bitcast_fusion.1
  (16 shorter events, 2.2 us)
Async XLA Ops:
  7.2 82.0 %all-gather.3.cloned.1.call-start = ((), (), s32[]{:S(2)}) async-start(), calls=%async_computation.4 | async-start | bytes 7028736 | tf_op jit(solution)/shard_map/all_gather | solution.py:539
  14.2 0.7 copy-start
  14.9 497.8 %reduce-scatter.3.cloned.1.call-start = ((), (), s32[]{:S(2)}) async-start(), calls=%async_computation.2 | async-start | bytes 4325376 | tf_op jit(solution)/shard_map/reduce_scatter | solution.py:552
  320.8 329.3 %reduce-scatter.5.cloned.1.call-start = ((), (), s32[]{:S(2)}) async-start(), calls=%async_computation.3 | async-start | bytes 9732096 | tf_op jit(solution)/shard_map/reduce_scatter | solution.py:551
Sparse Core Ops, SparseCore 0:
  15.0 74.1 all-gather.2
  320.9 191.6 reduce-scatter.2
  518.5 131.4 reduce-scatter.4

commit v2 on v1

--- a/solution.py
+++ b/solution.py
@@ -476,6 +476,266 @@
     )(g, tokens, dq, dk, dv, dkm, dvm, gfirst, vec, bup)
 
 
+MESH = pl.DeviceIdType.MESH
+AXES = {"z": (8, 4), "y": (4, 2), "x": (2, 2)}
+LAYOUT = ("z", "y", "x")
+
+
+class Place:
+    def __init__(self):
+        me = lax.axis_index("dp")
+        self.me = me
+        self.core = me % 2
+        self.partner = me + 1 - 2 * self.core
+        self.at = {a: (me // stride) % length for a, (stride, length) in AXES.items()}
+        self.mine = tuple(self.at[a] for a in LAYOUT)
+
+    def other(self, axis, distance):
+        stride, length = AXES[axis]
+        j = (self.at[axis] + distance) % length
+        return j, self.me + (j - self.at[axis]) * stride
+
+    def greet(self):
+        barrier = pltpu.get_barrier_semaphore()
+        peers = [self.partner]
+        for axis in LAYOUT:
+            peers += [self.other(axis, d)[1] for d in range(1, AXES[axis][1])]
+        for peer in peers:
+            pl.semaphore_signal(barrier, inc=1, device_id=(peer,), device_id_type=MESH)
+        pl.semaphore_wait(barrier, len(peers))
+
+
+class Copies:
+    def __init__(self, send, recv):
+        self.send, self.recv, self.count, self.open = send, recv, 0, []
+
+    def number(self):
+        self.count += 1
+        return self.count - 1
+
+    def make(self, src, dst, number, device):
+        return pltpu.make_async_remote_copy(
+            src_ref=src, dst_ref=dst, send_sem=self.send.at[number], recv_sem=self.recv.at[number],
+            device_id=(device,), device_id_type=MESH,
+        )
+
+    def start(self, src, dst, number, device):
+        copy = self.make(src, dst, number, device)
+        copy.start()
+        self.open.append(copy)
+
+    def landed(self, block, number, device):
+        self.make(block, block, number, device).wait_recv()
+
+    def finish(self):
+        for copy in self.open:
+            copy.wait_send()
+        self.open = []
+
+
+def run_events(parts):
+    live = []
+    for index, part in enumerate(parts):
+        live.append([next(part), index, part])
+    while live:
+        live.sort(key=lambda item: item[:2])
+        item = live[0]
+        try:
+            item[0] = next(item[2])
+        except StopIteration:
+            live.pop(0)
+
+
+LOAD = {2: 1.0, 4: 4.0}
+HOP = 120.0
+
+
+def gather_part(place, copies, own, whole, rows, order, arrivals):
+    size, known, clock, done = rows.stop - rows.start, 1, 0.0, ()
+
+    def block(axis, j, core):
+        index = tuple(j if a == axis else (slice(None) if a in done else place.at[a]) for a in LAYOUT)
+        return whole.at[index + (core, rows)]
+
+    for axis in order:
+        length = AXES[axis][1]
+        numbers = [copies.number() for _ in range(2 * length - 2)]
+        here = block(axis, place.at[axis], place.core)
+        for d in range(1, length):
+            copies.start(here if done else own.at[rows], here, numbers[d - 1], place.other(axis, d)[1])
+        clock += LOAD[length] * known * size + HOP
+        yield clock
+        for d in range(1, length):
+            j, device = place.other(axis, length - d)
+            there = block(axis, j, place.core)
+            copies.landed(there, numbers[d - 1], device)
+            copies.start(there, there, numbers[length - 2 + d], place.partner)
+            arrivals.append((block(axis, j, 1 - place.core), numbers[length - 2 + d]))
+        done += (axis,)
+        known *= length
+
+
+def gather_all(place, copies, own, whole, parts):
+    arrivals = []
+    for rows, _ in parts:
+        number = copies.number()
+        copies.start(own.at[rows], whole.at[place.mine + (place.core, rows)], number, place.partner)
+        arrivals.append((whole.at[place.mine + (1 - place.core, rows)], number))
+    run_events([gather_part(place, copies, own, whole, rows, order, arrivals) for rows, order in parts])
+    return arrivals
+
+
+GATHER_PARTS = (
+    (slice(0, 32), "zxy"),
+    (slice(32, 64), "zyx"),
+    (slice(64, 96), "yzx"),
+    (slice(96, 128), "xzy"),
+    (slice(128, 160), "zxy"),
+    (slice(160, 208), "zyx"),
+)
+GATHER_COPIES = 11 * len(GATHER_PARTS)
+
+
+def gather_kernel(parts, own_ref, whole_ref, send, recv, local):
+    place = Place()
+    place.greet()
+    copies = Copies(send, recv)
+    keep = pltpu.make_async_copy(own_ref, whole_ref.at[place.mine + (place.core,)], local)
+    keep.start()
+    keep.wait()
+    arrivals = gather_all(place, copies, own_ref, whole_ref, parts)
+    for block, number in arrivals:
+        copies.landed(block, number, place.partner)
+    copies.finish()
+
+
+def gather(packed):
+    whole = pl.pallas_call(
+        functools.partial(gather_kernel, GATHER_PARTS),
+        in_specs=[pl.BlockSpec(memory_space=pltpu.VMEM)],
+        out_specs=pl.BlockSpec(memory_space=pl.ANY),
+        out_shape=jax.ShapeDtypeStruct((4, 2, 2, 2, ROWS, 512), BF16),
+        scratch_shapes=[
+            pltpu.SemaphoreType.DMA((GATHER_COPIES,)),
+            pltpu.SemaphoreType.DMA((GATHER_COPIES,)),
+            pltpu.SemaphoreType.DMA,
+        ],
+        compiler_params=params(collective_id=0, has_side_effects=True),
+        name="gather",
+    )(packed)
+    return whole.reshape(PARTS, ROWS, 512)
+
+
+def scatter_part(place, copies, acc, slots, out, rows, order):
+    size, clock, done = rows.stop - rows.start, 0.0, ()
+    left = 16
+
+    def block(axis, j):
+        index = tuple(j if a == axis else (place.at[a] if a in done else slice(None)) for a in LAYOUT)
+        return index + (rows,)
+
+    for axis in order:
+        length = AXES[axis][1]
+        left //= length
+        numbers = [copies.number() for _ in range(length - 1)]
+        for d in range(1, length):
+            j, device = place.other(axis, d)
+            copies.start(acc.at[block(axis, j)], slots[axis, d], numbers[d - 1], device)
+        clock += LOAD[length] * left * size + HOP
+        yield clock
+        for d in range(1, length):
+            copies.landed(slots[axis, d], numbers[d - 1], place.partner)
+        mine = block(axis, place.at[axis])
+        total = acc[mine].astype(F32)
+        for d in range(1, length):
+            total = total + slots[axis, d][...].astype(F32)
+        if axis == order[-1]:
+            out[rows, :] = total
+        else:
+            acc[mine] = total.astype(BF16)
+        done += (axis,)
+
+
+SCATTER_PARTS = (
+    (slice(64, 96), "yxz"),
+    (slice(96, 128), "xyz"),
+    (slice(128, 144), "xzy"),
+    (slice(144, 160), "yzx"),
+    (slice(160, 176), "xzy"),
+    (slice(176, 208), "yxz"),
+    (slice(0, 32), "xyz"),
+    (slice(32, 64), "yxz"),
+)
+SCATTER_COPIES = 6 * len(SCATTER_PARTS)
+
+
+def slot_shapes(parts):
+    shapes = {}
+    for number, (rows, order) in enumerate(parts):
+        left = ["z", "y", "x"]
+        for axis in order:
+            left.remove(axis)
+            shape = tuple(AXES[a][1] for a in LAYOUT if a in left) + (rows.stop - rows.start, 512)
+            for d in range(1, AXES[axis][1]):
+                shapes[number, axis, d] = shape
+    return shapes
+
+
+def scatter_kernel(all_parts, late_ref, early_ref, out_ref, acc, other, send, recv, local, *landing):
+    place = Place()
+    slots = dict(zip(slot_shapes(all_parts), landing))
+
+    def source(rows, core):
+        if rows.start < 64:
+            return late_ref.at[:, :, :, core, rows]
+        return early_ref.at[:, :, :, core, slice(rows.start - 64, rows.stop - 64)]
+
+    loads = [
+        pltpu.make_async_copy(source(rows, place.core), acc.at[:, :, :, rows], local.at[index])
+        for index, (rows, _) in enumerate(all_parts)
+    ]
+    place.greet()
+    copies = Copies(send, recv)
+    numbers = [copies.number() for _ in all_parts]
+    for load, number, (rows, _) in zip(loads, numbers, all_parts):
+        copies.start(source(rows, 1 - place.core), other.at[:, :, :, rows], number, place.partner)
+        load.start()
+    parts = []
+    for index, (rows, order) in enumerate(all_parts):
+        loads[index].wait()
+        copies.landed(other.at[:, :, :, rows], numbers[index], place.partner)
+
+        @pl.loop(0, 4)
+        def _(z):
+            acc[z, :, :, rows] = (acc[z, :, :, rows].astype(F32) + other[z, :, :, rows].astype(F32)).astype(BF16)
+
+        mine = {key[1:]: slot for key, slot in slots.items() if key[0] == index}
+        parts.append(scatter_part(place, copies, acc, mine, out_ref, rows, order))
+        next(parts[-1])
+    run_events(parts)
+    copies.finish()
+
+
+def scatter(late, early):
+    shapes = slot_shapes(SCATTER_PARTS)
+    return pl.pallas_call(
+        functools.partial(scatter_kernel, SCATTER_PARTS),
+        in_specs=[pl.BlockSpec(memory_space=pl.ANY)] * 2,
+        out_specs=pl.BlockSpec(memory_space=pltpu.VMEM),
+        out_shape=jax.ShapeDtypeStruct((ROWS, 512), F32),
+        scratch_shapes=[
+            pltpu.VMEM((4, 2, 2, ROWS, 512), BF16),
+            pltpu.VMEM((4, 2, 2, ROWS, 512), BF16),
+            pltpu.SemaphoreType.DMA((SCATTER_COPIES,)),
+            pltpu.SemaphoreType.DMA((SCATTER_COPIES,)),
+            pltpu.SemaphoreType.DMA((len(SCATTER_PARTS),)),
+        ]
+        + [pltpu.VMEM(shape, BF16) for shape in shapes.values()],
+        compiler_params=params(collective_id=1, has_side_effects=True),
+        name="scatter",
+    )(late.reshape(4, 2, 2, 2, 64, 512), early.reshape(4, 2, 2, 2, 144, 512))
+
+
 NAMES = (
     "memory", "w_query", "b_query", "w_key", "w_value", "b_value", "w_out", "b_out", "gain_attn",
     "shift_attn", "w_up", "b_up", "w_down", "b_down", "gain_ffn", "shift_ffn",
@@ -536,7 +796,7 @@
     mem_rows = p["memory"].shape[0]
     me = lax.axis_index("dp")
     if n == PARTS:
-        g = lax.all_gather(pack_part(p, me), "dp", axis=0, tiled=False)
+        g = gather(pack_part(p, me))
     else:
         g = pack_whole(
             {k: lax.all_gather(v, "dp", axis=1 if k == "memory" else 0, tiled=True) for k, v in p.items()}
@@ -548,9 +808,8 @@
     dq, dk, dv, dkm, dvm = attend_backward(seg2, counts, qa, ka, va, km, vm, mgrad, lse, delta)
     gtok, late = tail(g, tokens, dq, dk, dv, dkm, dvm, gfirst, vec, bup)
     if n == PARTS:
-        early = lax.psum_scatter(early.astype(F32), "dp", scatter_dimension=0)
-        late = lax.psum_scatter(late.astype(F32), "dp", scatter_dimension=0)
-        grads = unpack_part(early, late, mem_rows, me)
+        owned = scatter(late, early)
+        grads = unpack_part(owned[64:ROWS], owned[0:64], mem_rows, me)
     else:
         parts = [unpack_part(early[d].astype(F32), late[d].astype(F32), mem_rows, d) for d in range(PARTS)]
         grads = {}

time: 661 us -> 397 us (0.60)
  waiting for transfers between devices: 392 us -> 0 us
  Pallas kernels: 227 us -> 373 us
  between operations: 14.4 us -> 1.35 us
  other arithmetic: 12.1 us -> 0.71 us
    reduce_scatter x2 -> x0, waiting for transfers between devices: 318 us -> none  [the longest x1 184 us: shards(): late = lax.psum_scatter(late.astype(F32), 'dp', scatter_dimension=0)]
    pallas_call x0 -> x2, Pallas kernels: none -> 110 us  [the longest x1 61.9 us: scatter(): pl.pallas_call(functools.partial(scatter_kernel, SCATTER_PARTS), in_specs...]
    all_gather x1 -> x0, waiting for transfers between devices: 73.6 us -> none  [shards(): g = lax.all_gather(pack_part(p, me), 'dp', axis=0, tiled=False)]
    pallas_call x1, Pallas kernels: 74.5 us -> 92.5 us  [attend_forward(): pl.pallas_call(functools.partial(fwd_kernel, slots), grid=(slots // BQ,),...]
    pallas_call x1, Pallas kernels: 79 us -> 95.8 us  [attend_backward(): pl.pallas_call(functools.partial(bwd_kernel, slots), grid=(slots // BQ,),...]
    convert_element_type x2 -> x0, other arithmetic: 11.4 us -> none  [the longest x1 7.32 us: shards(): early = lax.psum_scatter(early.astype(F32), 'dp', scatter_dimension=0)]
  transfers between devices with their start and end apart: 3 -> 0, of which waited for: 3 -> 0; matrix products, arithmetic and copies ran while one was open for 2% -> 0% of each run, Pallas kernels for 0% -> 0%
where the time goes in v2:
time: 397 us; the launch traced here: 395 us
  Pallas kernels  373 us (94%)
  local copies, waits for them, and re-layouts  20.2 us (5%)
    pallas_call x1, Pallas kernels, attend_backward(): pl.pallas_call(functools.partial(bwd_kernel, slots), grid=(slots // BQ,),...  95.8 us
    pallas_call x1, Pallas kernels, attend_forward(): pl.pallas_call(functools.partial(fwd_kernel, slots), grid=(slots // BQ,),...  92.5 us
    pallas_call x1, Pallas kernels, scatter(): pl.pallas_call(functools.partial(scatter_kernel, SCATTER_PARTS), in_specs...  61.9 us
    pallas_call x1, Pallas kernels, middle(): pl.pallas_call(functools.partial(mid_kernel, rb), grid=(slots // rb,), in...  51.6 us
    pallas_call x1, Pallas kernels, gather(): pl.pallas_call(functools.partial(gather_kernel, GATHER_PARTS), in_specs=[...  48.5 us
    pallas_call x1, Pallas kernels, tail(): pl.pallas_call(tail_kernel, grid=(slots // rb,), in_specs=[pl.BlockSpec((...  13.6 us
    pallas_call x1, Pallas kernels, qkv(): pl.pallas_call(functools.partial(qkv_kernel, mem_rows), grid=(slots // rb...  8.78 us

profile of v2, /device:TPU:0, one launch (start us, length us, event | category | flops | bytes accessed | tf_op | source)
XLA Modules:
  0.0 395.0 jit_solution(10656641940946858953)
XLA Ops:
  2.1 0.7 copy.48
  2.8 0.7 copy.49
  3.6 0.7 copy.50
  4.3 0.7 copy.51
  5.0 0.7 copy.52
  5.8 0.7 copy.53
  6.5 0.7 copy.54
  7.3 0.7 copy.55
  8.1 0.8 copy.62
  9.0 0.7 constant_dynamic-update-slice_fusion.5
  9.7 0.7 constant_dynamic-update-slice_fusion.4
  10.4 0.7 constant_dynamic-update-slice_fusion.3
  11.8 0.8 constant_dynamic-update-slice_fusion.1
  14.1 48.5 %gather.1 = bf16[4,2,2,2,208,512]{5,4,3,2,1,0:T(8,128)(2,1)} custom-call(bf16[208,512]{1,0:T(8,128)(2,1)} %copy-done), custom_call_target="tpu_custom_call" | custom-call | tf_op jit(solution)/shard_map/gather/pallas_call | solution.py:613
  62.6 8.8 %qkv.1 = (bf16[8,80,2048]{2,1,0:T(8,128)(2,1)}, bf16[8,80,2048]{2,1,0:T(8,128)(2,1)}, bf16[8,80,2048]{2,1,0:T(8,128)(2,1)}, bf16[8,80,128]{2,1,0:T(8,128)(2,1)}, bf16[8,80,128]{2,1,0:T(8,128)(2,1)}) custom-call(bf16[32,208,512]{2,1,0:T(8,128)(2,1)} %bitcast.31, bf16[2048,512]{1,0:T(8,128)(2,1)} %tok_ref.5, s32[1,2048]{1,0:T(1,128)} %bitcast.42, ...), custom_call_target="tpu_custom_call" | custom-call | tf_op jit(solution)/shard_map/qkv/pallas_call | solution.py:85
  71.4 92.5 %attend_forward.1 = (bf16[512,2048]{1,0:T(8,128)(2,1)}, f32[8,2048]{1,0:T(8,128)}) custom-call(s32[16,128]{1,0:T(8,128)} %bitcast.43, s32[1]{0:T(128)S(6)} %copy.69.cnt_ref, bf16[8,80,2048]{2,1,0:T(8,128)(2,1)} %get-tuple-element.39.qa_ref, bf16[8,80,2048]{2,1,0:T(8,128)(2,1)} %get-tuple-element.40.ka_ref, bf16[8,80,2048]{2,1,0:T(8,128)(2,1)} %get-tuple-element.41.va_ref, ...), custom_call_target="tpu_custom_call" | custom-call | tf_op jit(solution)/shard_map/attend_forward/pallas_call | solution.py:150
  163.9 51.6 %middle.1 = (bf16[2048,512]{1,0:T(8,128)(2,1)}, f32[2048,512]{1,0:T(8,128)}, bf16[512,2048]{1,0:T(8,128)(2,1)}, f32[8,2048]{1,0:T(8,128)}, bf16[32,144,512]{2,1,...) custom-call(s32[1]{0:T(128)S(6)} %copy.69.cnt_ref, bf16[32,208,512]{2,1,0:T(8,128)(2,1)} %bitcast.32, ...), custom_call_target="tpu_custom_call" | custom-call | tf_op jit(solution)/shard_map/middle/pallas_call | solution.py:267
  215.5 95.8 %attend_backward.1 = (bf16[512,2048]{1,0:T(8,128)(2,1)}, bf16[512,2048]{1,0:T(8,128)(2,1)}, bf16[512,2048]{1,0:T(8,128)(2,1)}, bf16[512,128]{1,0:T(8,128)(2,1)}, bf16[512,128]{1,0:T(8,128)(2,1)}) custom-call(s32[16,128]{1,0:T(8,128)} %bitcast.44, s32[1]{0:T(128)S(6)} %copy.69.cnt_ref, bf16[8,80,2048]{2,1,0:T(8,128)(2,1)} %get-tuple-element.39.qa_ref, ...), custom_call_target="tpu_custom_call" | custom-call | tf_op jit(solution)/shard_map/attend_backward/pallas_call | solution.py:380
  311.3 13.6 %tail.1 = (f32[2048,512]{1,0:T(8,128)}, bf16[32,64,512]{2,1,0:T(8,128)(2,1)}) custom-call(bf16[32,208,512]{2,1,0:T(8,128)(2,1)} %bitcast.36, bf16[2048,512]{1,0:T(8,128)(2,1)} %tok_ref.5, bf16[512,2048]{1,0:T(8,128)(2,1)} %get-tuple-element.49.dq_ref, bf16[512,2048]{1,0:T(8,128)(2,1)} %get-tuple-element.50.dk_ref, ...), custom_call_target="tpu_custom_call" | custom-call | tf_op jit(solution)/shard_map/tail/pallas_call | solution.py:458
  324.9 61.9 %scatter.1 = f32[208,512]{1,0:T(8,128)} custom-call(bf16[4,2,2,2,64,512]{5,4,3,2,1,0:T(8,128)(2,1)} %bitcast.38, bf16[4,2,2,2,144,512]{5,4,3,2,1,0:T(8,128)(2,1)} %bitcast.37), custom_call_target="tpu_custom_call" | custom-call | tf_op jit(solution)/shard_map/scatter/pallas_call | solution.py:721
  386.8 1.8 slice_reduce_fusion
  389.9 1.3 slice_bitcast_fusion.1
  391.2 1.5 fusion.13
  392.7 1.6 fusion.12
  (13 shorter events, 4.9 us)
Async XLA Ops:
  13.4 0.7 copy-start

commit v3 on v2

--- a/solution.py
+++ b/solution.py
@@ -31,7 +31,15 @@
     return pltpu.CompilerParams(vmem_limit_bytes=VMEM_LIMIT, **kw)
 
 
-def qkv_kernel(mem_rows, g_ref, tok_ref, seg_ref, cnt_ref, qa_ref, ka_ref, va_ref, km_ref, vm_ref, wt_ref):
+def head_block(rows, features):
+    block = jnp.concatenate([rows, features], axis=0)
+    return block, jnp.concatenate([block, jnp.zeros((128 - HA, rows.shape[1]), BF16)], axis=0).T
+
+
+def qkv_kernel(
+    mem_rows, g_ref, tok_ref, seg_ref, cnt_ref,
+    qa_ref, ka_ref, va_ref, kn_ref, vn_ref, km_ref, vm_ref, kmn_ref, vmn_ref, wt_ref,
+):
     step = pl.program_id(0)
     rows = tok_ref.shape[0]
     small = g_ref[:, 48:64, :].reshape(512, 512)
@@ -50,10 +58,10 @@
         kf = jnp.where(frow < 3, jnp.where(lane < mem_rows, 0.0, 1.0), jnp.where(frow < 6, 1.0, 0.0)).astype(BF16)
         vf = jnp.where(frow < 3, 1.0, 0.0).astype(BF16)
         for h in range(H):
-            km_ref[h, 0:64, :] = km[64 * h : 64 * h + 64, :]
-            km_ref[h, 64:80, :] = kf
-            vm_ref[h, 0:64, :] = vm[64 * h : 64 * h + 64, :]
-            vm_ref[h, 64:80, :] = vf
+            km_ref[h], turned = head_block(km[64 * h : 64 * h + 64, :], kf)
+            kmn_ref[h] = turned[0:MP]
+            vm_ref[h], turned = head_block(vm[64 * h : 64 * h + 64, :], vf)
+            vmn_ref[h] = turned[0:MP]
 
     tok = tok_ref[...]
     q = ((dot(wt_ref[0:512, :], tok, 1, 1) + bq).astype(BF16) * jnp.asarray(HD ** -0.5, BF16))
@@ -70,18 +78,21 @@
         s = slice(64 * h, 64 * h + 64)
         qa_ref[h, 0:64, :] = q[s]
         qa_ref[h, 64:80, :] = qf
-        ka_ref[h, 0:64, :] = k[s]
-        ka_ref[h, 64:80, :] = kf
-        va_ref[h, 0:64, :] = v[s]
-        va_ref[h, 64:80, :] = vf
+        ka_ref[h], kn_ref[h] = head_block(k[s], kf)
+        va_ref[h], vn_ref[h] = head_block(v[s], vf)
 
 
 def qkv(g, tokens, segment, counts, mem_rows):
     slots = tokens.shape[0]
     rb = 512
-    out = [jax.ShapeDtypeStruct((H, HA, slots), BF16)] * 3 + [jax.ShapeDtypeStruct((H, HA, 128), BF16)] * 2
+    wide = jax.ShapeDtypeStruct((H, HA, slots), BF16)
+    tall = jax.ShapeDtypeStruct((H, slots, 128), BF16)
+    mwide = jax.ShapeDtypeStruct((H, HA, 128), BF16)
+    mtall = jax.ShapeDtypeStruct((H, MP, 128), BF16)
     blk = pl.BlockSpec((H, HA, rb), lambda i: (0, 0, i))
+    tblk = pl.BlockSpec((H, rb, 128), lambda i: (0, i, 0))
     mblk = pl.BlockSpec((H, HA, 128), lambda i: (0, 0, 0))
+    mtblk = pl.BlockSpec((H, MP, 128), lambda i: (0, 0, 0))
     return pl.pallas_call(
         functools.partial(qkv_kernel, mem_rows),
         grid=(slots // rb,),
@@ -91,62 +102,111 @@
             pl.BlockSpec((1, rb), lambda i: (0, i)),
             pl.BlockSpec(memory_space=pltpu.SMEM),
         ],
-        out_specs=[blk, blk, blk, mblk, mblk],
-        out_shape=out,
+        out_specs=[blk, blk, blk, tblk, tblk, mblk, mblk, mtblk, mtblk],
+        out_shape=[wide, wide, wide, tall, tall, mwide, mwide, mtall, mtall],
         scratch_shapes=[pltpu.VMEM((1536, 512), BF16)],
         compiler_params=params(),
         name="qkv",
     )(g, tokens, segment.reshape(1, slots), counts)
 
 
-def key_range(seg, count, first, slots):
+def key_ranges(seg, count, slots, out):
     r, c = seg.shape
     pos = lax.broadcasted_iota(jnp.int32, (r, c), 0) * c + lax.broadcasted_iota(jnp.int32, (r, c), 1)
     valid = pos < count
-    last = jnp.minimum(first + BQ, count)
-    low, high, start = jnp.int32(slots), jnp.int32(0), jnp.int32(0)
-    for s in range(3):
-        end = jnp.sum(jnp.where(valid & (seg <= s), 1.0, 0.0)).astype(jnp.int32)
-        hit = (end > first) & (start < last) & (end > start)
-        low = jnp.where(hit, jnp.minimum(low, start), low)
-        high = jnp.where(hit, jnp.maximum(high, end), high)
-        start = end
-    begin = low // 128
-    blocks = jnp.where(high > low, (high - begin * 128 + BK - 1) // BK, 0)
-    begin = jnp.minimum(begin, slots // 128 - blocks * (BK // 128))
-    return begin, blocks
-
-
-def fwd_kernel(slots, seg_ref, cnt_ref, qa_ref, ka_ref, va_ref, km_ref, vm_ref, mix_ref, lse_ref, acc_ref, m_ref):
-    begin, blocks = key_range(seg_ref[...], cnt_ref[0], pl.program_id(0) * BQ, slots)
+    ends = [jnp.sum(jnp.where(valid & (seg <= s), 1.0, 0.0)).astype(jnp.int32) for s in range(3)]
+    for block in range(slots // BQ):
+        first = block * BQ
+        last = jnp.minimum(first + BQ, count)
+        low, high, start = jnp.int32(slots), jnp.int32(0), jnp.int32(0)
+        for end in ends:
+            hit = (end > first) & (start < last) & (end > start)
+            low = jnp.where(hit, jnp.minimum(low, start), low)
+            high = jnp.where(hit, jnp.maximum(high, end), high)
+            start = end
+        begin = low // 128
+        blocks = jnp.where(high > low, (high - begin * 128 + BK - 1) // BK, 0)
+        out[0, block] = jnp.minimum(begin, slots // 128 - blocks * (BK // 128))
+        out[1, block] = blocks
+
+
+def key_slots(begin, block):
+    return pl.ds(pl.multiple_of((begin + block * (BK // 128)) * 128, 128), BK)
+
+
+def pipelined(blocks, work, first, second):
+    @pl.when(blocks > 0)
+    def _():
+        work((0, first), None)
+
+    pairs = jnp.maximum(blocks - 1, 0) // 2
+
+    @pl.loop(0, pairs)
+    def _(i):
+        work((2 * i + 1, second), (2 * i, first))
+        work((2 * i + 2, first), (2 * i + 1, second))
+
+    j = 2 * pairs
+
+    @pl.when(blocks - j == 2)
+    def _():
+        work((j + 1, second), (j, first))
+        work(None, (j + 1, second))
+
+    @pl.when(blocks - j == 1)
+    def _():
+        work(None, (j, first))
+
+
+def fwd_kernel(
+    slots, seg_ref, cnt_ref, qa_ref, kn_ref, va_ref, kmn_ref, vm_ref,
+    mix_ref, lse_ref, acc_ref, m_ref, sa_ref, sb_ref, range_ref,
+):
+    step = pl.program_id(0)
+
+    @pl.when(step == 0)
+    def _():
+        key_ranges(seg_ref[...], cnt_ref[0], slots, range_ref)
+
+    begin, blocks = range_ref[0, step], range_ref[1, step]
+
+    def weights(h, s):
+        old = m_ref[h : h + 1, :]
+        top = jnp.maximum(old, jnp.max(s, axis=0, keepdims=True))
+        return jnp.exp(s - top).astype(BF16), jnp.exp(old - top), top
+
+    def work(new, old):
+        kept = {}
+        for h in range(H + 1):
+            if h < H and new:
+                new[1][h] = dot(kn_ref[h, key_slots(begin, new[0]), 0:HA], qa_ref[h], 1, 0)
+            if h < H and old:
+                kept[h] = weights(h, old[1][h])
+            if h > 0 and old:
+                p, fade, top = kept.pop(h - 1)
+                acc_ref[h - 1] = acc_ref[h - 1] * fade + dot(va_ref[h - 1, :, key_slots(begin, old[0])], p, 1, 0)
+                m_ref[h - 1 : h, :] = top
+
+    scores = [dot(kmn_ref[h, :, 0:HA], qa_ref[h], 1, 0) for h in range(H)]
     for h in range(H):
-        s = dot(km_ref[h, :, 0:MP], qa_ref[h], 0, 0)
-        top = jnp.max(s, axis=0, keepdims=True)
-        p = jnp.exp(s - top).astype(BF16)
+        top = jnp.max(scores[h], axis=0, keepdims=True)
+        p = jnp.exp(scores[h] - top).astype(BF16)
         acc_ref[h] = dot(vm_ref[h, :, 0:MP], p, 1, 0)
         m_ref[h : h + 1, :] = top
-
-    @pl.loop(0, blocks)
-    def _(j):
-        ks = pl.ds(pl.multiple_of((begin + j * (BK // 128)) * 128, 128), BK)
-        for h in range(H):
-            s = dot(ka_ref[h, :, ks], qa_ref[h], 0, 0)
-            old = m_ref[h : h + 1, :]
-            top = jnp.maximum(old, jnp.max(s, axis=0, keepdims=True))
-            p = jnp.exp(s - top).astype(BF16)
-            acc_ref[h] = acc_ref[h] * jnp.exp(old - top) + dot(va_ref[h, :, ks], p, 1, 0)
-            m_ref[h : h + 1, :] = top
-
+    pipelined(blocks, work, sa_ref, sb_ref)
     for h in range(H):
         total = acc_ref[h, 64:65, :]
-        mix_ref[64 * h : 64 * h + 64, :] = (acc_ref[h, 0:64, :] / total).astype(BF16)
+        mix_ref[64 * h : 64 * h + 64, :] = (acc_ref[h, 0:64, :] * (1.0 / total)).astype(BF16)
         lse_ref[h : h + 1, :] = m_ref[h : h + 1, :] + jnp.log(total)
 
 
-def attend_forward(seg2, counts, qa, ka, va, km, vm):
+def attend_forward(seg2, counts, qa, kn, va, kmn, vm):
     slots = qa.shape[2]
-    full = pl.BlockSpec((H, HA, slots), lambda i: (0, 0, 0))
-    mfull = pl.BlockSpec((H, HA, 128), lambda i: (0, 0, 0))
+    once = pl.Buffered(1)
+
+    def whole(a):
+        return pl.BlockSpec(a.shape, lambda i: (0, 0, 0), pipeline_mode=once)
+
     return pl.pallas_call(
         functools.partial(fwd_kernel, slots),
         grid=(slots // BQ,),
@@ -154,14 +214,20 @@
             pl.BlockSpec(seg2.shape, lambda i: (0, 0)),
             pl.BlockSpec(memory_space=pltpu.SMEM),
             pl.BlockSpec((H, HA, BQ), lambda i: (0, 0, i)),
-            full, full, mfull, mfull,
+            whole(kn), whole(va), whole(kmn), whole(vm),
         ],
         out_specs=[pl.BlockSpec((512, BQ), lambda i: (0, i)), pl.BlockSpec((H, BQ), lambda i: (0, i))],
         out_shape=[jax.ShapeDtypeStruct((512, slots), BF16), jax.ShapeDtypeStruct((H, slots), F32)],
-        scratch_shapes=[pltpu.VMEM((H, HA, BQ), F32), pltpu.VMEM((H, BQ), F32)],
+        scratch_shapes=[
+            pltpu.VMEM((H, HA, BQ), F32),
+            pltpu.VMEM((H, BQ), F32),
+            pltpu.VMEM((H, BK, BQ), F32),
+            pltpu.VMEM((H, BK, BQ), F32),
+            pltpu.SMEM((2, slots // BQ), jnp.int32),
+        ],
         compiler_params=params(),
         name="attend_forward",
-    )(seg2, counts, qa, ka, va, km, vm)
+    )(seg2, counts, qa, kn, va, kmn, vm)
 
 
 def norm_parts(value):
@@ -313,19 +379,21 @@
 
 
 def bwd_kernel(
-    slots, seg_ref, cnt_ref, qa_ref, ka_ref, va_ref, km_ref, vm_ref, do_ref, lse_ref, delta_ref,
-    dq_ref, dk_ref, dv_ref, dkm_ref, dvm_ref, q2_ref, do2_ref, dqa_ref, dka_ref, dva_ref, dkma_ref, dvma_ref,
+    slots, seg_ref, cnt_ref, qa_ref, kn_ref, ka_ref, vn_ref, kmn_ref, km_ref, vmn_ref, do_ref, lse_ref, delta_ref,
+    dq_ref, dk_ref, dv_ref, dkm_ref, dvm_ref,
+    q2_ref, do2_ref, dqa_ref, dka_ref, dva_ref, dkma_ref, dvma_ref, sa_ref, ga_ref, sb_ref, gb_ref, range_ref,
 ):
     step = pl.program_id(0)
-    begin, blocks = key_range(seg_ref[...], cnt_ref[0], step * BQ, slots)
 
     @pl.when(step == 0)
     def _():
+        key_ranges(seg_ref[...], cnt_ref[0], slots, range_ref)
         dka_ref[...] = jnp.zeros_like(dka_ref)
         dva_ref[...] = jnp.zeros_like(dva_ref)
         dkma_ref[...] = jnp.zeros_like(dkma_ref)
         dvma_ref[...] = jnp.zeros_like(dvma_ref)
 
+    begin, blocks = range_ref[0, step], range_ref[1, step]
     frow = lax.broadcasted_iota(jnp.int32, (16, BQ), 0)
 
     def feature(value, at):
@@ -338,23 +406,30 @@
         do2_ref[h, 0:64, :] = do_ref[64 * h : 64 * h + 64, :]
         do2_ref[h, 64:80, :] = feature(-delta_ref[h : h + 1, :], 0).astype(BF16)
 
+    def work(new, old):
+        kept = {}
+        for h in range(H + 1):
+            if h < H and new:
+                ks = key_slots(begin, new[0])
+                new[1][0][h] = dot(kn_ref[h, ks, 0:HA], q2_ref[h], 1, 0)
+                new[1][1][h] = dot(vn_ref[h, ks, 0:HA], do2_ref[h], 1, 0)
+            if h < H and old:
+                p = jnp.exp(old[1][0][h])
+                kept[h] = p.astype(BF16), (p * old[1][1][h]).astype(BF16)
+            if h > 0 and old:
+                ks = key_slots(begin, old[0])
+                p, ds = kept.pop(h - 1)
+                dva_ref[h - 1, :, ks] += dot(do2_ref[h - 1, 0:64, :], p, 1, 1)
+                dka_ref[h - 1, :, ks] += dot(q2_ref[h - 1, 0:64, :], ds, 1, 1)
+                dqa_ref[h - 1] += dot(ka_ref[h - 1, 0:64, ks], ds, 1, 0)
+
+    ps = [jnp.exp(dot(kmn_ref[h, :, 0:HA], q2_ref[h], 1, 0)) for h in range(H)]
+    dss = [(ps[h] * dot(vmn_ref[h, :, 0:HA], do2_ref[h], 1, 0)).astype(BF16) for h in range(H)]
     for h in range(H):
-        p = jnp.exp(dot(km_ref[h, :, 0:MP], q2_ref[h], 0, 0))
-        ds = (p * dot(vm_ref[h, :, 0:MP], do2_ref[h], 0, 0)).astype(BF16)
-        dvma_ref[h, :, 0:MP] += dot(do2_ref[h, 0:64, :], p.astype(BF16), 1, 1)
-        dkma_ref[h, :, 0:MP] += dot(q2_ref[h, 0:64, :], ds, 1, 1)
-        dqa_ref[h] = dot(km_ref[h, 0:64, 0:MP], ds, 1, 0)
-
-    @pl.loop(0, blocks)
-    def _(j):
-        ks = pl.ds(pl.multiple_of((begin + j * (BK // 128)) * 128, 128), BK)
-        for h in range(H):
-            p = jnp.exp(dot(ka_ref[h, :, ks], q2_ref[h], 0, 0))
-            ds = (p * dot(va_ref[h, :, ks], do2_ref[h], 0, 0)).astype(BF16)
-            dva_ref[h, :, ks] += dot(do2_ref[h, 0:64, :], p.astype(BF16), 1, 1)
-            dka_ref[h, :, ks] += dot(q2_ref[h, 0:64, :], ds, 1, 1)
-            dqa_ref[h] += dot(ka_ref[h, 0:64, ks], ds, 1, 0)
-
+        dvma_ref[h, :, 0:MP] += dot(do2_ref[h, 0:64, :], ps[h].astype(BF16), 1, 1)
+        dkma_ref[h, :, 0:MP] += dot(q2_ref[h, 0:64, :], dss[h], 1, 1)
+        dqa_ref[h] = dot(km_ref[h, 0:64, 0:MP], dss[h], 1, 0)
+    pipelined(blocks, work, (sa_ref, ga_ref), (sb_ref, gb_ref))
     for h in range(H):
         dq_ref[64 * h : 64 * h + 64, :] = (dqa_ref[h] * HD ** -0.5).astype(BF16)
 
@@ -368,15 +443,18 @@
             dvm_ref[s, :] = dvma_ref[h].astype(BF16)
 
 
-def attend_backward(seg2, counts, qa, ka, va, km, vm, mgrad, lse, delta):
+def attend_backward(seg2, counts, qa, kn, ka, vn, kmn, km, vmn, mgrad, lse, delta):
     slots = qa.shape[2]
     once = pl.Buffered(1)
-    full = pl.BlockSpec((H, HA, slots), lambda i: (0, 0, 0), pipeline_mode=once)
-    mfull = pl.BlockSpec((H, HA, 128), lambda i: (0, 0, 0))
+
+    def full(a):
+        return pl.BlockSpec(a.shape, lambda i: (0, 0, 0), pipeline_mode=once)
+
     cols = pl.BlockSpec((512, BQ), lambda i: (0, i))
     stat = pl.BlockSpec((H, BQ), lambda i: (0, i))
     whole = pl.BlockSpec((512, slots), lambda i: (0, 0), pipeline_mode=once)
     mwhole = pl.BlockSpec((512, 128), lambda i: (0, 0))
+    block = pltpu.VMEM((H, BK, BQ), F32)
     return pl.pallas_call(
         functools.partial(bwd_kernel, slots),
         grid=(slots // BQ,),
@@ -384,7 +462,7 @@
             pl.BlockSpec(seg2.shape, lambda i: (0, 0)),
             pl.BlockSpec(memory_space=pltpu.SMEM),
             pl.BlockSpec((H, HA, BQ), lambda i: (0, 0, i)),
-            full, full, mfull, mfull, cols, stat, stat,
+            full(kn), full(ka), full(vn), full(kmn), full(km), full(vmn), cols, stat, stat,
         ],
         out_specs=[cols, whole, whole, mwhole, mwhole],
         out_shape=[jax.ShapeDtypeStruct((512, slots), BF16)] * 3 + [jax.ShapeDtypeStruct((512, 128), BF16)] * 2,
@@ -396,10 +474,12 @@
             pltpu.VMEM((H, HD, slots), F32),
             pltpu.VMEM((H, HD, 128), F32),
             pltpu.VMEM((H, HD, 128), F32),
+            block, block, block, block,
+            pltpu.SMEM((2, slots // BQ), jnp.int32),
         ],
         compiler_params=params(),
         name="attend_backward",
-    )(seg2, counts, qa, ka, va, km, vm, mgrad, lse, delta)
+    )(seg2, counts, qa, kn, ka, vn, kmn, km, vmn, mgrad, lse, delta)
 
 
 def tail_kernel(
@@ -802,10 +882,10 @@
             {k: lax.all_gather(v, "dp", axis=1 if k == "memory" else 0, tiled=True) for k, v in p.items()}
         )
     seg2 = segment.reshape(slots // 128, 128)
-    qa, ka, va, km, vm = qkv(g, tokens, segment, counts, mem_rows)
-    mixt, lse = attend_forward(seg2, counts, qa, ka, va, km, vm)
+    qa, ka, va, kn, vn, km, vm, kmn, vmn = qkv(g, tokens, segment, counts, mem_rows)
+    mixt, lse = attend_forward(seg2, counts, qa, kn, va, kmn, vm)
     output, gfirst, mgrad, delta, early, vec, bup = middle(g, counts, mixt, tokens, cotangent)
-    dq, dk, dv, dkm, dvm = attend_backward(seg2, counts, qa, ka, va, km, vm, mgrad, lse, delta)
+    dq, dk, dv, dkm, dvm = attend_backward(seg2, counts, qa, kn, ka, vn, kmn, km, vmn, mgrad, lse, delta)
     gtok, late = tail(g, tokens, dq, dk, dv, dkm, dvm, gfirst, vec, bup)
     if n == PARTS:
         owned = scatter(late, early)

time: 397 us -> 285 us (0.72)
  Pallas kernels: 373 us -> 261 us
    pallas_call x1, Pallas kernels: 92.5 us -> 33.2 us  [attend_forward(): pl.pallas_call(functools.partial(fwd_kernel, slots), grid=(slots // BQ,),...]
    pallas_call x1, Pallas kernels: 95.8 us -> 59.6 us  [attend_backward(): pl.pallas_call(functools.partial(bwd_kernel, slots), grid=(slots // BQ,),...]
    pallas_call x1, Pallas kernels: 61.9 us -> 44.3 us  [scatter(): pl.pallas_call(functools.partial(scatter_kernel, SCATTER_PARTS), in_specs...]
where the time goes in v3:
time: 285 us; the launch traced here: 284 us
  Pallas kernels  261 us (92%)
  local copies, waits for them, and re-layouts  20.2 us (7%)
    pallas_call x1, Pallas kernels, attend_backward(): pl.pallas_call(functools.partial(bwd_kernel, slots), grid=(slots // BQ,),...  59.6 us
    pallas_call x1, Pallas kernels, middle(): pl.pallas_call(functools.partial(mid_kernel, rb), grid=(slots // rb,), in...  51.5 us
    pallas_call x1, Pallas kernels, gather(): pl.pallas_call(functools.partial(gather_kernel, GATHER_PARTS), in_specs=[...  48.5 us
    pallas_call x1, Pallas kernels, scatter(): pl.pallas_call(functools.partial(scatter_kernel, SCATTER_PARTS), in_specs...  44.3 us
    pallas_call x1, Pallas kernels, attend_forward(): pl.pallas_call(functools.partial(fwd_kernel, slots), grid=(slots // BQ,),...  33.2 us
    pallas_call x1, Pallas kernels, tail(): pl.pallas_call(tail_kernel, grid=(slots // rb,), in_specs=[pl.BlockSpec((...  13.8 us
    pallas_call x1, Pallas kernels, qkv(): pl.pallas_call(functools.partial(qkv_kernel, mem_rows), grid=(slots // rb...  10.6 us
    another operation x9, local copies, waits for them, and re-layouts, pack_part(): vectors = pad_lanes(jnp.stack([p[name] for name in VECTORS], axis=1), 128)  6.05 us

profile of v3, /device:TPU:0, one launch (start us, length us, event | category | flops | bytes accessed | tf_op | source)
XLA Modules:
  0.0 283.8 jit_solution(12512807126664813194)
XLA Ops:
  2.1 0.7 copy.48
  2.8 0.7 copy.49
  3.6 0.7 copy.50
  4.3 0.7 copy.51
  5.0 0.7 copy.52
  5.8 0.7 copy.53
  6.5 0.7 copy.54
  7.3 0.7 copy.55
  8.1 0.8 copy.62
  9.0 0.7 constant_dynamic-update-slice_fusion.5
  9.7 0.7 constant_dynamic-update-slice_fusion.4
  10.4 0.7 constant_dynamic-update-slice_fusion.3
  11.8 0.8 constant_dynamic-update-slice_fusion.1
  14.1 48.5 %gather.1 = bf16[4,2,2,2,208,512]{5,4,3,2,1,0:T(8,128)(2,1)} custom-call(bf16[208,512]{1,0:T(8,128)(2,1)} %copy-done), custom_call_target="tpu_custom_call" | custom-call | tf_op jit(solution)/shard_map/gather/pallas_call | solution.py:693
  62.6 10.6 %qkv.1 = (bf16[8,80,2048]{2,1,0:T(8,128)(2,1)}, bf16[8,80,2048]{2,1,0:T(8,128)(2,1)}, bf16[8,80,2048]{2,1,0:T(8,128)(2,1)}, bf16[8,2048,128]{2,1,0:T(8,128)(2,1)...) custom-call(bf16[32,208,512]{2,1,0:T(8,128)(2,1)} %bitcast.31, ...), custom_call_target="tpu_custom_call" | custom-call | tf_op jit(solution)/shard_map/qkv/pallas_call | solution.py:96
  73.2 33.2 %attend_forward.1 = (bf16[512,2048]{1,0:T(8,128)(2,1)}, f32[8,2048]{1,0:T(8,128)}) custom-call(s32[16,128]{1,0:T(8,128)} %bitcast.43, s32[1]{0:T(128)S(6)} %copy.69.cnt_ref, bf16[8,80,2048]{2,1,0:T(8,128)(2,1)} %get-tuple-element.43.qa_ref, bf16[8,2048,128]{2,1,0:T(8,128)(2,1)} %get-tuple-element.44.kn_ref, bf16[8,80,2048]{2,1,0:T(8,128)(2,1)} %get-tuple-element.45.va_ref, ...), custom_call_target="tpu_custom_call" | custom-call | tf_op jit(solution)/shard_map/attend_forward/pallas_call | solution.py:210
  106.4 51.5 %middle.1 = (bf16[2048,512]{1,0:T(8,128)(2,1)}, f32[2048,512]{1,0:T(8,128)}, bf16[512,2048]{1,0:T(8,128)(2,1)}, f32[8,2048]{1,0:T(8,128)}, bf16[32,144,512]{2,1,...) custom-call(s32[1]{0:T(128)S(6)} %copy.69.cnt_ref, bf16[32,208,512]{2,1,0:T(8,128)(2,1)} %bitcast.32, ...), custom_call_target="tpu_custom_call" | custom-call | tf_op jit(solution)/shard_map/middle/pallas_call | solution.py:333
  157.9 59.6 %attend_backward.1 = (bf16[512,2048]{1,0:T(8,128)(2,1)}, bf16[512,2048]{1,0:T(8,128)(2,1)}, bf16[512,2048]{1,0:T(8,128)(2,1)}, bf16[512,128]{1,0:T(8,128)(2,1)}, bf16[512,128]{1,0:T(8,128)(2,1)}) custom-call(s32[16,128]{1,0:T(8,128)} %bitcast.44, s32[1]{0:T(128)S(6)} %copy.69.cnt_ref, bf16[8,80,2048]{2,1,0:T(8,128)(2,1)} %get-tuple-element.43.qa_ref, ...), custom_call_target="tpu_custom_call" | custom-call | tf_op jit(solution)/shard_map/attend_backward/pallas_call | solution.py:458
  217.6 13.8 %tail.1 = (f32[2048,512]{1,0:T(8,128)}, bf16[32,64,512]{2,1,0:T(8,128)(2,1)}) custom-call(bf16[32,208,512]{2,1,0:T(8,128)(2,1)} %bitcast.36, bf16[2048,512]{1,0:T(8,128)(2,1)} %tok_ref.5, bf16[512,2048]{1,0:T(8,128)(2,1)} %get-tuple-element.57.dq_ref, bf16[512,2048]{1,0:T(8,128)(2,1)} %get-tuple-element.58.dk_ref, ...), custom_call_target="tpu_custom_call" | custom-call | tf_op jit(solution)/shard_map/tail/pallas_call | solution.py:538
  231.3 44.3 %scatter.1 = f32[208,512]{1,0:T(8,128)} custom-call(bf16[4,2,2,2,64,512]{5,4,3,2,1,0:T(8,128)(2,1)} %bitcast.38, bf16[4,2,2,2,144,512]{5,4,3,2,1,0:T(8,128)(2,1)} %bitcast.37), custom_call_target="tpu_custom_call" | custom-call | tf_op jit(solution)/shard_map/scatter/pallas_call | solution.py:801
  275.6 1.8 slice_reduce_fusion
  278.7 1.3 slice_bitcast_fusion.1
  280.0 1.5 fusion.13
  281.4 1.6 fusion.12
  (13 shorter events, 4.9 us)
Async XLA Ops:
  13.4 0.7 copy-start

commit v4 on v1

v4 whole, which is shorter than its diff:
```python
import functools
import jax
import jax.numpy as jnp
from jax import lax
from jax.experimental import pallas as pl
from jax.experimental.pallas import tpu as pltpu
from jax.sharding import PartitionSpec as P

H = 8
HD = 64
HA = 80
EPS = 1e-05
BIG = 1e30
PARTS = 32
ROWS = 208
BQ = 256
BK = 256
MP = 32
F32 = jnp.float32
BF16 = jnp.bfloat16
VMEM_LIMIT = 60 << 20

V_BQ, V_BV, V_BO, V_GA, V_SA, V_BD, V_GF, V_SF = range(8)


def dot(left, right, lc, rc):
    return lax.dot_general(left, right, (((lc,), (rc,)), ((), ())), preferred_element_type=F32)


def params(**kw):
    return pltpu.CompilerParams(vmem_limit_bytes=VMEM_LIMIT, **kw)


MESH = pl.DeviceIdType.MESH
AXES = {"z": (8, 4), "y": (4, 2), "x": (2, 2)}
LAYOUT = ("z", "y", "x")


class Place:
    def __init__(self):
        me = lax.axis_index("dp")
        self.me = me
        self.core = me % 2
        self.far = 1 - self.core
        self.partner = me + 1 - 2 * self.core
        self.at = {a: (me // stride) % length for a, (stride, length) in AXES.items()}
        self.mine = tuple(self.at[a] for a in LAYOUT)
        self.others = {}
        for axis, (stride, length) in AXES.items():
            for distance in range(1, length):
                j = (self.at[axis] + distance) % length
                self.others[axis, distance] = j, me + (j - self.at[axis]) * stride

    def other(self, axis, distance):
        return self.others[axis, distance]

    def greet(self):
        barrier = pltpu.get_barrier_semaphore()
        peers = [self.partner]
        for axis in LAYOUT:
            peers += [self.other(axis, d)[1] for d in range(1, AXES[axis][1])]
        for peer in peers:
            pl.semaphore_signal(barrier, inc=1, device_id=(peer,), device_id_type=MESH)
        return lambda: pl.semaphore_wait(barrier, len(peers))


class Copies:
    def __init__(self, send, recv):
        self.send, self.recv, self.count, self.open = send, recv, 0, []

    def number(self):
        self.count += 1
        return self.count - 1

    def make(self, src, dst, number, device):
        return pltpu.make_async_remote_copy(
            src_ref=src, dst_ref=dst, send_sem=self.send.at[number], recv_sem=self.recv.at[number],
            device_id=(device,), device_id_type=MESH,
        )

    def start(self, src, dst, number, device):
        self.make(src(), dst(), number, device).start()
        self.open.append((src, dst, number, device))

    def landed(self, block, number, device):
        self.make(block, block, number, device).wait_recv()

    def finish(self):
        for src, dst, number, device in self.open:
            self.make(src(), dst(), number, device).wait_send()
        self.open = []


def gather_part(place, copies, own, base, whole, rows, order, arrivals):
    done = ()

    def mine():
        return own.at[slice(base + rows.start, base + rows.stop)]

    def block(axis, j, core):
        index = tuple(j if a == axis else (slice(None) if a in done else place.at[a]) for a in LAYOUT)
        return lambda: whole.at[index + (core, rows)]

    for axis in order:
        length = AXES[axis][1]
        numbers = [copies.number() for _ in range(2 * length - 2)]
        here = block(axis, place.at[axis], place.core)
        for d in range(1, length):
            copies.start(here if done else mine, here, numbers[d - 1], place.other(axis, d)[1])
        if not done:
            number = copies.number()
            copies.start(mine, here, number, place.partner)
            arrivals.append((block(axis, place.at[axis], place.far), number))
        yield
        for d in range(1, length):
            j, device = place.other(axis, length - d)
            there = block(axis, j, place.core)
            copies.landed(there(), numbers[d - 1], device)
            number = numbers[length - 2 + d]
            copies.start(there, there, number, place.partner)
            arrivals.append((block(axis, j, place.far), number))
        done += (axis,)
    yield


def advance(parts):
    for part in parts:
        next(part)


def scatter_part(place, copies, acc, slots, out, rows, order):
    done = ()

    def block(axis, j):
        index = tuple(j if a == axis else (place.at[a] if a in done else slice(None)) for a in LAYOUT)
        return index + (rows,)

    def taken(index):
        return lambda: acc.at[index]

    def landing(axis, d):
        return lambda: slots[axis, d]

    for axis in order:
        length = AXES[axis][1]
        numbers = [copies.number() for _ in range(length - 1)]
        for d in range(1, length):
            j, device = place.other(axis, d)
            copies.start(taken(block(axis, j)), landing(axis, d), numbers[d - 1], device)
        yield
        for d in range(1, length):
            copies.landed(slots[axis, d], numbers[d - 1], place.partner)
        mine = block(axis, place.at[axis])
        total = acc[mine].astype(F32)
        for d in range(1, length):
            total = total + slots[axis, d][...].astype(F32)
        if axis == order[-1]:
            out[rows, :] = total
        else:
            acc[mine] = total.astype(BF16)
        done += (axis,)
    yield


def slot_shapes(parts):
    shapes = {}
    for number, (rows, order) in enumerate(parts):
        left = ["z", "y", "x"]
        for axis in order:
            left.remove(axis)
            shape = tuple(AXES[a][1] for a in LAYOUT if a in left) + (rows.stop - rows.start, 512)
            for d in range(1, AXES[axis][1]):
                shapes[number, axis, d] = shape
    return shapes


def join(place, copies, acc, source, other, rows, number):
    copies.landed(other.at[:, :, :, rows], number, place.partner)

    @pl.loop(0, 4)
    def _(z):
        mine = source(z) if source else acc[z, :, :, rows]
        acc[z, :, :, rows] = (mine.astype(F32) + other[z, :, :, rows].astype(F32)).astype(BF16)


VECTORS = ("b_query", "b_value", "b_out", "gain_attn", "shift_attn", "b_down", "gain_ffn", "shift_ffn")
EARLY = 64
LATE = 144
EARLY_PARTS = ((slice(0, 32), "zxy"), (slice(32, 64), "zyx"))
LATE_PARTS = (
    (slice(0, 48), "zxy"),
    (slice(48, 96), "zyx"),
    (slice(96, 128), "yzx"),
    (slice(128, 144), "xzy"),
)
GATHER_COPIES = 11 * (len(EARLY_PARTS) + len(LATE_PARTS))


def head_block(rows, features):
    block = jnp.concatenate([rows, features], axis=0)
    return block, jnp.concatenate([block, jnp.zeros((128 - HA, rows.shape[1]), BF16)], axis=0).T


def pack(own, place, wq, wk, wv, wo, up, dn, memory, vectors, b_up):
    own[0:16] = wq[...]
    own[16:32] = wk[...]
    own[32:48] = wv[...]
    mem_rows = memory.shape[0]
    own[48:64] = jnp.zeros((16, 512), BF16)
    own[48:64, 0:mem_rows] = memory[...].astype(F32).T.astype(BF16)
    own[48:64, 128:136] = vectors[...].astype(F32).T.astype(BF16)
    value = jnp.concatenate([b_up[...].astype(F32)] * 4, axis=1)
    row = lax.broadcasted_iota(jnp.int32, (16, 256), 0)
    lane = lax.broadcasted_iota(jnp.int32, (16, 256), 1)
    own[48:64, 256:512] = jnp.where(row * 4 + lane // 64 == place.me, value, 0.0).astype(BF16)
    for c in range(4):
        own[64 + 16 * c : 80 + 16 * c] = up[:, 512 * c : 512 * c + 512]
    own[128:192] = dn[...]
    own[192:208] = wo[...]


def prepare(mem_rows, early, wt_ref, memt_ref, rows_ref, rbup_ref, bias_ref, km_ref, vm_ref, kmn_ref, vmn_ref):
    for j in range(3):
        wt_ref[512 * j : 512 * j + 512, :] = early[..., 16 * j : 16 * j + 16, :].reshape(512, 512).T
    small = early[..., 48:64, 0:256].reshape(512, 256)
    memt = small[:, 0:128]
    memt_ref[...] = memt
    vectors = small[:, 128:256].astype(F32)
    bias_ref[...] = vectors
    rows_ref[...] = vectors.T[0:8, :]
    bup = jnp.sum(early[..., 48:64, 256:512].reshape(PARTS, 16, 256).astype(F32), axis=0)
    for v in range(8):
        rbup_ref[0:1, 256 * v : 256 * v + 256] = bup[v : v + 1, :]
    bv = vectors[:, V_BV : V_BV + 1]
    km = dot(wt_ref[512:1024, :], memt, 1, 0).astype(BF16)
    vm = (dot(wt_ref[1024:1536, :], memt, 1, 0) + bv).astype(BF16)
    frow = lax.broadcasted_iota(jnp.int32, (16, 128), 0)
    lane = lax.broadcasted_iota(jnp.int32, (16, 128), 1)
    kf = jnp.where(frow < 3, jnp.where(lane < mem_rows, 0.0, 1.0), jnp.where(frow < 6, 1.0, 0.0)).astype(BF16)
    vf = jnp.where(frow < 3, 1.0, 0.0).astype(BF16)
    for h in range(H):
        km_ref[h], turned = head_block(km[64 * h : 64 * h + 64, :], kf)
        kmn_ref[h] = turned[0:MP]
        vm_ref[h], turned = head_block(vm[64 * h : 64 * h + 64, :], vf)
        vmn_ref[h] = turned[0:MP]


def project(step, tok_ref, seg_ref, cnt_ref, wt_ref, bias_ref, qa_ref, ka_ref, va_ref, kn_ref, vn_ref):
    rows = tok_ref.shape[0]
    tok = tok_ref[...]
    bq = bias_ref[:, V_BQ : V_BQ + 1]
    bv = bias_ref[:, V_BV : V_BV + 1]
    q = (dot(wt_ref[0:512, :], tok, 1, 1) + bq).astype(BF16) * jnp.asarray(HD ** -0.5, BF16)
    k = dot(wt_ref[512:1024, :], tok, 1, 1).astype(BF16)
    v = (dot(wt_ref[1024:1536, :], tok, 1, 1) + bv).astype(BF16)
    frow = lax.broadcasted_iota(jnp.int32, (16, rows), 0)
    seg = jnp.broadcast_to(seg_ref[...], (16, rows))
    pos = lax.broadcasted_iota(jnp.int32, (16, rows), 1) + step * rows
    valid = pos < cnt_ref[0]
    qf = jnp.where((frow < 3) & (frow != seg), -BIG, 0.0).astype(BF16)
    kf = jnp.where(frow < 3, jnp.where(valid & (frow != seg), 0.0, 1.0), jnp.where(frow < 6, 1.0, 0.0)).astype(BF16)
    vf = jnp.where(frow < 3, 1.0, 0.0).astype(BF16)
    for h in range(H):
        s = slice(64 * h, 64 * h + 64)
        qa_ref[h, 0:64, :] = q[s]
        qa_ref[h, 64:80, :] = qf
        ka_ref[h], kn_ref[h] = head_block(k[s], kf)
        va_ref[h], vn_ref[h] = head_block(v[s], vf)


def gather_kernel(
    mem_rows, wq, wk, wv, wo, up, dn, memory, vectors, b_up, tok_ref, seg_ref, cnt_ref,
    late_ref, qa_ref, ka_ref, va_ref, kn_ref, vn_ref, km_ref, vm_ref, kmn_ref, vmn_ref,
    wt_ref, memt_ref, rows_ref, rbup_ref, own, early, bias_ref, send, recv, local,
):
    step = pl.program_id(0)
    place = Place()
    copies = Copies(send, recv)
    arrivals, late_arrivals = [], []
    firsts = [gather_part(place, copies, own, 0, early, *part, arrivals) for part in EARLY_PARTS]
    lasts = [gather_part(place, copies, own, EARLY, late_ref, *part, late_arrivals) for part in LATE_PARTS]

    @pl.when(step == 0)
    def _():
        everyone = place.greet()
        pack(own, place, wq, wk, wv, wo, up, dn, memory, vectors, b_up)
        early[place.mine + (place.core,)] = own[0:EARLY]
        everyone()
        advance(firsts)
        keep = pltpu.make_async_copy(own.at[EARLY:ROWS], late_ref.at[place.mine + (place.core,)], local)
        keep.start()
        advance(lasts)
        advance(firsts)
        advance(firsts)
        advance(firsts)
        for block, number in arrivals:
            copies.landed(block(), number, place.partner)
        keep.wait()
        advance(lasts)
        prepare(
            mem_rows, early, wt_ref, memt_ref, rows_ref, rbup_ref, bias_ref,
            km_ref, vm_ref, kmn_ref, vmn_ref,
        )

    project(step, tok_ref, seg_ref, cnt_ref, wt_ref, bias_ref, qa_ref, ka_ref, va_ref, kn_ref, vn_ref)

    @pl.when(step == 1)
    def _():
        advance(lasts)

    @pl.when(step == pl.num_programs(0) - 1)
    def _():
        advance(lasts)
        for block, number in late_arrivals:
            copies.landed(block(), number, place.partner)
        copies.finish()


def project_kernel(
    mem_rows, g_ref, tok_ref, seg_ref, cnt_ref, qa_ref, ka_ref, va_ref, kn_ref, vn_ref, km_ref, vm_ref, kmn_ref, vmn_ref,
    wt_ref, memt_ref, rows_ref, rbup_ref, bias_ref,
):
    step = pl.program_id(0)

    @pl.when(step == 0)
    def _():
        prepare(
            mem_rows, g_ref, wt_ref, memt_ref, rows_ref, rbup_ref, bias_ref, km_ref, vm_ref, kmn_ref, vmn_ref
        )

    project(step, tok_ref, seg_ref, cnt_ref, wt_ref, bias_ref, qa_ref, ka_ref, va_ref, kn_ref, vn_ref)


def projections(p, whole, tokens, segment, counts, mem_rows):
    slots = tokens.shape[0]
    rb = 512

    def fixed(*shape):
        return pl.BlockSpec(shape, lambda i: (0,) * len(shape))

    wide, tall = (H, HA, slots), (H, slots, 128)
    shapes = [wide, wide, wide, tall, tall] + [(H, HA, 128)] * 2 + [(H, MP, 128)] * 2 + [(1536, 512), (512, 128)]
    outs = [jax.ShapeDtypeStruct(s, BF16) for s in shapes]
    outs += [jax.ShapeDtypeStruct((8, 512), F32), jax.ShapeDtypeStruct((1, 2048), F32)]
    blk = pl.BlockSpec((H, HA, rb), lambda i: (0, 0, i))
    tblk = pl.BlockSpec((H, rb, 128), lambda i: (0, i, 0))
    specs = [blk, blk, blk, tblk, tblk] + [fixed(*o.shape) for o in outs[5:]]
    common = [
        pl.BlockSpec((rb, 512), lambda i: (i, 0)),
        pl.BlockSpec((1, rb), lambda i: (0, i)),
        pl.BlockSpec(memory_space=pltpu.SMEM),
    ]
    args = (tokens, segment.reshape(1, slots), counts)
    if whole is not None:
        found = pl.pallas_call(
            functools.partial(project_kernel, mem_rows),
            grid=(slots // rb,),
            in_specs=[fixed(PARTS, EARLY, 512)] + common,
            out_specs=specs,
            out_shape=outs,
            scratch_shapes=[pltpu.VMEM((512, 128), F32)],
            compiler_params=params(),
            name="projections",
        )(whole[:, 0:EARLY], *args)
        return (whole[:, EARLY:],) + tuple(found)
    weights = [p[name] for name in ("w_query", "w_key", "w_value", "w_out", "w_up", "w_down", "memory")]
    weights += [jnp.stack([p[name] for name in VECTORS]), p["b_up"].reshape(1, 64)]
    found = pl.pallas_call(
        functools.partial(gather_kernel, mem_rows),
        grid=(slots // rb,),
        in_specs=[fixed(*w.shape) for w in weights] + common,
        out_specs=[pl.BlockSpec(memory_space=pl.ANY)] + specs,
        out_shape=[jax.ShapeDtypeStruct((4, 2, 2, 2, LATE, 512), BF16)] + outs,
        scratch_shapes=[
            pltpu.VMEM((ROWS, 512), BF16),
            pltpu.VMEM((4, 2, 2, 2, EARLY, 512), BF16),
            pltpu.VMEM((512, 128), F32),
            pltpu.SemaphoreType.DMA((GATHER_COPIES,)),
            pltpu.SemaphoreType.DMA((GATHER_COPIES,)),
            pltpu.SemaphoreType.DMA,
        ],
        compiler_params=params(collective_id=0, has_side_effects=True),
        name="gather_projections",
    )(*weights, *args)
    return (found[0].reshape(PARTS, LATE, 512),) + tuple(found[1:])


def key_ranges(seg, count, slots, out):
    r, c = seg.shape
    pos = lax.broadcasted_iota(jnp.int32, (r, c), 0) * c + lax.broadcasted_iota(jnp.int32, (r, c), 1)
    valid = pos < count
    ends = [jnp.sum(jnp.where(valid & (seg <= s), 1.0, 0.0)).astype(jnp.int32) for s in range(3)]
    for block in range(slots // BQ):
        first = block * BQ
        last = jnp.minimum(first + BQ, count)
        low, high, start = jnp.int32(slots), jnp.int32(0), jnp.int32(0)
        for end in ends:
            hit = (end > first) & (start < last) & (end > start)
            low = jnp.where(hit, jnp.minimum(low, start), low)
            high = jnp.where(hit, jnp.maximum(high, end), high)
            start = end
        begin = low // 128
        blocks = jnp.where(high > low, (high - begin * 128 + BK - 1) // BK, 0)
        out[0, block] = jnp.minimum(begin, slots // 128 - blocks * (BK // 128))
        out[1, block] = blocks


def key_slots(begin, block):
    return pl.ds(pl.multiple_of((begin + block * (BK // 128)) * 128, 128), BK)


def pipelined(blocks, work, first, second):
    @pl.when(blocks > 0)
    def _():
        work((0, first), None)

    pairs = jnp.maximum(blocks - 1, 0) // 2

    @pl.loop(0, pairs)
    def _(i):
        work((2 * i + 1, second), (2 * i, first))
        work((2 * i + 2, first), (2 * i + 1, second))

    j = 2 * pairs

    @pl.when(blocks - j == 2)
    def _():
        work((j + 1, second), (j, first))
        work(None, (j + 1, second))

    @pl.when(blocks - j == 1)
    def _():
        work(None, (j, first))


def fwd_kernel(
    slots, seg_ref, cnt_ref, qa_ref, kn_ref, va_ref, kmn_ref, vm_ref,
    mix_ref, lse_ref, acc_ref, m_ref, sa_ref, sb_ref, range_ref,
):
    step = pl.program_id(0)

    @pl.when(step == 0)
    def _():
        key_ranges(seg_ref[...], cnt_ref[0], slots, range_ref)

    begin, blocks = range_ref[0, step], range_ref[1, step]

    def weights(h, s):
        old = m_ref[h : h + 1, :]
        top = jnp.maximum(old, jnp.max(s, axis=0, keepdims=True))
        return jnp.exp(s - top).astype(BF16), jnp.exp(old - top), top

    def work(new, old):
        kept = {}
        for h in range(H + 1):
            if h < H and new:
                new[1][h] = dot(kn_ref[h, key_slots(begin, new[0]), 0:HA], qa_ref[h], 1, 0)
            if h < H and old:
                kept[h] = weights(h, old[1][h])
            if h > 0 and old:
                p, fade, top = kept.pop(h - 1)
                acc_ref[h - 1] = acc_ref[h - 1] * fade + dot(va_ref[h - 1, :, key_slots(begin, old[0])], p, 1, 0)
                m_ref[h - 1 : h, :] = top

    scores = [dot(kmn_ref[h, :, 0:HA], qa_ref[h], 1, 0) for h in range(H)]
    for h in range(H):
        top = jnp.max(scores[h], axis=0, keepdims=True)
        p = jnp.exp(scores[h] - top).astype(BF16)
        acc_ref[h] = dot(vm_ref[h, :, 0:MP], p, 1, 0)
        m_ref[h : h + 1, :] = top
    pipelined(blocks, work, sa_ref, sb_ref)
    for h in range(H):
        total = acc_ref[h, 64:65, :]
        mix_ref[64 * h : 64 * h + 64, :] = (acc_ref[h, 0:64, :] * (1.0 / total)).astype(BF16)
        lse_ref[h : h + 1, :] = m_ref[h : h + 1, :] + jnp.log(total)


def attend_forward(seg2, counts, qa, kn, va, kmn, vm):
    slots = qa.shape[2]
    once = pl.Buffered(1)

    def whole(a):
        return pl.BlockSpec(a.shape, lambda i: (0, 0, 0), pipeline_mode=once)

    return pl.pallas_call(
        functools.partial(fwd_kernel, slots),
        grid=(slots // BQ,),
        in_specs=[
            pl.BlockSpec(seg2.shape, lambda i: (0, 0)),
            pl.BlockSpec(memory_space=pltpu.SMEM),
            pl.BlockSpec((H, HA, BQ), lambda i: (0, 0, i)),
            whole(kn), whole(va), whole(kmn), whole(vm),
        ],
        out_specs=[pl.BlockSpec((512, BQ), lambda i: (0, i)), pl.BlockSpec((H, BQ), lambda i: (0, i))],
        out_shape=[jax.ShapeDtypeStruct((512, slots), BF16), jax.ShapeDtypeStruct((H, slots), F32)],
        scratch_shapes=[
            pltpu.VMEM((H, HA, BQ), F32),
            pltpu.VMEM((H, BQ), F32),
            pltpu.VMEM((H, BK, BQ), F32),
            pltpu.VMEM((H, BK, BQ), F32),
            pltpu.SMEM((2, slots // BQ), jnp.int32),
        ],
        compiler_params=params(),
        name="attend_forward",
    )(seg2, counts, qa, kn, va, kmn, vm)


def norm_parts(value):
    mean = jnp.mean(value, axis=-1, keepdims=True)
    centred = value - mean
    rstd = lax.rsqrt(jnp.mean(centred * centred, axis=-1, keepdims=True) + EPS)
    return centred * rstd, rstd


def norm_grad(grad_hat, hat, rstd):
    return rstd * (
        grad_hat
        - jnp.mean(grad_hat, axis=-1, keepdims=True)
        - hat * jnp.mean(grad_hat * hat, axis=-1, keepdims=True)
    )


def colsum(value):
    return jnp.sum(value, axis=0, keepdims=True)


def mid_kernel(
    rb, cnt_ref, row_ref, rbup_ref, late_ref, mix_ref, tok_ref, cot_ref,
    out_ref, gfirst_ref, mgrad_ref, delta_ref, gw_ref, vec_ref, bup_ref,
    wup_ref, wdn_ref, aup_ref, adn_ref, ao_ref,
):
    step = pl.program_id(0)

    @pl.when(step == 0)
    def _():
        for c in range(4):
            wup_ref[:, 512 * c : 512 * c + 512] = late_ref[:, 16 * c : 16 * c + 16, :].reshape(512, 512)
        wdn_ref[...] = late_ref[:, 64:128, :].reshape(2048, 512)
        aup_ref[...] = jnp.zeros_like(aup_ref)
        adn_ref[...] = jnp.zeros_like(adn_ref)
        ao_ref[...] = jnp.zeros_like(ao_ref)
        vec_ref[...] = jnp.zeros_like(vec_ref)
        bup_ref[...] = jnp.zeros_like(bup_ref)

    wo = late_ref[:, 128:144, :].reshape(512, 512)

    def row(v):
        return row_ref[v : v + 1, :]

    mixt = mix_ref[...]
    attention = dot(mixt, wo, 0, 0) + row(V_BO)
    hat1, rstd1 = norm_parts(tok_ref[...].astype(F32) + attention)
    first = hat1 * row(V_GA) + row(V_SA)
    first_low = first.astype(BF16)
    hidden = dot(first_low, wup_ref[...], 1, 0) + rbup_ref[...]
    cdf = 0.5 + 0.5 * lax.erf(hidden * (2.0 ** -0.5))
    active = (hidden * cdf).astype(BF16)
    slope = cdf + hidden * jnp.exp(hidden * hidden * -0.5) * 0.3989422804014327
    branch = dot(active, wdn_ref[...], 1, 0) + row(V_BD)
    hat2, rstd2 = norm_parts(first + branch)
    valid = lax.broadcasted_iota(jnp.int32, (rb, 1), 0) + step * rb < cnt_ref[0]
    out_ref[...] = jnp.where(valid, hat2 * row(V_GF) + row(V_SF), 0.0).astype(BF16)

    seed = jnp.where(valid, cot_ref[...].astype(F32), 0.0)
    vec_ref[V_GF : V_GF + 1, :] += colsum(seed * hat2)
    vec_ref[V_SF : V_SF + 1, :] += colsum(seed)
    grad_second = norm_grad(seed * row(V_GF), hat2, rstd2)
    branch_grad = grad_second.astype(BF16)
    adn_ref[...] += dot(active, branch_grad, 0, 0)
    vec_ref[V_BD : V_BD + 1, :] += colsum(branch_grad.astype(F32))
    hidden_grad = (dot(branch_grad, wdn_ref[...], 1, 1) * slope).astype(BF16)
    aup_ref[...] += dot(first_low, hidden_grad, 0, 0)
    bup_ref[...] += colsum(hidden_grad.astype(F32))
    first_grad = grad_second + dot(hidden_grad, wup_ref[...], 1, 1)
    vec_ref[V_GA : V_GA + 1, :] += colsum(first_grad * hat1)
    vec_ref[V_SA : V_SA + 1, :] += colsum(first_grad)
    grad_first = norm_grad(first_grad * row(V_GA), hat1, rstd1)
    gfirst_ref[...] = grad_first
    attention_grad = grad_first.astype(BF16)
    vec_ref[V_BO : V_BO + 1, :] += colsum(attention_grad.astype(F32))
    ao_ref[...] += dot(mixt, attention_grad, 1, 0)
    mgrad = dot(wo, attention_grad, 1, 1).astype(BF16)
    mgrad_ref[...] = mgrad
    prod = mgrad.astype(F32) * mixt.astype(F32)
    for h in range(H):
        delta_ref[h : h + 1, :] = jnp.sum(prod[64 * h : 64 * h + 64, :], axis=0, keepdims=True)

    @pl.when(step == pl.num_programs(0) - 1)
    def _():
        gw_ref[:, 0:16, :] = ao_ref[...].astype(gw_ref.dtype).reshape(PARTS, 16, 512)
        for c in range(4):
            gw_ref[:, 16 + 16 * c : 32 + 16 * c, :] = (
                aup_ref[:, 512 * c : 512 * c + 512].astype(gw_ref.dtype).reshape(PARTS, 16, 512)
            )
        gw_ref[:, 80:144, :] = adn_ref[...].astype(gw_ref.dtype).reshape(PARTS, 64, 512)


def middle(late, rows8, rbup, counts, mixt, tokens, cotangent, rb=256):
    slots = tokens.shape[0]
    rows = pl.BlockSpec((rb, 512), lambda i: (i, 0))
    cols = pl.BlockSpec((512, rb), lambda i: (0, i))
    once = pl.Buffered(1)
    return pl.pallas_call(
        functools.partial(mid_kernel, rb),
        grid=(slots // rb,),
        in_specs=[
            pl.BlockSpec(memory_space=pltpu.SMEM),
            pl.BlockSpec((8, 512), lambda i: (0, 0)),
            pl.BlockSpec((1, 2048), lambda i: (0, 0)),
            pl.BlockSpec((PARTS, LATE, 512), lambda i: (0, 0, 0), pipeline_mode=once),
            cols, rows, rows,
        ],
        out_specs=[
            rows, rows, cols,
            pl.BlockSpec((H, rb), lambda i: (0, i)),
            pl.BlockSpec((PARTS, 144, 512), lambda i: (0, 0, 0), pipeline_mode=once),
            pl.BlockSpec((8, 512), lambda i: (0, 0)),
            pl.BlockSpec((1, 2048), lambda i: (0, 0)),
        ],
        out_shape=[
            jax.ShapeDtypeStruct((slots, 512), BF16),
            jax.ShapeDtypeStruct((slots, 512), F32),
            jax.ShapeDtypeStruct((512, slots), BF16),
            jax.ShapeDtypeStruct((H, slots), F32),
            jax.ShapeDtypeStruct((PARTS, 144, 512), BF16),
            jax.ShapeDtypeStruct((8, 512), F32),
            jax.ShapeDtypeStruct((1, 2048), F32),
        ],
        scratch_shapes=[
            pltpu.VMEM((512, 2048), BF16),
            pltpu.VMEM((2048, 512), BF16),
            pltpu.VMEM((512, 2048), F32),
            pltpu.VMEM((2048, 512), F32),
            pltpu.VMEM((512, 512), F32),
        ],
        compiler_params=params(),
        name="middle",
    )(counts, rows8, rbup, late, mixt, tokens, cotangent)


def split3(value):
    high = value.astype(BF16)
    rest = value - high.astype(F32)
    mid = rest.astype(BF16)
    return high, mid, (rest - mid.astype(F32)).astype(BF16)


def bwd_kernel(
    slots, seg_ref, cnt_ref, qa_ref, kn_ref, ka_ref, vn_ref, kmn_ref, km_ref, vmn_ref, do_ref, lse_ref, delta_ref,
    dq_ref, dk_ref, dv_ref, dkm_ref, dvm_ref,
    q2_ref, do2_ref, dqa_ref, dka_ref, dva_ref, dkma_ref, dvma_ref, sa_ref, ga_ref, sb_ref, gb_ref, range_ref,
):
    step = pl.program_id(0)

    @pl.when(step == 0)
    def _():
        key_ranges(seg_ref[...], cnt_ref[0], slots, range_ref)
        dka_ref[...] = jnp.zeros_like(dka_ref)
        dva_ref[...] = jnp.zeros_like(dva_ref)
        dkma_ref[...] = jnp.zeros_like(dkma_ref)
        dvma_ref[...] = jnp.zeros_like(dvma_ref)

    begin, blocks = range_ref[0, step], range_ref[1, step]
    frow = lax.broadcasted_iota(jnp.int32, (16, BQ), 0)

    def feature(value, at):
        high, mid, low = (jnp.broadcast_to(v.astype(F32), (16, BQ)) for v in split3(value))
        return jnp.where(frow == at, high, jnp.where(frow == at + 1, mid, jnp.where(frow == at + 2, low, 0.0)))

    for h in range(H):
        q2_ref[h, 0:64, :] = qa_ref[h, 0:64, :]
        q2_ref[h, 64:80, :] = (qa_ref[h, 64:80, :].astype(F32) + feature(-lse_ref[h : h + 1, :], 3)).astype(BF16)
        do2_ref[h, 0:64, :] = do_ref[64 * h : 64 * h + 64, :]
        do2_ref[h, 64:80, :] = feature(-delta_ref[h : h + 1, :], 0).astype(BF16)

    def work(new, old):
        kept = {}
        for h in range(H + 1):
            if h < H and new:
                ks = key_slots(begin, new[0])
                new[1][0][h] = dot(kn_ref[h, ks, 0:HA], q2_ref[h], 1, 0)
                new[1][1][h] = dot(vn_ref[h, ks, 0:HA], do2_ref[h], 1, 0)
            if h < H and old:
                p = jnp.exp(old[1][0][h])
                kept[h] = p.astype(BF16), (p * old[1][1][h]).astype(BF16)
            if h > 0 and old:
                ks = key_slots(begin, old[0])
                p, ds = kept.pop(h - 1)
                dva_ref[h - 1, :, ks] += dot(do2_ref[h - 1, 0:64, :], p, 1, 1)
                dka_ref[h - 1, :, ks] += dot(q2_ref[h - 1, 0:64, :], ds, 1, 1)
                dqa_ref[h - 1] += dot(ka_ref[h - 1, 0:64, ks], ds, 1, 0)

    ps = [jnp.exp(dot(kmn_ref[h, :, 0:HA], q2_ref[h], 1, 0)) for h in range(H)]
    dss = [(ps[h] * dot(vmn_ref[h, :, 0:HA], do2_ref[h], 1, 0)).astype(BF16) for h in range(H)]
    for h in range(H):
        dvma_ref[h, :, 0:MP] += dot(do2_ref[h, 0:64, :], ps[h].astype(BF16), 1, 1)
        dkma_ref[h, :, 0:MP] += dot(q2_ref[h, 0:64, :], dss[h], 1, 1)
        dqa_ref[h] = dot(km_ref[h, 0:64, 0:MP], dss[h], 1, 0)
    pipelined(blocks, work, (sa_ref, ga_ref), (sb_ref, gb_ref))
    for h in range(H):
        dq_ref[64 * h : 64 * h + 64, :] = (dqa_ref[h] * HD ** -0.5).astype(BF16)

    @pl.when(step == pl.num_programs(0) - 1)
    def _():
        for h in range(H):
            s = slice(64 * h, 64 * h + 64)
            dk_ref[s, :] = dka_ref[h].astype(BF16)
            dv_ref[s, :] = dva_ref[h].astype(BF16)
            dkm_ref[s, :] = dkma_ref[h].astype(BF16)
            dvm_ref[s, :] = dvma_ref[h].astype(BF16)


def attend_backward(seg2, counts, qa, kn, ka, vn, kmn, km, vmn, mgrad, lse, delta):
    slots = qa.shape[2]
    once = pl.Buffered(1)

    def full(a):
        return pl.BlockSpec(a.shape, lambda i: (0, 0, 0), pipeline_mode=once)

    cols = pl.BlockSpec((512, BQ), lambda i: (0, i))
    stat = pl.BlockSpec((H, BQ), lambda i: (0, i))
    whole = pl.BlockSpec((512, slots), lambda i: (0, 0), pipeline_mode=once)
    mwhole = pl.BlockSpec((512, 128), lambda i: (0, 0))
    block = pltpu.VMEM((H, BK, BQ), F32)
    return pl.pallas_call(
        functools.partial(bwd_kernel, slots),
        grid=(slots // BQ,),
        in_specs=[
            pl.BlockSpec(seg2.shape, lambda i: (0, 0)),
            pl.BlockSpec(memory_space=pltpu.SMEM),
            pl.BlockSpec((H, HA, BQ), lambda i: (0, 0, i)),
            full(kn), full(ka), full(vn), full(kmn), full(km), full(vmn), cols, stat, stat,
        ],
        out_specs=[cols, whole, whole, mwhole, mwhole],
        out_shape=[jax.ShapeDtypeStruct((512, slots), BF16)] * 3 + [jax.ShapeDtypeStruct((512, 128), BF16)] * 2,
        scratch_shapes=[
            pltpu.VMEM((H, HA, BQ), BF16),
            pltpu.VMEM((H, HA, BQ), BF16),
            pltpu.VMEM((H, HD, BQ), F32),
            pltpu.VMEM((H, HD, slots), F32),
            pltpu.VMEM((H, HD, slots), F32),
            pltpu.VMEM((H, HD, 128), F32),
            pltpu.VMEM((H, HD, 128), F32),
            block, block, block, block,
            pltpu.SMEM((2, slots // BQ), jnp.int32),
        ],
        compiler_params=params(),
        name="attend_backward",
    )(seg2, counts, qa, kn, ka, vn, kmn, km, vmn, mgrad, lse, delta)


SUM_EARLY = (
    (slice(0, 48), "yxz"),
    (slice(48, 96), "xyz"),
    (slice(96, 112), "xzy"),
    (slice(112, 144), "yzx"),
)
SUM_LATE = ((slice(144, 176), "xyz"), (slice(176, 208), "yxz"))
SUM_PARTS = SUM_EARLY + SUM_LATE
SUM_COPIES = 6 * len(SUM_PARTS)


def weight_grads(step, tok_ref, dq_ref, dk_ref, dv_ref, dkm_ref, dvm_ref, memt_ref, acc_ref, sum_ref):
    @pl.when(step == 0)
    def _():
        acc_ref[0:512, :] = jnp.zeros((512, 512), F32)
        acc_ref[512:1024, :] = dot(dkm_ref[...], memt_ref[...], 1, 1)
        acc_ref[1024:1536, :] = dot(dvm_ref[...], memt_ref[...], 1, 1)
        sum_ref[...] = jnp.zeros_like(sum_ref)
        sum_ref[:, 1:2] = jnp.sum(dvm_ref[...].astype(F32), axis=1, keepdims=True)

    tok = tok_ref[...]
    dq, dk, dv = dq_ref[...], dk_ref[...], dv_ref[...]
    acc_ref[0:512, :] += dot(dq, tok, 1, 0)
    acc_ref[512:1024, :] += dot(dk, tok, 1, 0)
    acc_ref[1024:1536, :] += dot(dv, tok, 1, 0)
    sum_ref[:, 0:1] += jnp.sum(dq.astype(F32), axis=1, keepdims=True)
    sum_ref[:, 1:2] += jnp.sum(dv.astype(F32), axis=1, keepdims=True)


def late_grads(dkm_ref, dvm_ref, vec_ref, bup_ref, wt_ref, acc_ref, sum_ref, late):
    for j in range(3):
        late(slice(16 * j, 16 * j + 16), slice(0, 512), acc_ref[512 * j : 512 * j + 512, :].T.astype(BF16))
    gmem = dot(wt_ref[512:1024, :], dkm_ref[...], 0, 0) + dot(wt_ref[1024:1536, :], dvm_ref[...], 0, 0)
    late(slice(48, 64), slice(0, 128), gmem.astype(BF16))
    lane = lax.broadcasted_iota(jnp.int32, (512, 128), 1)
    vecs = jnp.concatenate([vec_ref[...], jnp.zeros((120, 512), F32)], axis=0).T
    late(slice(48, 64), slice(128, 256), jnp.where(lane < 2, sum_ref[...], vecs).astype(BF16))
    rows = [bup_ref[0:1, 256 * v : 256 * v + 256] for v in range(8)] + [jnp.zeros((8, 256), F32)]
    rows = jnp.concatenate(rows, axis=0).astype(BF16)
    late(slice(48, 64), slice(256, 512), jnp.broadcast_to(rows[None], (PARTS, 16, 256)).reshape(512, 256))


def token_grads(gtok_ref, gfirst_ref, dq_ref, dk_ref, dv_ref, wt_ref):
    gtok_ref[...] = (
        gfirst_ref[...]
        + dot(dq_ref[...], wt_ref[0:512, :], 0, 0)
        + dot(dk_ref[...], wt_ref[512:1024, :], 0, 0)
        + dot(dv_ref[...], wt_ref[1024:1536, :], 0, 0)
    )


def scatter_kernel(
    half, tok_ref, dq_ref, dk_ref, dv_ref, dkm_ref, dvm_ref, gfirst_ref, vec_ref, bup_ref, wt_ref, memt_ref, early_ref,
    gtok_ref, out_ref, acc_ref, sum_ref, late, parts_sum, other, send, recv, local, *landing,
):
    step = pl.program_id(0)
    place = Place()
    copies = Copies(send, recv)
    slots = dict(zip(slot_shapes(SUM_PARTS), landing))
    crossing = [copies.number() for _ in SUM_PARTS]
    parts = []
    for index, (rows, order) in enumerate(SUM_PARTS):
        mine = {key[1:]: slot for key, slot in slots.items() if key[0] == index}
        parts.append(scatter_part(place, copies, parts_sum, mine, out_ref, rows, order))
    firsts, lasts = parts[: len(SUM_EARLY)], parts[len(SUM_EARLY) :]

    def load(index):
        rows = SUM_EARLY[index][0]
        return pltpu.make_async_copy(
            early_ref.at[:, :, :, place.core, rows], parts_sum.at[:, :, :, rows], local.at[index]
        )

    def cross(source, base, rows, number):
        old = slice(rows.start - base, rows.stop - base)
        copies.start(
            lambda: source.at[:, :, :, place.far, old], lambda: other.at[:, :, :, rows], number, place.partner
        )

    @pl.when(step == 0)
    def _():
        everyone = place.greet()
        for index in range(len(SUM_EARLY)):
            load(index).start()
        everyone()
        for number, (rows, _) in zip(crossing, SUM_EARLY):
            cross(early_ref, 0, rows, number)

    @pl.when(step == 2)
    def _():
        for index, (rows, _) in enumerate(SUM_EARLY):
            load(index).wait()
            join(place, copies, parts_sum, None, other, rows, crossing[index])
            next(firsts[index])

    @pl.when(step < half)
    def _():
        weight_grads(step, tok_ref, dq_ref, dk_ref, dv_ref, dkm_ref, dvm_ref, memt_ref, acc_ref, sum_ref)

    @pl.when(step == half - 1)
    def _():
        def put(rows, lanes, value):
            late[:, :, :, :, rows, lanes] = value.reshape(4, 2, 2, 2, 16, value.shape[1])

        late_grads(dkm_ref, dvm_ref, vec_ref, bup_ref, wt_ref, acc_ref, sum_ref, put)
        for number, (rows, _) in zip(crossing[len(SUM_EARLY) :], SUM_LATE):
            cross(late, LATE, rows, number)
        advance(firsts)

    @pl.when(step >= half)
    def _():
        token_grads(gtok_ref, gfirst_ref, dq_ref, dk_ref, dv_ref, wt_ref)

    @pl.when(step == half)
    def _():
        for index, (rows, _) in enumerate(SUM_LATE):
            join(
                place, copies, parts_sum,
                lambda z, old=slice(rows.start - LATE, rows.stop - LATE): late[z, :, :, place.core, old],
                other, rows, crossing[len(SUM_EARLY) + index],
            )
            next(lasts[index])

    @pl.when(step == half + 1)
    def _():
        advance(firsts)

    @pl.when(step == half + 2)
    def _():
        advance(lasts)

    @pl.when(step == 2 * half - 1)
    def _():
        advance(firsts)
        advance(lasts)
        advance(lasts)
        copies.finish()


def plain_kernel(
    half, tok_ref, dq_ref, dk_ref, dv_ref, dkm_ref, dvm_ref, gfirst_ref, vec_ref, bup_ref, wt_ref, memt_ref,
    gtok_ref, late_ref, acc_ref, sum_ref,
):
    step = pl.program_id(0)

    @pl.when(step < half)
    def _():
        weight_grads(step, tok_ref, dq_ref, dk_ref, dv_ref, dkm_ref, dvm_ref, memt_ref, acc_ref, sum_ref)

    @pl.when(step == half - 1)
    def _():
        def put(rows, lanes, value):
            late_ref[:, rows, lanes] = value.reshape(PARTS, 16, value.shape[1])

        late_grads(dkm_ref, dvm_ref, vec_ref, bup_ref, wt_ref, acc_ref, sum_ref, put)

    @pl.when(step >= half)
    def _():
        token_grads(gtok_ref, gfirst_ref, dq_ref, dk_ref, dv_ref, wt_ref)


def tail(early, tokens, dq, dk, dv, dkm, dvm, gfirst, vec, bup, wt, memt, remote):
    slots = tokens.shape[0]
    rb = 512
    half = slots // rb

    def fixed(*shape):
        return pl.BlockSpec(shape, lambda i: (0,) * len(shape))

    cols = pl.BlockSpec((512, rb), lambda i: (0, i % half))
    later = pl.BlockSpec((rb, 512), lambda i: (jnp.maximum(i - half, 0), 0))
    in_specs = [
        pl.BlockSpec((rb, 512), lambda i: (jnp.minimum(i, half - 1), 0)),
        cols, cols, cols, fixed(512, 128), fixed(512, 128), later,
        fixed(8, 512), fixed(1, 2048), fixed(1536, 512), fixed(512, 128),
    ]
    args = (tokens, dq, dk, dv, dkm, dvm, gfirst, vec, bup, wt, memt)
    gtok = jax.ShapeDtypeStruct((slots, 512), F32)
    scratch = [pltpu.VMEM((1536, 512), F32), pltpu.VMEM((512, 128), F32)]
    if not remote:
        return pl.pallas_call(
            functools.partial(plain_kernel, half),
            grid=(2 * half,),
            in_specs=in_specs,
            out_specs=[later, fixed(PARTS, EARLY, 512)],
            out_shape=[gtok, jax.ShapeDtypeStruct((PARTS, EARLY, 512), BF16)],
            scratch_shapes=scratch,
            compiler_params=params(),
            name="tail",
        )(*args)
    return pl.pallas_call(
        functools.partial(scatter_kernel, half),
        grid=(2 * half,),
        in_specs=in_specs + [pl.BlockSpec(memory_space=pl.ANY)],
        out_specs=[later, fixed(ROWS, 512)],
        out_shape=[gtok, jax.ShapeDtypeStruct((ROWS, 512), F32)],
        scratch_shapes=scratch
        + [
            pltpu.VMEM((4, 2, 2, 2, EARLY, 512), BF16),
            pltpu.VMEM((4, 2, 2, ROWS, 512), BF16),
            pltpu.VMEM((4, 2, 2, ROWS, 512), BF16),
            pltpu.SemaphoreType.DMA((SUM_COPIES,)),
            pltpu.SemaphoreType.DMA((SUM_COPIES,)),
            pltpu.SemaphoreType.DMA((len(SUM_EARLY),)),
        ]
        + [pltpu.VMEM(shape, BF16) for shape in slot_shapes(SUM_PARTS).values()],
        compiler_params=params(collective_id=1, has_side_effects=True),
        name="tail_scatter",
    )(*args, early.reshape(4, 2, 2, 2, LATE, 512))


def unpack_kernel(sum_ref, wo, up, dn, wq, wk, wv, memory, vectors, b_up):
    me = lax.axis_index("dp")
    wo[...] = sum_ref[0:16]
    for c in range(4):
        up[:, 512 * c : 512 * c + 512] = sum_ref[16 + 16 * c : 32 + 16 * c]
    dn[...] = sum_ref[80:144]
    wq[...] = sum_ref[144:160]
    wk[...] = sum_ref[160:176]
    wv[...] = sum_ref[176:192]
    memory[...] = sum_ref[192:208, 0:128].T[0 : memory.shape[0], :]
    vectors[...] = sum_ref[192:208, 128:256].T[0:8, :]
    row = lax.broadcasted_iota(jnp.int32, (16, 256), 0)
    lane = lax.broadcasted_iota(jnp.int32, (16, 256), 1)
    own = jnp.sum(jnp.where(row * 4 + lane // 64 == me, sum_ref[192:208, 256:512], 0.0), axis=0, keepdims=True)
    b_up[...] = own[:, 0:64] + own[:, 64:128] + own[:, 128:192] + own[:, 192:256]


def unpack(sums, mem_rows):
    shapes = [(16, 512), (16, 2048), (64, 512), (16, 512), (16, 512), (16, 512), (mem_rows, 16), (8, 16), (1, 64)]
    found = pl.pallas_call(
        unpack_kernel,
        out_shape=[jax.ShapeDtypeStruct(s, F32) for s in shapes],
        compiler_params=params(),
        name="unpack",
    )(sums)
    out = dict(zip(("w_out", "w_up", "w_down", "w_query", "w_key", "w_value", "memory"), found[:7]))
    for index, name in enumerate(VECTORS):
        out[name] = found[7][index]
    out["b_up"] = found[8].reshape(64)
    return out


NAMES = (
    "memory", "w_query", "b_query", "w_key", "w_value", "b_value", "w_out", "b_out", "gain_attn",
    "shift_attn", "w_up", "b_up", "w_down", "b_down", "gain_ffn", "shift_ffn",
)


def pack_whole(p):
    mem_rows = p["memory"].shape[0]
    mats = [p[name].reshape(PARTS, 16, 512) for name in ("w_query", "w_key", "w_value", "w_out")]
    up = p["w_up"].reshape(PARTS, 16, 4, 512).transpose(0, 2, 1, 3).reshape(PARTS, 64, 512)
    memory = jnp.pad(p["memory"].T, ((0, 0), (0, 128 - mem_rows))).reshape(PARTS, 16, 128)
    vectors = jnp.stack([p[name] for name in VECTORS], axis=1)
    vectors = jnp.pad(vectors, ((0, 0), (0, 120))).reshape(PARTS, 16, 128)
    own = jnp.arange(2048)[None] // 64 == jnp.arange(PARTS)[:, None]
    b_up = jnp.where(own, p["b_up"][None], 0).astype(BF16).reshape(PARTS, 8, 256)
    b_up = jnp.pad(b_up, ((0, 0), (0, 8), (0, 0)))
    small = jnp.concatenate([memory, vectors, b_up], axis=2)
    return jnp.concatenate(mats[:3] + [small, up, p["w_down"].reshape(PARTS, 64, 512), mats[3]], axis=1)


def unpack_whole(early, late, mem_rows):
    small = late[:, 48:64]
    vectors = small[:, :, 128:136].reshape(512, 8)
    out = {
        "memory": small[:, :, 0:mem_rows].reshape(512, mem_rows).T,
        "w_query": late[:, 0:16].reshape(512, 512),
        "w_key": late[:, 16:32].reshape(512, 512),
        "w_value": late[:, 32:48].reshape(512, 512),
        "w_out": early[:, 0:16].reshape(512, 512),
        "w_up": early[:, 16:80].reshape(PARTS, 4, 16, 512).transpose(0, 2, 1, 3).reshape(512, 2048),
        "w_down": early[:, 80:144].reshape(2048, 512),
        "b_up": small[0, 0:8, 256:512].reshape(2048),
    }
    for index, name in enumerate(VECTORS):
        out[name] = vectors[:, index]
    return out


def axis_of(name):
    return 1 if name == "memory" else 0


def shards(n, tokens, segment, counts, *rest):
    p = dict(zip(NAMES, rest[:-1]))
    cotangent = rest[-1]
    slots = tokens.shape[0]
    mem_rows = p["memory"].shape[0]
    whole = None
    if n != PARTS:
        whole = pack_whole({k: lax.all_gather(v, "dp", axis=axis_of(k), tiled=True) for k, v in p.items()})
    found = projections(p, whole, tokens, segment, counts, mem_rows)
    late, qa, ka, va, kn, vn, km, vm, kmn, vmn, wt, memt, rows8, rbup = found
    seg2 = segment.reshape(slots // 128, 128)
    mixt, lse = attend_forward(seg2, counts, qa, kn, va, kmn, vm)
    output, gfirst, mgrad, delta, early, vec, bup = middle(late, rows8, rbup, counts, mixt, tokens, cotangent)
    dq, dk, dv, dkm, dvm = attend_backward(seg2, counts, qa, kn, ka, vn, kmn, km, vmn, mgrad, lse, delta)
    gtok, sums = tail(early, tokens, dq, dk, dv, dkm, dvm, gfirst, vec, bup, wt, memt, n == PARTS)
    if n == PARTS:
        grads = unpack(sums, mem_rows)
    else:
        full = unpack_whole(early.astype(F32), sums.astype(F32), mem_rows)
        grads = {
            k: lax.psum_scatter(v, "dp", scatter_dimension=axis_of(k), tiled=True) for k, v in full.items()
        }
    return (output, gtok) + tuple(grads[name] for name in NAMES)


def solution(mesh):
    n = mesh.shape["dp"]
    row, mat, mem = P("dp"), P("dp", None), P(None, "dp")
    spec = {name: mat if name.startswith("w_") else row for name in NAMES}
    spec["memory"] = mem
    weights = tuple(spec[name] for name in NAMES)
    return jax.shard_map(
        functools.partial(shards, n),
        mesh=mesh,
        in_specs=(mat, row, row) + weights + (mat,),
        out_specs=(mat, mat) + weights,
        check_vma=False,
    )
```

time: 661 us -> 261 us (0.39)
  waiting for transfers between devices: 392 us -> 0 us
  Pallas kernels: 227 us -> 248 us
  between operations: 14.4 us -> 1.33 us
  other arithmetic: 12.1 us -> 0 us
    reduce_scatter x2 -> x0, waiting for transfers between devices: 318 us -> none  [the longest x1 184 us: shards(): late = lax.psum_scatter(late.astype(F32), 'dp', scatter_dimension=0)]
    pallas_call x2 -> x3, Pallas kernels: 22.5 us -> 104 us  [the longest x1 54.1 us: projections(): pl.pallas_call(functools.partial(gather_kernel, mem_rows), grid=(slots //...]
    all_gather x1 -> x0, waiting for transfers between devices: 73.6 us -> none  [shards(): g = lax.all_gather(pack_part(p, me), 'dp', axis=0, tiled=False)]
    pallas_call x1, Pallas kernels: 74.5 us -> 33.2 us  [attend_forward(): pl.pallas_call(functools.partial(fwd_kernel, slots), grid=(slots // BQ,),...]
    pallas_call x1, Pallas kernels: 79 us -> 59.7 us  [attend_backward(): pl.pallas_call(functools.partial(bwd_kernel, slots), grid=(slots // BQ,),...]
    convert_element_type x2 -> x0, other arithmetic: 11.4 us -> none  [the longest x1 7.32 us: shards(): early = lax.psum_scatter(early.astype(F32), 'dp', scatter_dimension=0)]
  transfers between devices with their start and end apart: 3 -> 0, of which waited for: 3 -> 0; matrix products, arithmetic and copies ran while one was open for 2% -> 0% of each run, Pallas kernels for 0% -> 0%
where the time goes in v4:
time: 261 us; the launch traced here: 259 us
  Pallas kernels  248 us (95%)
  local copies, waits for them, and re-layouts  10.3 us (4%)
    pallas_call x1, Pallas kernels, attend_backward(): pl.pallas_call(functools.partial(bwd_kernel, slots), grid=(slots // BQ,),...  59.7 us
    pallas_call x1, Pallas kernels, projections(): pl.pallas_call(functools.partial(gather_kernel, mem_rows), grid=(slots //...  54.1 us
    pallas_call x1, Pallas kernels, middle(): pl.pallas_call(functools.partial(mid_kernel, rb), grid=(slots // rb,), in...  51.1 us
    pallas_call x1, Pallas kernels, tail(): pl.pallas_call(functools.partial(scatter_kernel, half), grid=(2 * half,),...  47.8 us
    pallas_call x1, Pallas kernels, attend_forward(): pl.pallas_call(functools.partial(fwd_kernel, slots), grid=(slots // BQ,),...  33.2 us
    unnamed x3, local copies, waits for them, and re-layouts  7.38 us

profile of v4, /device:TPU:0, one launch (start us, length us, event | category | flops | bytes accessed | tf_op | source)
XLA Modules:
  0.0 259.2 jit_solution(2474168625081425528)
XLA Ops:
  1.3 1.4 stack.35.vectors
  2.7 1.4 copy.38.memory
  4.0 54.1 %gather_projections.1 = (bf16[4,2,2,2,144,512]{5,4,3,2,1,0:T(8,128)(2,1)}, bf16[8,80,2048]{2,1,0:T(8,128)(2,1)}, bf16[8,80,2048]{2,1,0:T(8,128)(2,1)}, bf16[8,80...) custom-call(bf16[16,512]{1,0:T(8,128)(2,1)} %wq.1, ...), custom_call_target="tpu_custom_call" | custom-call | tf_op jit(solution)/shard_map/gather_projections/pallas_call | solution.py:368
  58.1 33.2 %attend_forward.1 = (bf16[512,2048]{1,0:T(8,128)(2,1)}, f32[8,2048]{1,0:T(8,128)}) custom-call(s32[16,128]{1,0:T(8,128)} %bitcast.33, s32[1]{0:T(128)S(6)} %copy.41.cnt_ref, bf16[8,80,2048]{2,1,0:T(8,128)(2,1)} %get-tuple-element.60.qa_ref, bf16[8,2048,128]{2,1,0:T(8,128)(2,1)} %get-tuple-element.61.kn_ref, bf16[8,80,2048]{2,1,0:T(8,128)(2,1)} %get-tuple-element.62.va_ref, ...), custom_call_target="tpu_custom_call" | custom-call | tf_op jit(solution)/shard_map/attend_forward/pallas_call | solution.py:485
  91.3 51.1 %middle.1 = (bf16[2048,512]{1,0:T(8,128)(2,1)}, f32[2048,512]{1,0:T(8,128)}, bf16[512,2048]{1,0:T(8,128)(2,1)}, f32[8,2048]{1,0:T(8,128)}, bf16[32,144,512]{2,1,...) custom-call(s32[1]{0:T(128)S(6)} %copy.41.cnt_ref, f32[8,512]{1,0:T(8,128)} %get-tuple-element.57.row_ref, ...), custom_call_target="tpu_custom_call" | custom-call | tf_op jit(solution)/shard_map/middle/pallas_call | solution.py:603
  142.4 59.7 %attend_backward.1 = (bf16[512,2048]{1,0:T(8,128)(2,1)}, bf16[512,2048]{1,0:T(8,128)(2,1)}, bf16[512,2048]{1,0:T(8,128)(2,1)}, bf16[512,128]{1,0:T(8,128)(2,1)}, bf16[512,128]{1,0:T(8,128)(2,1)}) custom-call(s32[16,128]{1,0:T(8,128)} %bitcast.34, s32[1]{0:T(128)S(6)} %copy.41.cnt_ref, bf16[8,80,2048]{2,1,0:T(8,128)(2,1)} %get-tuple-element.60.qa_ref, ...), custom_call_target="tpu_custom_call" | custom-call | tf_op jit(solution)/shard_map/attend_backward/pallas_call | solution.py:725
  202.1 47.8 %tail_scatter.1 = (f32[2048,512]{1,0:T(8,128)}, f32[208,512]{1,0:T(8,128)}) custom-call(bf16[2048,512]{1,0:T(8,128)(2,1)} %tok_ref.5, bf16[512,2048]{1,0:T(8,128)(2,1)} %get-tuple-element.74.dq_ref, bf16[512,2048]{1,0:T(8,128)(2,1)} %get-tuple-element.75.dk_ref, bf16[512,2048]{1,0:T(8,128)(2,1)} %get-tuple-element.76.dv_ref, ...), custom_call_target="tpu_custom_call" | custom-call | tf_op jit(solution)/shard_map/tail_scatter/pallas_call | solution.py:941
  249.9 1.8 unpack.1
  251.6 1.4 copy.39
  253.0 1.5 slice_bitcast_fusion
  254.5 4.6 %copy.42 = f32[2048,512]{1,0:T(8,128)} copy(f32[2048,512]{1,0:T(8,128)} %get-tuple-element.141) | data formatting | bytes 8388608

commit v5 on v4

--- a/solution.py
+++ b/solution.py
@@ -16,6 +16,7 @@
 BQ = 256
 BK = 256
 MP = 32
+LONGEST = 1024
 F32 = jnp.float32
 BF16 = jnp.bfloat16
 VMEM_LIMIT = 60 << 20
@@ -201,14 +202,14 @@
     return block, jnp.concatenate([block, jnp.zeros((128 - HA, rows.shape[1]), BF16)], axis=0).T
 
 
-def pack(own, place, wq, wk, wv, wo, up, dn, memory, vectors, b_up):
+def pack(own, place, wq, wk, wv, wo, up, dn, memory, b_up, vectors):
     own[0:16] = wq[...]
     own[16:32] = wk[...]
     own[32:48] = wv[...]
-    mem_rows = memory.shape[0]
     own[48:64] = jnp.zeros((16, 512), BF16)
-    own[48:64, 0:mem_rows] = memory[...].astype(F32).T.astype(BF16)
-    own[48:64, 128:136] = vectors[...].astype(F32).T.astype(BF16)
+    own[48:64, 0 : memory.shape[1]] = memory[...]
+    values = jnp.concatenate([vector[...].astype(F32) for vector in vectors], axis=0)
+    own[48:64, 128:136] = values.T.astype(BF16)
     value = jnp.concatenate([b_up[...].astype(F32)] * 4, axis=1)
     row = lax.broadcasted_iota(jnp.int32, (16, 256), 0)
     lane = lax.broadcasted_iota(jnp.int32, (16, 256), 1)
@@ -269,11 +270,13 @@
 
 
 def gather_kernel(
-    mem_rows, wq, wk, wv, wo, up, dn, memory, vectors, b_up, tok_ref, seg_ref, cnt_ref,
-    late_ref, qa_ref, ka_ref, va_ref, kn_ref, vn_ref, km_ref, vm_ref, kmn_ref, vmn_ref,
-    wt_ref, memt_ref, rows_ref, rbup_ref, own, early, bias_ref, send, recv, local,
+    mem_rows, half, wq, wk, wv, wo, up, dn, memory, b_up, v0, v1, v2, v3, v4, v5, v6, v7, tok_ref, seg_ref, cnt_ref,
+    late_ref, qa_ref, ka_ref, kn_ref, vn_ref, km_ref, kmn_ref, vmn_ref,
+    wt_ref, memt_ref, rows_ref, rbup_ref, mix_ref, lse_ref,
+    own, early, bias_ref, vm_ref, va_block, qa_all, kn_all, va_all, acc_ref, m_ref, sa_ref, sb_ref, send, recv, local,
 ):
     step = pl.program_id(0)
+    slots = kn_all.shape[1]
     place = Place()
     copies = Copies(send, recv)
     arrivals, late_arrivals = [], []
@@ -283,28 +286,48 @@
     @pl.when(step == 0)
     def _():
         everyone = place.greet()
-        pack(own, place, wq, wk, wv, wo, up, dn, memory, vectors, b_up)
+        pack(own, place, wq, wk, wv, wo, up, dn, memory, b_up, (v0, v1, v2, v3, v4, v5, v6, v7))
         early[place.mine + (place.core,)] = own[0:EARLY]
         everyone()
         advance(firsts)
         keep = pltpu.make_async_copy(own.at[EARLY:ROWS], late_ref.at[place.mine + (place.core,)], local)
         keep.start()
-        advance(lasts)
         advance(firsts)
         advance(firsts)
+        keep.wait()
+        advance(lasts)
         advance(firsts)
         for block, number in arrivals:
             copies.landed(block(), number, place.partner)
-        keep.wait()
+        prepare(
+            mem_rows, early, wt_ref, memt_ref, rows_ref, rbup_ref, bias_ref, km_ref, vm_ref, kmn_ref, vmn_ref,
+        )
+
+    @pl.when(step < half)
+    def _():
+        project(step, tok_ref, seg_ref, cnt_ref, wt_ref, bias_ref, qa_ref, ka_ref, va_block, kn_ref, vn_ref)
+        here = pl.ds(pl.multiple_of(step * tok_ref.shape[0], 128), tok_ref.shape[0])
+        qa_all[:, :, here] = qa_ref[...]
+        va_all[:, :, here] = va_block[...]
+        kn_all[:, here, :] = kn_ref[...]
+
+    @pl.when(step == half - 1)
+    def _():
         advance(lasts)
-        prepare(
-            mem_rows, early, wt_ref, memt_ref, rows_ref, rbup_ref, bias_ref,
-            km_ref, vm_ref, kmn_ref, vmn_ref,
+
+    @pl.when(step >= half)
+    def _():
+        block = step - half
+        reach = LONGEST // BQ
+        begin = jnp.maximum(block - reach, 0)
+        end = jnp.minimum(block + reach + 1, slots // BQ)
+        queries = qa_all.at[:, :, pl.ds(pl.multiple_of(block * BQ, BQ), BQ)]
+        attend(
+            begin * (BQ // 128), (end - begin) * (BQ // BK), queries, kn_all, va_all, kmn_ref, vm_ref, mix_ref, lse_ref,
+            acc_ref, m_ref, sa_ref, sb_ref,
         )
 
-    project(step, tok_ref, seg_ref, cnt_ref, wt_ref, bias_ref, qa_ref, ka_ref, va_ref, kn_ref, vn_ref)
-
-    @pl.when(step == 1)
+    @pl.when(step == half + 2)
     def _():
         advance(lasts)
 
@@ -331,56 +354,83 @@
     project(step, tok_ref, seg_ref, cnt_ref, wt_ref, bias_ref, qa_ref, ka_ref, va_ref, kn_ref, vn_ref)
 
 
+def fixed(*shape):
+    return pl.BlockSpec(shape, lambda i: (0,) * len(shape))
+
+
 def projections(p, whole, tokens, segment, counts, mem_rows):
     slots = tokens.shape[0]
     rb = 512
-
-    def fixed(*shape):
-        return pl.BlockSpec(shape, lambda i: (0,) * len(shape))
-
+    half = slots // rb
     wide, tall = (H, HA, slots), (H, slots, 128)
-    shapes = [wide, wide, wide, tall, tall] + [(H, HA, 128)] * 2 + [(H, MP, 128)] * 2 + [(1536, 512), (512, 128)]
-    outs = [jax.ShapeDtypeStruct(s, BF16) for s in shapes]
-    outs += [jax.ShapeDtypeStruct((8, 512), F32), jax.ShapeDtypeStruct((1, 2048), F32)]
-    blk = pl.BlockSpec((H, HA, rb), lambda i: (0, 0, i))
-    tblk = pl.BlockSpec((H, rb, 128), lambda i: (0, i, 0))
-    specs = [blk, blk, blk, tblk, tblk] + [fixed(*o.shape) for o in outs[5:]]
+    mwide, mtall = (H, HA, 128), (H, MP, 128)
+
+    def at(i):
+        return jnp.minimum(i, half - 1)
+
+    blk = pl.BlockSpec((H, HA, rb), lambda i: (0, 0, at(i)))
+    tblk = pl.BlockSpec((H, rb, 128), lambda i: (0, at(i), 0))
     common = [
-        pl.BlockSpec((rb, 512), lambda i: (i, 0)),
-        pl.BlockSpec((1, rb), lambda i: (0, i)),
+        pl.BlockSpec((rb, 512), lambda i: (at(i), 0)),
+        pl.BlockSpec((1, rb), lambda i: (0, at(i))),
         pl.BlockSpec(memory_space=pltpu.SMEM),
     ]
     args = (tokens, segment.reshape(1, slots), counts)
+
+    def outs(shapes):
+        found = [jax.ShapeDtypeStruct(s, BF16) for s in shapes]
+        return found + [jax.ShapeDtypeStruct((8, 512), F32), jax.ShapeDtypeStruct((1, 2048), F32)]
+
     if whole is not None:
+        shapes = outs([wide, wide, wide, tall, tall, mwide, mwide, mtall, mtall, (1536, 512), (512, 128)])
         found = pl.pallas_call(
             functools.partial(project_kernel, mem_rows),
-            grid=(slots // rb,),
+            grid=(half,),
             in_specs=[fixed(PARTS, EARLY, 512)] + common,
-            out_specs=specs,
-            out_shape=outs,
+            out_specs=[blk, blk, blk, tblk, tblk] + [fixed(*o.shape) for o in shapes[5:]],
+            out_shape=shapes,
             scratch_shapes=[pltpu.VMEM((512, 128), F32)],
             compiler_params=params(),
             name="projections",
         )(whole[:, 0:EARLY], *args)
-        return (whole[:, EARLY:],) + tuple(found)
-    weights = [p[name] for name in ("w_query", "w_key", "w_value", "w_out", "w_up", "w_down", "memory")]
-    weights += [jnp.stack([p[name] for name in VECTORS]), p["b_up"].reshape(1, 64)]
+        qa, ka, va, kn, vn, km, vm, kmn, vmn, wt, memt, rows8, rbup = found
+        mixt, lse = attend_forward(segment.reshape(slots // 128, 128), counts, qa, kn, va, kmn, vm)
+        return whole[:, EARLY:], qa, ka, kn, vn, km, kmn, vmn, wt, memt, rows8, rbup, mixt, lse
+    weights = [p[name] for name in ("w_query", "w_key", "w_value", "w_out", "w_up", "w_down")]
+    weights += [p["memory"].T, p["b_up"].reshape(1, 64)] + [p[name].reshape(1, 16) for name in VECTORS]
+    shapes = outs([wide, wide, tall, tall, mwide, mtall, mtall, (1536, 512), (512, 128)])
     found = pl.pallas_call(
-        functools.partial(gather_kernel, mem_rows),
-        grid=(slots // rb,),
+        functools.partial(gather_kernel, mem_rows, half),
+        grid=(half + slots // BQ,),
         in_specs=[fixed(*w.shape) for w in weights] + common,
-        out_specs=[pl.BlockSpec(memory_space=pl.ANY)] + specs,
-        out_shape=[jax.ShapeDtypeStruct((4, 2, 2, 2, LATE, 512), BF16)] + outs,
+        out_specs=[pl.BlockSpec(memory_space=pl.ANY), blk, blk, tblk, tblk]
+        + [fixed(*o.shape) for o in shapes[4:]]
+        + [
+            pl.BlockSpec((512, BQ), lambda i: (0, jnp.maximum(i - half, 0))),
+            pl.BlockSpec((H, BQ), lambda i: (0, jnp.maximum(i - half, 0))),
+        ],
+        out_shape=[jax.ShapeDtypeStruct((4, 2, 2, 2, LATE, 512), BF16)]
+        + shapes
+        + [jax.ShapeDtypeStruct((512, slots), BF16), jax.ShapeDtypeStruct((H, slots), F32)],
         scratch_shapes=[
             pltpu.VMEM((ROWS, 512), BF16),
             pltpu.VMEM((4, 2, 2, 2, EARLY, 512), BF16),
             pltpu.VMEM((512, 128), F32),
+            pltpu.VMEM(mwide, BF16),
+            pltpu.VMEM((H, HA, rb), BF16),
+            pltpu.VMEM(wide, BF16),
+            pltpu.VMEM(tall, BF16),
+            pltpu.VMEM(wide, BF16),
+            pltpu.VMEM((H, HA, BQ), F32),
+            pltpu.VMEM((H, BQ), F32),
+            pltpu.VMEM((H, BK, BQ), F32),
+            pltpu.VMEM((H, BK, BQ), F32),
             pltpu.SemaphoreType.DMA((GATHER_COPIES,)),
             pltpu.SemaphoreType.DMA((GATHER_COPIES,)),
             pltpu.SemaphoreType.DMA,
         ],
         compiler_params=params(collective_id=0, has_side_effects=True),
-        name="gather_projections",
+        name="gather_attend",
     )(*weights, *args)
     return (found[0].reshape(PARTS, LATE, 512),) + tuple(found[1:])
 
@@ -433,18 +483,7 @@
         work(None, (j, first))
 
 
-def fwd_kernel(
-    slots, seg_ref, cnt_ref, qa_ref, kn_ref, va_ref, kmn_ref, vm_ref,
-    mix_ref, lse_ref, acc_ref, m_ref, sa_ref, sb_ref, range_ref,
-):
-    step = pl.program_id(0)
-
-    @pl.when(step == 0)
-    def _():
-        key_ranges(seg_ref[...], cnt_ref[0], slots, range_ref)
-
-    begin, blocks = range_ref[0, step], range_ref[1, step]
-
+def attend(begin, blocks, qa_ref, kn_ref, va_ref, kmn_ref, vm_ref, mix_ref, lse_ref, acc_ref, m_ref, sa_ref, sb_ref):
     def weights(h, s):
         old = m_ref[h : h + 1, :]
         top = jnp.maximum(old, jnp.max(s, axis=0, keepdims=True))
@@ -473,6 +512,22 @@
         total = acc_ref[h, 64:65, :]
         mix_ref[64 * h : 64 * h + 64, :] = (acc_ref[h, 0:64, :] * (1.0 / total)).astype(BF16)
         lse_ref[h : h + 1, :] = m_ref[h : h + 1, :] + jnp.log(total)
+
+
+def fwd_kernel(
+    slots, seg_ref, cnt_ref, qa_ref, kn_ref, va_ref, kmn_ref, vm_ref,
+    mix_ref, lse_ref, acc_ref, m_ref, sa_ref, sb_ref, range_ref,
+):
+    step = pl.program_id(0)
+
+    @pl.when(step == 0)
+    def _():
+        key_ranges(seg_ref[...], cnt_ref[0], slots, range_ref)
+
+    attend(
+        range_ref[0, step], range_ref[1, step], qa_ref, kn_ref, va_ref, kmn_ref, vm_ref, mix_ref, lse_ref,
+        acc_ref, m_ref, sa_ref, sb_ref,
+    )
 
 
 def attend_forward(seg2, counts, qa, kn, va, kmn, vm):
@@ -524,12 +579,17 @@
     return jnp.sum(value, axis=0, keepdims=True)
 
 
+SUB = 256
+FC = 512
+
+
 def mid_kernel(
     rb, cnt_ref, row_ref, rbup_ref, late_ref, mix_ref, tok_ref, cot_ref,
     out_ref, gfirst_ref, mgrad_ref, delta_ref, gw_ref, vec_ref, bup_ref,
-    wup_ref, wdn_ref, aup_ref, adn_ref, ao_ref,
+    wup_ref, wdn_ref, aup_ref, adn_ref, ao_ref, *scratch,
 ):
     step = pl.program_id(0)
+    subs = rb // SUB
 
     @pl.when(step == 0)
     def _():
@@ -547,43 +607,112 @@
     def row(v):
         return row_ref[v : v + 1, :]
 
-    mixt = mix_ref[...]
-    attention = dot(mixt, wo, 0, 0) + row(V_BO)
-    hat1, rstd1 = norm_parts(tok_ref[...].astype(F32) + attention)
-    first = hat1 * row(V_GA) + row(V_SA)
-    first_low = first.astype(BF16)
-    hidden = dot(first_low, wup_ref[...], 1, 0) + rbup_ref[...]
-    cdf = 0.5 + 0.5 * lax.erf(hidden * (2.0 ** -0.5))
-    active = (hidden * cdf).astype(BF16)
-    slope = cdf + hidden * jnp.exp(hidden * hidden * -0.5) * 0.3989422804014327
-    branch = dot(active, wdn_ref[...], 1, 0) + row(V_BD)
-    hat2, rstd2 = norm_parts(first + branch)
-    valid = lax.broadcasted_iota(jnp.int32, (rb, 1), 0) + step * rb < cnt_ref[0]
-    out_ref[...] = jnp.where(valid, hat2 * row(V_GF) + row(V_SF), 0.0).astype(BF16)
-
-    seed = jnp.where(valid, cot_ref[...].astype(F32), 0.0)
-    vec_ref[V_GF : V_GF + 1, :] += colsum(seed * hat2)
-    vec_ref[V_SF : V_SF + 1, :] += colsum(seed)
-    grad_second = norm_grad(seed * row(V_GF), hat2, rstd2)
-    branch_grad = grad_second.astype(BF16)
-    adn_ref[...] += dot(active, branch_grad, 0, 0)
-    vec_ref[V_BD : V_BD + 1, :] += colsum(branch_grad.astype(F32))
-    hidden_grad = (dot(branch_grad, wdn_ref[...], 1, 1) * slope).astype(BF16)
-    aup_ref[...] += dot(first_low, hidden_grad, 0, 0)
-    bup_ref[...] += colsum(hidden_grad.astype(F32))
-    first_grad = grad_second + dot(hidden_grad, wup_ref[...], 1, 1)
-    vec_ref[V_GA : V_GA + 1, :] += colsum(first_grad * hat1)
-    vec_ref[V_SA : V_SA + 1, :] += colsum(first_grad)
-    grad_first = norm_grad(first_grad * row(V_GA), hat1, rstd1)
-    gfirst_ref[...] = grad_first
-    attention_grad = grad_first.astype(BF16)
-    vec_ref[V_BO : V_BO + 1, :] += colsum(attention_grad.astype(F32))
-    ao_ref[...] += dot(mixt, attention_grad, 1, 0)
-    mgrad = dot(wo, attention_grad, 1, 1).astype(BF16)
-    mgrad_ref[...] = mgrad
-    prod = mgrad.astype(F32) * mixt.astype(F32)
-    for h in range(H):
-        delta_ref[h : h + 1, :] = jnp.sum(prod[64 * h : 64 * h + 64, :], axis=0, keepdims=True)
+    class Block:
+        def __init__(self, index):
+            self.s = slice(SUB * index, SUB * index + SUB)
+            self.first_row = step * rb + SUB * index
+            self.active, self.slope, self.hgrad = scratch[3 * (index % 2) : 3 * (index % 2) + 3]
+            self.up_part, self.dact_part = {}, {}
+
+        def head(self):
+            self.mixt = mix_ref[:, self.s]
+            attention = dot(self.mixt, wo, 0, 0) + row(V_BO)
+            self.hat1, self.rstd1 = norm_parts(tok_ref[self.s, :].astype(F32) + attention)
+            self.first = self.hat1 * row(V_GA) + row(V_SA)
+            self.low = self.first.astype(BF16)
+            self.branch = self.first + row(V_BD)
+
+        def up(self, c):
+            f = slice(FC * c, FC * c + FC)
+            self.up_part[c] = dot(self.low, wup_ref[:, f], 1, 0) + rbup_ref[:, f]
+
+        def gelu(self, c):
+            f = slice(FC * c, FC * c + FC)
+            hidden = self.up_part.pop(c)
+            cdf = 0.5 + 0.5 * lax.erf(hidden * (2.0 ** -0.5))
+            self.active[:, f] = (hidden * cdf).astype(BF16)
+            self.slope[:, f] = cdf + hidden * jnp.exp(hidden * hidden * -0.5) * 0.3989422804014327
+
+        def down(self, c):
+            f = slice(FC * c, FC * c + FC)
+            self.branch = self.branch + dot(self.active[:, f], wdn_ref[f, :], 1, 0)
+
+        def turn(self):
+            hat2, rstd2 = norm_parts(self.branch)
+            valid = lax.broadcasted_iota(jnp.int32, (SUB, 1), 0) + self.first_row < cnt_ref[0]
+            out_ref[self.s, :] = jnp.where(valid, hat2 * row(V_GF) + row(V_SF), 0.0).astype(BF16)
+            seed = jnp.where(valid, cot_ref[self.s, :].astype(F32), 0.0)
+            vec_ref[V_GF : V_GF + 1, :] += colsum(seed * hat2)
+            vec_ref[V_SF : V_SF + 1, :] += colsum(seed)
+            self.total = norm_grad(seed * row(V_GF), hat2, rstd2)
+            self.bgrad = self.total.astype(BF16)
+            vec_ref[V_BD : V_BD + 1, :] += colsum(self.bgrad.astype(F32))
+
+        def dact(self, c):
+            f = slice(FC * c, FC * c + FC)
+            self.dact_part[c] = dot(self.bgrad, wdn_ref[f, :], 1, 1)
+
+        def grad_down(self, c):
+            f = slice(FC * c, FC * c + FC)
+            adn_ref[f, :] += dot(self.active[:, f], self.bgrad, 0, 0)
+
+        def hidden_grad(self, c):
+            f = slice(FC * c, FC * c + FC)
+            grad = (self.dact_part.pop(c) * self.slope[:, f]).astype(BF16)
+            self.hgrad[:, f] = grad
+            bup_ref[:, f] += colsum(grad.astype(F32))
+
+        def grad_up(self, c):
+            f = slice(FC * c, FC * c + FC)
+            aup_ref[:, f] += dot(self.low, self.hgrad[:, f], 0, 0)
+
+        def first_grad(self, c):
+            f = slice(FC * c, FC * c + FC)
+            self.total = self.total + dot(self.hgrad[:, f], wup_ref[:, f], 1, 1)
+
+        def finish(self):
+            vec_ref[V_GA : V_GA + 1, :] += colsum(self.total * self.hat1)
+            vec_ref[V_SA : V_SA + 1, :] += colsum(self.total)
+            grad_first = norm_grad(self.total * row(V_GA), self.hat1, self.rstd1)
+            gfirst_ref[self.s, :] = grad_first
+            agrad = grad_first.astype(BF16)
+            vec_ref[V_BO : V_BO + 1, :] += colsum(agrad.astype(F32))
+            mgrad = dot(wo, agrad, 1, 1).astype(BF16)
+            ao_ref[...] += dot(self.mixt, agrad, 1, 0)
+            mgrad_ref[:, self.s] = mgrad
+            prod = mgrad.astype(F32) * self.mixt.astype(F32)
+            for h in range(H):
+                delta_ref[h : h + 1, self.s] = jnp.sum(prod[64 * h : 64 * h + 64, :], axis=0, keepdims=True)
+
+    chunks = 2048 // FC
+
+    def both(ahead, behind):
+        if ahead:
+            ahead.head()
+            ahead.up(0)
+        for c in range(chunks):
+            if behind:
+                behind.dact(c)
+            if ahead and c + 1 < chunks:
+                ahead.up(c + 1)
+            if behind:
+                behind.grad_down(c)
+            if ahead:
+                ahead.gelu(c)
+            if behind:
+                behind.hidden_grad(c)
+                behind.grad_up(c)
+                behind.first_grad(c)
+            if ahead:
+                ahead.down(c)
+        if behind:
+            behind.finish()
+        if ahead:
+            ahead.turn()
+
+    blocks = [Block(index) for index in range(subs)]
+    for ahead, behind in zip(blocks + [None], [None] + blocks):
+        both(ahead, behind)
 
     @pl.when(step == pl.num_programs(0) - 1)
     def _():
@@ -595,7 +724,7 @@
         gw_ref[:, 80:144, :] = adn_ref[...].astype(gw_ref.dtype).reshape(PARTS, 64, 512)
 
 
-def middle(late, rows8, rbup, counts, mixt, tokens, cotangent, rb=256):
+def middle(late, rows8, rbup, counts, mixt, tokens, cotangent, rb=512):
     slots = tokens.shape[0]
     rows = pl.BlockSpec((rb, 512), lambda i: (i, 0))
     cols = pl.BlockSpec((512, rb), lambda i: (0, i))
@@ -632,7 +761,8 @@
             pltpu.VMEM((512, 2048), F32),
             pltpu.VMEM((2048, 512), F32),
             pltpu.VMEM((512, 512), F32),
-        ],
+        ]
+        + [pltpu.VMEM((SUB, 2048), BF16), pltpu.VMEM((SUB, 2048), F32), pltpu.VMEM((SUB, 2048), BF16)] * 2,
         compiler_params=params(),
         name="middle",
     )(counts, rows8, rbup, late, mixt, tokens, cotangent)
@@ -913,9 +1043,6 @@
     slots = tokens.shape[0]
     rb = 512
     half = slots // rb
-
-    def fixed(*shape):
-        return pl.BlockSpec(shape, lambda i: (0,) * len(shape))
 
     cols = pl.BlockSpec((512, rb), lambda i: (0, i % half))
     later = pl.BlockSpec((rb, 512), lambda i: (jnp.maximum(i - half, 0), 0))
@@ -959,7 +1086,7 @@
     )(*args, early.reshape(4, 2, 2, 2, LATE, 512))
 
 
-def unpack_kernel(sum_ref, wo, up, dn, wq, wk, wv, memory, vectors, b_up):
+def unpack_kernel(sum_ref, wo, up, dn, wq, wk, wv, memory, b_up, *vectors):
     me = lax.axis_index("dp")
     wo[...] = sum_ref[0:16]
     for c in range(4):
@@ -968,8 +1095,10 @@
     wq[...] = sum_ref[144:160]
     wk[...] = sum_ref[160:176]
     wv[...] = sum_ref[176:192]
-    memory[...] = sum_ref[192:208, 0:128].T[0 : memory.shape[0], :]
-    vectors[...] = sum_ref[192:208, 128:256].T[0:8, :]
+    memory[...] = sum_ref[192:208, 0 : memory.shape[1]]
+    turned = sum_ref[192:208, 128:256].T
+    for index, vector in enumerate(vectors):
+        vector[...] = turned[index : index + 1, :]
     row = lax.broadcasted_iota(jnp.int32, (16, 256), 0)
     lane = lax.broadcasted_iota(jnp.int32, (16, 256), 1)
     own = jnp.sum(jnp.where(row * 4 + lane // 64 == me, sum_ref[192:208, 256:512], 0.0), axis=0, keepdims=True)
@@ -977,7 +1106,7 @@
 
 
 def unpack(sums, mem_rows):
-    shapes = [(16, 512), (16, 2048), (64, 512), (16, 512), (16, 512), (16, 512), (mem_rows, 16), (8, 16), (1, 64)]
+    shapes = [(16, 512), (16, 2048), (64, 512), (16, 512), (16, 512), (16, 512), (16, mem_rows), (1, 64)] + [(1, 16)] * 8
     found = pl.pallas_call(
         unpack_kernel,
         out_shape=[jax.ShapeDtypeStruct(s, F32) for s in shapes],
@@ -985,9 +1114,10 @@
         name="unpack",
     )(sums)
     out = dict(zip(("w_out", "w_up", "w_down", "w_query", "w_key", "w_value", "memory"), found[:7]))
-    for index, name in enumerate(VECTORS):
-        out[name] = found[7][index]
-    out["b_up"] = found[8].reshape(64)
+    out["memory"] = out["memory"].T
+    out["b_up"] = found[7].reshape(64)
+    for name, value in zip(VECTORS, found[8:]):
+        out[name] = value.reshape(16)
     return out
 
 
@@ -1042,9 +1172,8 @@
     if n != PARTS:
         whole = pack_whole({k: lax.all_gather(v, "dp", axis=axis_of(k), tiled=True) for k, v in p.items()})
     found = projections(p, whole, tokens, segment, counts, mem_rows)
-    late, qa, ka, va, kn, vn, km, vm, kmn, vmn, wt, memt, rows8, rbup = found
+    late, qa, ka, kn, vn, km, kmn, vmn, wt, memt, rows8, rbup, mixt, lse = found
     seg2 = segment.reshape(slots // 128, 128)
-    mixt, lse = attend_forward(seg2, counts, qa, kn, va, kmn, vm)
     output, gfirst, mgrad, delta, early, vec, bup = middle(late, rows8, rbup, counts, mixt, tokens, cotangent)
     dq, dk, dv, dkm, dvm = attend_backward(seg2, counts, qa, kn, ka, vn, kmn, km, vmn, mgrad, lse, delta)
     gtok, sums = tail(early, tokens, dq, dk, dv, dkm, dvm, gfirst, vec, bup, wt, memt, n == PARTS)

time: 261 us -> 241 us (0.923)
  Pallas kernels: 248 us -> 235 us
  local copies, waits for them, and re-layouts: 10.3 us -> 4.64 us
    pallas_call x1, Pallas kernels: 47.8 us -> 61.5 us  [tail(): pl.pallas_call(functools.partial(scatter_kernel, half), grid=(2 * half,),...]
    pallas_call x1, Pallas kernels: 59.7 us -> 46.6 us  [attend_backward(): pl.pallas_call(functools.partial(bwd_kernel, slots), grid=(slots // BQ,),...]
    pallas_call x2 -> x1, Pallas kernels: 87.3 us -> 77.6 us  [projections(): pl.pallas_call(functools.partial(gather_kernel, mem_rows, half), grid=(ha...]
    pallas_call x1, Pallas kernels: 51.1 us -> 47.3 us  [middle(): pl.pallas_call(functools.partial(mid_kernel, rb), grid=(slots // rb,), in...]
    unnamed x3 -> x1, local copies, waits for them, and re-layouts: 7.38 us -> 4.64 us
where the time goes in v5:
time: 241 us
  Pallas kernels  235 us (98%)
  local copies, waits for them, and re-layouts  4.64 us (2%)
    pallas_call x1, Pallas kernels, projections(): pl.pallas_call(functools.partial(gather_kernel, mem_rows, half), grid=(ha...  77.6 us
    pallas_call x1, Pallas kernels, tail(): pl.pallas_call(functools.partial(scatter_kernel, half), grid=(2 * half,),...  61.5 us
    pallas_call x1, Pallas kernels, middle(): pl.pallas_call(functools.partial(mid_kernel, rb), grid=(slots // rb,), in...  47.3 us
    pallas_call x1, Pallas kernels, attend_backward(): pl.pallas_call(functools.partial(bwd_kernel, slots), grid=(slots // BQ,),...  46.6 us

profile of v5, /device:TPU:0, one launch (start us, length us, event | category | flops | bytes accessed | tf_op | source)
XLA Modules:
  0.0 240.8 jit_solution(1154133359928289186)
XLA Ops:
  1.3 77.6 %gather_attend.1 = (bf16[4,2,2,2,144,512]{5,4,3,2,1,0:T(8,128)(2,1)}, bf16[8,80,2048]{2,1,0:T(8,128)(2,1)}, bf16[8,80,2048]{2,1,0:T(8,128)(2,1)}, bf16[8,2048,12...) custom-call(bf16[16,512]{1,0:T(8,128)(2,1)} %wq.1, ...), custom_call_target="tpu_custom_call" | custom-call | tf_op jit(solution)/shard_map/gather_attend/pallas_call | solution.py:402
  78.9 47.3 %middle.1 = (bf16[2048,512]{1,0:T(8,128)(2,1)}, f32[2048,512]{1,0:T(8,128)}, bf16[512,2048]{1,0:T(8,128)(2,1)}, f32[8,2048]{1,0:T(8,128)}, bf16[32,144,512]{2,1,...) custom-call(s32[1]{0:T(128)S(6)} %copy.39.cnt_ref, f32[8,512]{1,0:T(8,128)} %get-tuple-element.62.row_ref, ...), custom_call_target="tpu_custom_call" | custom-call | tf_op jit(solution)/shard_map/middle/pallas_call | solution.py:732
  126.2 46.6 %attend_backward.1 = (bf16[512,2048]{1,0:T(8,128)(2,1)}, bf16[512,2048]{1,0:T(8,128)(2,1)}, bf16[512,2048]{1,0:T(8,128)(2,1)}, bf16[512,128]{1,0:T(8,128)(2,1)}, bf16[512,128]{1,0:T(8,128)(2,1)}) custom-call(s32[16,128]{1,0:T(8,128)} %bitcast.27, s32[1]{0:T(128)S(6)} %copy.39.cnt_ref, bf16[8,80,2048]{2,1,0:T(8,128)(2,1)} %get-tuple-element.67.qa_ref, ...), custom_call_target="tpu_custom_call" | custom-call | tf_op jit(solution)/shard_map/attend_backward/pallas_call | solution.py:855
  172.8 61.5 %tail_scatter.1 = (f32[2048,512]{1,0:T(8,128)}, f32[208,512]{1,0:T(8,128)}) custom-call(bf16[2048,512]{1,0:T(8,128)(2,1)} %tok_ref.5, bf16[512,2048]{1,0:T(8,128)(2,1)} %get-tuple-element.77.dq_ref, bf16[512,2048]{1,0:T(8,128)(2,1)} %get-tuple-element.78.dk_ref, bf16[512,2048]{1,0:T(8,128)(2,1)} %get-tuple-element.79.dv_ref, ...), custom_call_target="tpu_custom_call" | custom-call | tf_op jit(solution)/shard_map/tail_scatter/pallas_call | solution.py:1068
  234.4 1.8 unpack.1
  236.2 4.6 %copy.40 = f32[2048,512]{1,0:T(8,128)} copy(f32[2048,512]{1,0:T(8,128)} %get-tuple-element.125) | data formatting | bytes 8388608

commit v6 on v5

--- a/solution.py
+++ b/solution.py
@@ -51,18 +51,19 @@
             for distance in range(1, length):
                 j = (self.at[axis] + distance) % length
                 self.others[axis, distance] = j, me + (j - self.at[axis]) * stride
+        self.peers = [self.partner] + [device for _, device in self.others.values()]
 
     def other(self, axis, distance):
         return self.others[axis, distance]
 
     def greet(self):
-        barrier = pltpu.get_barrier_semaphore()
-        peers = [self.partner]
-        for axis in LAYOUT:
-            peers += [self.other(axis, d)[1] for d in range(1, AXES[axis][1])]
-        for peer in peers:
-            pl.semaphore_signal(barrier, inc=1, device_id=(peer,), device_id_type=MESH)
-        return lambda: pl.semaphore_wait(barrier, len(peers))
+        for peer in self.peers:
+            pl.semaphore_signal(
+                pltpu.get_barrier_semaphore(), inc=1, device_id=(peer,), device_id_type=MESH
+            )
+
+    def met(self):
+        pl.semaphore_wait(pltpu.get_barrier_semaphore(), len(self.peers))
 
 
 class Copies:
@@ -246,7 +247,7 @@
         vmn_ref[h] = turned[0:MP]
 
 
-def project(step, tok_ref, seg_ref, cnt_ref, wt_ref, bias_ref, qa_ref, ka_ref, va_ref, kn_ref, vn_ref):
+def project(step, tok_ref, seg_ref, cnt_ref, wt_ref, bias_ref, qa_ref, ka_ref, va_ref):
     rows = tok_ref.shape[0]
     tok = tok_ref[...]
     bq = bias_ref[:, V_BQ : V_BQ + 1]
@@ -265,18 +266,20 @@
         s = slice(64 * h, 64 * h + 64)
         qa_ref[h, 0:64, :] = q[s]
         qa_ref[h, 64:80, :] = qf
-        ka_ref[h], kn_ref[h] = head_block(k[s], kf)
-        va_ref[h], vn_ref[h] = head_block(v[s], vf)
+        ka_ref[h, 0:64, :] = k[s]
+        ka_ref[h, 64:80, :] = kf
+        va_ref[h, 0:64, :] = v[s]
+        va_ref[h, 64:80, :] = vf
 
 
 def gather_kernel(
     mem_rows, half, wq, wk, wv, wo, up, dn, memory, b_up, v0, v1, v2, v3, v4, v5, v6, v7, tok_ref, seg_ref, cnt_ref,
-    late_ref, qa_ref, ka_ref, kn_ref, vn_ref, km_ref, kmn_ref, vmn_ref,
+    late_ref, qa_ref, ka_ref, va_ref, km_ref, kmn_ref, vmn_ref,
     wt_ref, memt_ref, rows_ref, rbup_ref, mix_ref, lse_ref,
-    own, early, bias_ref, vm_ref, va_block, qa_all, kn_all, va_all, acc_ref, m_ref, sa_ref, sb_ref, send, recv, local,
+    own, early, bias_ref, vm_ref, qa_all, ka_all, va_all, acc_ref, m_ref, sa_ref, sb_ref, send, recv, local,
 ):
     step = pl.program_id(0)
-    slots = kn_all.shape[1]
+    slots = ka_all.shape[2]
     place = Place()
     copies = Copies(send, recv)
     arrivals, late_arrivals = [], []
@@ -285,10 +288,10 @@
 
     @pl.when(step == 0)
     def _():
-        everyone = place.greet()
+        place.greet()
         pack(own, place, wq, wk, wv, wo, up, dn, memory, b_up, (v0, v1, v2, v3, v4, v5, v6, v7))
         early[place.mine + (place.core,)] = own[0:EARLY]
-        everyone()
+        place.met()
         advance(firsts)
         keep = pltpu.make_async_copy(own.at[EARLY:ROWS], late_ref.at[place.mine + (place.core,)], local)
         keep.start()
@@ -305,11 +308,11 @@
 
     @pl.when(step < half)
     def _():
-        project(step, tok_ref, seg_ref, cnt_ref, wt_ref, bias_ref, qa_ref, ka_ref, va_block, kn_ref, vn_ref)
+        project(step, tok_ref, seg_ref, cnt_ref, wt_ref, bias_ref, qa_ref, ka_ref, va_ref)
         here = pl.ds(pl.multiple_of(step * tok_ref.shape[0], 128), tok_ref.shape[0])
         qa_all[:, :, here] = qa_ref[...]
-        va_all[:, :, here] = va_block[...]
-        kn_all[:, here, :] = kn_ref[...]
+        ka_all[:, :, here] = ka_ref[...]
+        va_all[:, :, here] = va_ref[...]
 
     @pl.when(step == half - 1)
     def _():
@@ -323,7 +326,7 @@
         end = jnp.minimum(block + reach + 1, slots // BQ)
         queries = qa_all.at[:, :, pl.ds(pl.multiple_of(block * BQ, BQ), BQ)]
         attend(
-            begin * (BQ // 128), (end - begin) * (BQ // BK), queries, kn_all, va_all, kmn_ref, vm_ref, mix_ref, lse_ref,
+            begin * (BQ // 128), (end - begin) * (BQ // BK), queries, ka_all, va_all, kmn_ref, vm_ref, mix_ref, lse_ref,
             acc_ref, m_ref, sa_ref, sb_ref,
         )
 
@@ -340,7 +343,7 @@
 
 
 def project_kernel(
-    mem_rows, g_ref, tok_ref, seg_ref, cnt_ref, qa_ref, ka_ref, va_ref, kn_ref, vn_ref, km_ref, vm_ref, kmn_ref, vmn_ref,
+    mem_rows, g_ref, tok_ref, seg_ref, cnt_ref, qa_ref, ka_ref, va_ref, km_ref, vm_ref, kmn_ref, vmn_ref,
     wt_ref, memt_ref, rows_ref, rbup_ref, bias_ref,
 ):
     step = pl.program_id(0)
@@ -351,7 +354,7 @@
             mem_rows, g_ref, wt_ref, memt_ref, rows_ref, rbup_ref, bias_ref, km_ref, vm_ref, kmn_ref, vmn_ref
         )
 
-    project(step, tok_ref, seg_ref, cnt_ref, wt_ref, bias_ref, qa_ref, ka_ref, va_ref, kn_ref, vn_ref)
+    project(step, tok_ref, seg_ref, cnt_ref, wt_ref, bias_ref, qa_ref, ka_ref, va_ref)
 
 
 def fixed(*shape):
@@ -362,14 +365,13 @@
     slots = tokens.shape[0]
     rb = 512
     half = slots // rb
-    wide, tall = (H, HA, slots), (H, slots, 128)
+    wide = (H, HA, slots)
     mwide, mtall = (H, HA, 128), (H, MP, 128)
 
     def at(i):
         return jnp.minimum(i, half - 1)
 
     blk = pl.BlockSpec((H, HA, rb), lambda i: (0, 0, at(i)))
-    tblk = pl.BlockSpec((H, rb, 128), lambda i: (0, at(i), 0))
     common = [
         pl.BlockSpec((rb, 512), lambda i: (at(i), 0)),
         pl.BlockSpec((1, rb), lambda i: (0, at(i))),
@@ -382,29 +384,29 @@
         return found + [jax.ShapeDtypeStruct((8, 512), F32), jax.ShapeDtypeStruct((1, 2048), F32)]
 
     if whole is not None:
-        shapes = outs([wide, wide, wide, tall, tall, mwide, mwide, mtall, mtall, (1536, 512), (512, 128)])
+        shapes = outs([wide, wide, wide, mwide, mwide, mtall, mtall, (1536, 512), (512, 128)])
         found = pl.pallas_call(
             functools.partial(project_kernel, mem_rows),
             grid=(half,),
             in_specs=[fixed(PARTS, EARLY, 512)] + common,
-            out_specs=[blk, blk, blk, tblk, tblk] + [fixed(*o.shape) for o in shapes[5:]],
+            out_specs=[blk, blk, blk] + [fixed(*o.shape) for o in shapes[3:]],
             out_shape=shapes,
             scratch_shapes=[pltpu.VMEM((512, 128), F32)],
             compiler_params=params(),
             name="projections",
         )(whole[:, 0:EARLY], *args)
-        qa, ka, va, kn, vn, km, vm, kmn, vmn, wt, memt, rows8, rbup = found
-        mixt, lse = attend_forward(segment.reshape(slots // 128, 128), counts, qa, kn, va, kmn, vm)
-        return whole[:, EARLY:], qa, ka, kn, vn, km, kmn, vmn, wt, memt, rows8, rbup, mixt, lse
+        qa, ka, va, km, vm, kmn, vmn, wt, memt, rows8, rbup = found
+        mixt, lse = attend_forward(segment.reshape(slots // 128, 128), counts, qa, ka, va, kmn, vm)
+        return whole[:, EARLY:], qa, ka, va, km, kmn, vmn, wt, memt, rows8, rbup, mixt, lse
     weights = [p[name] for name in ("w_query", "w_key", "w_value", "w_out", "w_up", "w_down")]
     weights += [p["memory"].T, p["b_up"].reshape(1, 64)] + [p[name].reshape(1, 16) for name in VECTORS]
-    shapes = outs([wide, wide, tall, tall, mwide, mtall, mtall, (1536, 512), (512, 128)])
+    shapes = outs([wide, wide, wide, mwide, mtall, mtall, (1536, 512), (512, 128)])
     found = pl.pallas_call(
         functools.partial(gather_kernel, mem_rows, half),
         grid=(half + slots // BQ,),
         in_specs=[fixed(*w.shape) for w in weights] + common,
-        out_specs=[pl.BlockSpec(memory_space=pl.ANY), blk, blk, tblk, tblk]
-        + [fixed(*o.shape) for o in shapes[4:]]
+        out_specs=[pl.BlockSpec(memory_space=pl.ANY), blk, blk, blk]
+        + [fixed(*o.shape) for o in shapes[3:]]
         + [
             pl.BlockSpec((512, BQ), lambda i: (0, jnp.maximum(i - half, 0))),
             pl.BlockSpec((H, BQ), lambda i: (0, jnp.maximum(i - half, 0))),
@@ -417,9 +419,8 @@
             pltpu.VMEM((4, 2, 2, 2, EARLY, 512), BF16),
             pltpu.VMEM((512, 128), F32),
             pltpu.VMEM(mwide, BF16),
-            pltpu.VMEM((H, HA, rb), BF16),
             pltpu.VMEM(wide, BF16),
-            pltpu.VMEM(tall, BF16),
+            pltpu.VMEM(wide, BF16),
             pltpu.VMEM(wide, BF16),
             pltpu.VMEM((H, HA, BQ), F32),
             pltpu.VMEM((H, BQ), F32),
@@ -483,7 +484,7 @@
         work(None, (j, first))
 
 
-def attend(begin, blocks, qa_ref, kn_ref, va_ref, kmn_ref, vm_ref, mix_ref, lse_ref, acc_ref, m_ref, sa_ref, sb_ref):
+def attend(begin, blocks, qa_ref, ka_ref, va_ref, kmn_ref, vm_ref, mix_ref, lse_ref, acc_ref, m_ref, sa_ref, sb_ref):
     def weights(h, s):
         old = m_ref[h : h + 1, :]
         top = jnp.maximum(old, jnp.max(s, axis=0, keepdims=True))
@@ -493,7 +494,7 @@
         kept = {}
         for h in range(H + 1):
             if h < H and new:
-                new[1][h] = dot(kn_ref[h, key_slots(begin, new[0]), 0:HA], qa_ref[h], 1, 0)
+                new[1][h] = dot(ka_ref[h, :, key_slots(begin, new[0])], qa_ref[h], 0, 0)
             if h < H and old:
                 kept[h] = weights(h, old[1][h])
             if h > 0 and old:
@@ -515,7 +516,7 @@
 
 
 def fwd_kernel(
-    slots, seg_ref, cnt_ref, qa_ref, kn_ref, va_ref, kmn_ref, vm_ref,
+    slots, seg_ref, cnt_ref, qa_ref, ka_ref, va_ref, kmn_ref, vm_ref,
     mix_ref, lse_ref, acc_ref, m_ref, sa_ref, sb_ref, range_ref,
 ):
     step = pl.program_id(0)
@@ -525,12 +526,12 @@
         key_ranges(seg_ref[...], cnt_ref[0], slots, range_ref)
 
     attend(
-        range_ref[0, step], range_ref[1, step], qa_ref, kn_ref, va_ref, kmn_ref, vm_ref, mix_ref, lse_ref,
+        range_ref[0, step], range_ref[1, step], qa_ref, ka_ref, va_ref, kmn_ref, vm_ref, mix_ref, lse_ref,
         acc_ref, m_ref, sa_ref, sb_ref,
     )
 
 
-def attend_forward(seg2, counts, qa, kn, va, kmn, vm):
+def attend_forward(seg2, counts, qa, ka, va, kmn, vm):
     slots = qa.shape[2]
     once = pl.Buffered(1)
 
@@ -544,7 +545,7 @@
             pl.BlockSpec(seg2.shape, lambda i: (0, 0)),
             pl.BlockSpec(memory_space=pltpu.SMEM),
             pl.BlockSpec((H, HA, BQ), lambda i: (0, 0, i)),
-            whole(kn), whole(va), whole(kmn), whole(vm),
+            whole(ka), whole(va), whole(kmn), whole(vm),
         ],
         out_specs=[pl.BlockSpec((512, BQ), lambda i: (0, i)), pl.BlockSpec((H, BQ), lambda i: (0, i))],
         out_shape=[jax.ShapeDtypeStruct((512, slots), BF16), jax.ShapeDtypeStruct((H, slots), F32)],
@@ -557,7 +558,7 @@
         ],
         compiler_params=params(),
         name="attend_forward",
-    )(seg2, counts, qa, kn, va, kmn, vm)
+    )(seg2, counts, qa, ka, va, kmn, vm)
 
 
 def norm_parts(value):
@@ -579,23 +580,20 @@
     return jnp.sum(value, axis=0, keepdims=True)
 
 
-SUB = 256
+SUB = 512
 FC = 512
 
 
 def mid_kernel(
     rb, cnt_ref, row_ref, rbup_ref, late_ref, mix_ref, tok_ref, cot_ref,
     out_ref, gfirst_ref, mgrad_ref, delta_ref, gw_ref, vec_ref, bup_ref,
-    wup_ref, wdn_ref, aup_ref, adn_ref, ao_ref, *scratch,
+    aup_ref, adn_ref, ao_ref, *scratch,
 ):
     step = pl.program_id(0)
     subs = rb // SUB
 
     @pl.when(step == 0)
     def _():
-        for c in range(4):
-            wup_ref[:, 512 * c : 512 * c + 512] = late_ref[:, 16 * c : 16 * c + 16, :].reshape(512, 512)
-        wdn_ref[...] = late_ref[:, 64:128, :].reshape(2048, 512)
         aup_ref[...] = jnp.zeros_like(aup_ref)
         adn_ref[...] = jnp.zeros_like(adn_ref)
         ao_ref[...] = jnp.zeros_like(ao_ref)
@@ -603,6 +601,12 @@
         bup_ref[...] = jnp.zeros_like(bup_ref)
 
     wo = late_ref[:, 128:144, :].reshape(512, 512)
+
+    def w_up(c):
+        return late_ref[:, 16 * c : 16 * c + 16, :].reshape(512, 512)
+
+    def w_down(c):
+        return late_ref[8 * c : 8 * c + 8, 64:128, :].reshape(512, 512)
 
     def row(v):
         return row_ref[v : v + 1, :]
@@ -624,7 +628,7 @@
 
         def up(self, c):
             f = slice(FC * c, FC * c + FC)
-            self.up_part[c] = dot(self.low, wup_ref[:, f], 1, 0) + rbup_ref[:, f]
+            self.up_part[c] = dot(self.low, w_up(c), 1, 0) + rbup_ref[:, f]
 
         def gelu(self, c):
             f = slice(FC * c, FC * c + FC)
@@ -635,7 +639,7 @@
 
         def down(self, c):
             f = slice(FC * c, FC * c + FC)
-            self.branch = self.branch + dot(self.active[:, f], wdn_ref[f, :], 1, 0)
+            self.branch = self.branch + dot(self.active[:, f], w_down(c), 1, 0)
 
         def turn(self):
             hat2, rstd2 = norm_parts(self.branch)
@@ -650,7 +654,7 @@
 
         def dact(self, c):
             f = slice(FC * c, FC * c + FC)
-            self.dact_part[c] = dot(self.bgrad, wdn_ref[f, :], 1, 1)
+            self.dact_part[c] = dot(self.bgrad, w_down(c), 1, 1)
 
         def grad_down(self, c):
             f = slice(FC * c, FC * c + FC)
@@ -668,7 +672,7 @@
 
         def first_grad(self, c):
             f = slice(FC * c, FC * c + FC)
-            self.total = self.total + dot(self.hgrad[:, f], wup_ref[:, f], 1, 1)
+            self.total = self.total + dot(self.hgrad[:, f], w_up(c), 1, 1)
 
         def finish(self):
             vec_ref[V_GA : V_GA + 1, :] += colsum(self.total * self.hat1)
@@ -756,8 +760,6 @@
             jax.ShapeDtypeStruct((1, 2048), F32),
         ],
         scratch_shapes=[
-            pltpu.VMEM((512, 2048), BF16),
-            pltpu.VMEM((2048, 512), BF16),
             pltpu.VMEM((512, 2048), F32),
             pltpu.VMEM((2048, 512), F32),
             pltpu.VMEM((512, 512), F32),
@@ -775,22 +777,10 @@
     return high, mid, (rest - mid.astype(F32)).astype(BF16)
 
 
-def bwd_kernel(
-    slots, seg_ref, cnt_ref, qa_ref, kn_ref, ka_ref, vn_ref, kmn_ref, km_ref, vmn_ref, do_ref, lse_ref, delta_ref,
-    dq_ref, dk_ref, dv_ref, dkm_ref, dvm_ref,
-    q2_ref, do2_ref, dqa_ref, dka_ref, dva_ref, dkma_ref, dvma_ref, sa_ref, ga_ref, sb_ref, gb_ref, range_ref,
+def attend_back(
+    begin, blocks, qa_ref, ka_ref, va_ref, kmn_ref, km_ref, vmn_ref, do_ref, lse_ref, delta_ref,
+    q2_ref, do2_ref, dqa_ref, dka_ref, dva_ref, dkma_ref, dvma_ref, sa_ref, ga_ref, sb_ref, gb_ref,
 ):
-    step = pl.program_id(0)
-
-    @pl.when(step == 0)
-    def _():
-        key_ranges(seg_ref[...], cnt_ref[0], slots, range_ref)
-        dka_ref[...] = jnp.zeros_like(dka_ref)
-        dva_ref[...] = jnp.zeros_like(dva_ref)
-        dkma_ref[...] = jnp.zeros_like(dkma_ref)
-        dvma_ref[...] = jnp.zeros_like(dvma_ref)
-
-    begin, blocks = range_ref[0, step], range_ref[1, step]
     frow = lax.broadcasted_iota(jnp.int32, (16, BQ), 0)
 
     def feature(value, at):
@@ -808,8 +798,8 @@
         for h in range(H + 1):
             if h < H and new:
                 ks = key_slots(begin, new[0])
-                new[1][0][h] = dot(kn_ref[h, ks, 0:HA], q2_ref[h], 1, 0)
-                new[1][1][h] = dot(vn_ref[h, ks, 0:HA], do2_ref[h], 1, 0)
+                new[1][0][h] = dot(ka_ref[h, :, ks], q2_ref[h], 0, 0)
+                new[1][1][h] = dot(va_ref[h, :, ks], do2_ref[h], 0, 0)
             if h < H and old:
                 p = jnp.exp(old[1][0][h])
                 kept[h] = p.astype(BF16), (p * old[1][1][h]).astype(BF16)
@@ -827,6 +817,25 @@
         dkma_ref[h, :, 0:MP] += dot(q2_ref[h, 0:64, :], dss[h], 1, 1)
         dqa_ref[h] = dot(km_ref[h, 0:64, 0:MP], dss[h], 1, 0)
     pipelined(blocks, work, (sa_ref, ga_ref), (sb_ref, gb_ref))
+
+
+def bwd_kernel(
+    slots, seg_ref, cnt_ref, qa_ref, ka_ref, va_ref, kmn_ref, km_ref, vmn_ref, do_ref, lse_ref, delta_ref,
+    dq_ref, dk_ref, dv_ref, dkm_ref, dvm_ref,
+    q2_ref, do2_ref, dqa_ref, dka_ref, dva_ref, dkma_ref, dvma_ref, sa_ref, ga_ref, sb_ref, gb_ref, range_ref,
+):
+    step = pl.program_id(0)
+
+    @pl.when(step == 0)
+    def _():
+        key_ranges(seg_ref[...], cnt_ref[0], slots, range_ref)
+        for ref in (dka_ref, dva_ref, dkma_ref, dvma_ref):
+            ref[...] = jnp.zeros_like(ref)
+
+    attend_back(
+        range_ref[0, step], range_ref[1, step], qa_ref, ka_ref, va_ref, kmn_ref, km_ref, vmn_ref, do_ref, lse_ref,
+        delta_ref, q2_ref, do2_ref, dqa_ref, dka_ref, dva_ref, dkma_ref, dvma_ref, sa_ref, ga_ref, sb_ref, gb_ref,
+    )
     for h in range(H):
         dq_ref[64 * h : 64 * h + 64, :] = (dqa_ref[h] * HD ** -0.5).astype(BF16)
 
@@ -840,7 +849,7 @@
             dvm_ref[s, :] = dvma_ref[h].astype(BF16)
 
 
-def attend_backward(seg2, counts, qa, kn, ka, vn, kmn, km, vmn, mgrad, lse, delta):
+def attend_backward(seg2, counts, qa, ka, va, kmn, km, vmn, mgrad, lse, delta):
     slots = qa.shape[2]
     once = pl.Buffered(1)
 
@@ -859,7 +868,7 @@
             pl.BlockSpec(seg2.shape, lambda i: (0, 0)),
             pl.BlockSpec(memory_space=pltpu.SMEM),
             pl.BlockSpec((H, HA, BQ), lambda i: (0, 0, i)),
-            full(kn), full(ka), full(vn), full(kmn), full(km), full(vmn), cols, stat, stat,
+            full(ka), full(va), full(kmn), full(km), full(vmn), cols, stat, stat,
         ],
         out_specs=[cols, whole, whole, mwhole, mwhole],
         out_shape=[jax.ShapeDtypeStruct((512, slots), BF16)] * 3 + [jax.ShapeDtypeStruct((512, 128), BF16)] * 2,
@@ -876,7 +885,7 @@
         ],
         compiler_params=params(),
         name="attend_backward",
-    )(seg2, counts, qa, kn, ka, vn, kmn, km, vmn, mgrad, lse, delta)
+    )(seg2, counts, qa, ka, va, kmn, km, vmn, mgrad, lse, delta)
 
 
 SUM_EARLY = (
@@ -885,7 +894,7 @@
     (slice(96, 112), "xzy"),
     (slice(112, 144), "yzx"),
 )
-SUM_LATE = ((slice(144, 176), "xyz"), (slice(176, 208), "yxz"))
+SUM_LATE = ((slice(144, 160), "xyz"), (slice(160, 176), "yxz"), (slice(176, 192), "xyz"), (slice(192, 208), "yxz"))
 SUM_PARTS = SUM_EARLY + SUM_LATE
 SUM_COPIES = 6 * len(SUM_PARTS)
 
@@ -931,8 +940,11 @@
 
 
 def scatter_kernel(
-    half, tok_ref, dq_ref, dk_ref, dv_ref, dkm_ref, dvm_ref, gfirst_ref, vec_ref, bup_ref, wt_ref, memt_ref, early_ref,
-    gtok_ref, out_ref, acc_ref, sum_ref, late, parts_sum, other, send, recv, local, *landing,
+    blocks, qa_ref, ka_ref, va_ref, kmn_ref, km_ref, vmn_ref, do_ref, lse_ref, delta_ref,
+    tok_ref, gfirst_ref, vec_ref, bup_ref, wt_ref, memt_ref, early_ref, gtok_ref, out_ref,
+    q2_ref, do2_ref, dqa_ref, dka_ref, dva_ref, dkma_ref, dvma_ref, sa_ref, ga_ref, sb_ref, gb_ref,
+    dq_ref, dk_ref, dv_ref, dkm_ref, dvm_ref,
+    acc_ref, sum_ref, late, parts_sum, other, send, recv, local, *landing,
 ):
     step = pl.program_id(0)
     place = Place()
@@ -959,39 +971,84 @@
 
     @pl.when(step == 0)
     def _():
-        everyone = place.greet()
+        place.greet()
         for index in range(len(SUM_EARLY)):
             load(index).start()
-        everyone()
+        for ref in (dka_ref, dva_ref, dkma_ref, dvma_ref, sum_ref):
+            ref[...] = jnp.zeros_like(ref)
+        acc_ref[0:512, :] = jnp.zeros((512, 512), F32)
+
+    @pl.when(step < blocks)
+    def _():
+        reach = LONGEST // BQ
+        begin = jnp.maximum(step - reach, 0)
+        end = jnp.minimum(step + reach + 1, blocks)
+        attend_back(
+            begin * (BQ // 128), (end - begin) * (BQ // BK), qa_ref, ka_ref, va_ref, kmn_ref, km_ref, vmn_ref,
+            do_ref, lse_ref, delta_ref, q2_ref, do2_ref, dqa_ref, dka_ref, dva_ref, dkma_ref, dvma_ref,
+            sa_ref, ga_ref, sb_ref, gb_ref,
+        )
+        here = pl.ds(pl.multiple_of(step * BQ, BQ), BQ)
+        for h in range(H):
+            dq_ref[64 * h : 64 * h + 64, here] = (dqa_ref[h] * HD ** -0.5).astype(BF16)
+        dq = dq_ref[:, here]
+        acc_ref[0:512, :] += dot(dq, tok_ref[here, :], 1, 0)
+        sum_ref[:, 0:1] += jnp.sum(dq.astype(F32), axis=1, keepdims=True)
+
+    @pl.when(step == 0)
+    def _():
+        place.met()
         for number, (rows, _) in zip(crossing, SUM_EARLY):
             cross(early_ref, 0, rows, number)
 
-    @pl.when(step == 2)
+    @pl.when(step == 1)
     def _():
         for index, (rows, _) in enumerate(SUM_EARLY):
             load(index).wait()
             join(place, copies, parts_sum, None, other, rows, crossing[index])
             next(firsts[index])
 
-    @pl.when(step < half)
-    def _():
-        weight_grads(step, tok_ref, dq_ref, dk_ref, dv_ref, dkm_ref, dvm_ref, memt_ref, acc_ref, sum_ref)
-
-    @pl.when(step == half - 1)
-    def _():
+    @pl.when(step == 3)
+    def _():
+        advance(firsts)
+
+    @pl.when(step == 5)
+    def _():
+        advance(firsts)
+
+    @pl.when(step == blocks - 1)
+    def _():
+        advance(firsts)
+
+    @pl.when(step == blocks)
+    def _():
+        for h in range(H):
+            s = slice(64 * h, 64 * h + 64)
+            dk_ref[s, :] = dka_ref[h].astype(BF16)
+            dv_ref[s, :] = dva_ref[h].astype(BF16)
+            dkm_ref[s, :] = dkma_ref[h].astype(BF16)
+            dvm_ref[s, :] = dvma_ref[h].astype(BF16)
+        tok, dv, dvm = tok_ref[...], dv_ref[...], dvm_ref[...]
+        acc_ref[512:1024, :] = dot(dk_ref[...], tok, 1, 0) + dot(dkm_ref[...], memt_ref[...], 1, 1)
+        acc_ref[1024:1536, :] = dot(dv, tok, 1, 0) + dot(dvm, memt_ref[...], 1, 1)
+        sum_ref[:, 1:2] = jnp.sum(dv.astype(F32), axis=1, keepdims=True) + jnp.sum(
+            dvm.astype(F32), axis=1, keepdims=True
+        )
+
         def put(rows, lanes, value):
             late[:, :, :, :, rows, lanes] = value.reshape(4, 2, 2, 2, 16, value.shape[1])
 
         late_grads(dkm_ref, dvm_ref, vec_ref, bup_ref, wt_ref, acc_ref, sum_ref, put)
         for number, (rows, _) in zip(crossing[len(SUM_EARLY) :], SUM_LATE):
             cross(late, LATE, rows, number)
-        advance(firsts)
-
-    @pl.when(step >= half)
-    def _():
-        token_grads(gtok_ref, gfirst_ref, dq_ref, dk_ref, dv_ref, wt_ref)
-
-    @pl.when(step == half)
+
+    @pl.when(step > blocks)
+    def _():
+        rows = gtok_ref.shape[0]
+        here = pl.ds(pl.multiple_of((step - blocks - 1) * rows, 128), rows)
+        token_grads(gtok_ref, gfirst_ref, dq_ref.at[:, here], dk_ref.at[:, here], dv_ref.at[:, here], wt_ref)
+
+    @pl.when(step == blocks + 1)
     def _():
         for index, (rows, _) in enumerate(SUM_LATE):
             join(
@@ -1001,78 +1058,63 @@
             )
             next(lasts[index])
 
-    @pl.when(step == half + 1)
-    def _():
-        advance(firsts)
-
-    @pl.when(step == half + 2)
+    @pl.when(step == blocks + 3)
     def _():
         advance(lasts)
 
-    @pl.when(step == 2 * half - 1)
-    def _():
-        advance(firsts)
+    @pl.when(step == pl.num_programs(0) - 1)
+    def _():
         advance(lasts)
         advance(lasts)
         copies.finish()
 
 
-def plain_kernel(
-    half, tok_ref, dq_ref, dk_ref, dv_ref, dkm_ref, dvm_ref, gfirst_ref, vec_ref, bup_ref, wt_ref, memt_ref,
-    gtok_ref, late_ref, acc_ref, sum_ref,
-):
-    step = pl.program_id(0)
-
-    @pl.when(step < half)
-    def _():
-        weight_grads(step, tok_ref, dq_ref, dk_ref, dv_ref, dkm_ref, dvm_ref, memt_ref, acc_ref, sum_ref)
-
-    @pl.when(step == half - 1)
-    def _():
-        def put(rows, lanes, value):
-            late_ref[:, rows, lanes] = value.reshape(PARTS, 16, value.shape[1])
-
-        late_grads(dkm_ref, dvm_ref, vec_ref, bup_ref, wt_ref, acc_ref, sum_ref, put)
-
-    @pl.when(step >= half)
-    def _():
-        token_grads(gtok_ref, gfirst_ref, dq_ref, dk_ref, dv_ref, wt_ref)
-
-
-def tail(early, tokens, dq, dk, dv, dkm, dvm, gfirst, vec, bup, wt, memt, remote):
+def backward(seg2, counts, early, tokens, qa, ka, va, kmn, km, vmn, mgrad, lse, delta, gfirst, vec, bup, wt, memt, remote):
+    if not remote:
+        dq, dk, dv, dkm, dvm = attend_backward(seg2, counts, qa, ka, va, kmn, km, vmn, mgrad, lse, delta)
+        return tail(tokens, dq, dk, dv, dkm, dvm, gfirst, vec, bup, wt, memt)
     slots = tokens.shape[0]
     rb = 512
-    half = slots // rb
-
-    cols = pl.BlockSpec((512, rb), lambda i: (0, i % half))
-    later = pl.BlockSpec((rb, 512), lambda i: (jnp.maximum(i - half, 0), 0))
-    in_specs = [
-        pl.BlockSpec((rb, 512), lambda i: (jnp.minimum(i, half - 1), 0)),
-        cols, cols, cols, fixed(512, 128), fixed(512, 128), later,
-        fixed(8, 512), fixed(1, 2048), fixed(1536, 512), fixed(512, 128),
-    ]
-    args = (tokens, dq, dk, dv, dkm, dvm, gfirst, vec, bup, wt, memt)
-    gtok = jax.ShapeDtypeStruct((slots, 512), F32)
-    scratch = [pltpu.VMEM((1536, 512), F32), pltpu.VMEM((512, 128), F32)]
-    if not remote:
-        return pl.pallas_call(
-            functools.partial(plain_kernel, half),
-            grid=(2 * half,),
-            in_specs=in_specs,
-            out_specs=[later, fixed(PARTS, EARLY, 512)],
-            out_shape=[gtok, jax.ShapeDtypeStruct((PARTS, EARLY, 512), BF16)],
-            scratch_shapes=scratch,
-            compiler_params=params(),
-            name="tail",
-        )(*args)
+    blocks = slots // BQ
+    once = pl.Buffered(1)
+
+    def full(a):
+        return pl.BlockSpec(a.shape, lambda i: (0,) * len(a.shape), pipeline_mode=once)
+
+    def at(i):
+        return jnp.minimum(i, blocks - 1)
+
+    later = pl.BlockSpec((rb, 512), lambda i: (jnp.maximum(i - blocks - 1, 0), 0))
+    stat = pl.BlockSpec((H, BQ), lambda i: (0, at(i)))
+    score = pltpu.VMEM((H, BK, BQ), F32)
     return pl.pallas_call(
-        functools.partial(scatter_kernel, half),
-        grid=(2 * half,),
-        in_specs=in_specs + [pl.BlockSpec(memory_space=pl.ANY)],
+        functools.partial(scatter_kernel, blocks),
+        grid=(blocks + 1 + slots // rb,),
+        in_specs=[
+            pl.BlockSpec((H, HA, BQ), lambda i: (0, 0, at(i))),
+            full(ka), full(va), full(kmn), full(km), full(vmn),
+            pl.BlockSpec((512, BQ), lambda i: (0, at(i))), stat, stat,
+            full(tokens), later, full(vec), full(bup), full(wt), full(memt),
+            pl.BlockSpec(memory_space=pl.ANY),
+        ],
         out_specs=[later, fixed(ROWS, 512)],
-        out_shape=[gtok, jax.ShapeDtypeStruct((ROWS, 512), F32)],
-        scratch_shapes=scratch
-        + [
+        out_shape=[jax.ShapeDtypeStruct((slots, 512), F32), jax.ShapeDtypeStruct((ROWS, 512), F32)],
+        scratch_shapes=[
+            pltpu.VMEM((H, HA, BQ), BF16),
+            pltpu.VMEM((H, HA, BQ), BF16),
+            pltpu.VMEM((H, HD, BQ), F32),
+            pltpu.VMEM((H, HD, slots), F32),
+            pltpu.VMEM((H, HD, slots), F32),
+            pltpu.VMEM((H, HD, 128), F32),
+            pltpu.VMEM((H, HD, 128), F32),
+            score, score, score, score,
+            pltpu.VMEM((512, slots), BF16),
+            pltpu.VMEM((512, slots), BF16),
+            pltpu.VMEM((512, slots), BF16),
+            pltpu.VMEM((512, 128), BF16),
+            pltpu.VMEM((512, 128), BF16),
+            pltpu.VMEM((1536, 512), F32),
+            pltpu.VMEM((512, 128), F32),
             pltpu.VMEM((4, 2, 2, 2, EARLY, 512), BF16),
             pltpu.VMEM((4, 2, 2, ROWS, 512), BF16),
             pltpu.VMEM((4, 2, 2, ROWS, 512), BF16),
@@ -1082,8 +1124,55 @@
         ]
         + [pltpu.VMEM(shape, BF16) for shape in slot_shapes(SUM_PARTS).values()],
         compiler_params=params(collective_id=1, has_side_effects=True),
-        name="tail_scatter",
-    )(*args, early.reshape(4, 2, 2, 2, LATE, 512))
+        name="backward_scatter",
+    )(
+        qa, ka, va, kmn, km, vmn, mgrad, lse, delta, tokens, gfirst, vec, bup, wt, memt,
+        early.reshape(4, 2, 2, 2, LATE, 512),
+    )
+
+
+def plain_kernel(
+    half, tok_ref, dq_ref, dk_ref, dv_ref, dkm_ref, dvm_ref, gfirst_ref, vec_ref, bup_ref, wt_ref, memt_ref,
+    gtok_ref, late_ref, acc_ref, sum_ref,
+):
+    step = pl.program_id(0)
+
+    @pl.when(step < half)
+    def _():
+        weight_grads(step, tok_ref, dq_ref, dk_ref, dv_ref, dkm_ref, dvm_ref, memt_ref, acc_ref, sum_ref)
+
+    @pl.when(step == half - 1)
+    def _():
+        def put(rows, lanes, value):
+            late_ref[:, rows, lanes] = value.reshape(PARTS, 16, value.shape[1])
+
+        late_grads(dkm_ref, dvm_ref, vec_ref, bup_ref, wt_ref, acc_ref, sum_ref, put)
+
+    @pl.when(step >= half)
+    def _():
+        token_grads(gtok_ref, gfirst_ref, dq_ref, dk_ref, dv_ref, wt_ref)
+
+
+def tail(tokens, dq, dk, dv, dkm, dvm, gfirst, vec, bup, wt, memt):
+    slots = tokens.shape[0]
+    rb = 512
+    half = slots // rb
+    cols = pl.BlockSpec((512, rb), lambda i: (0, i % half))
+    later = pl.BlockSpec((rb, 512), lambda i: (jnp.maximum(i - half, 0), 0))
+    return pl.pallas_call(
+        functools.partial(plain_kernel, half),
+        grid=(2 * half,),
+        in_specs=[
+            pl.BlockSpec((rb, 512), lambda i: (jnp.minimum(i, half - 1), 0)),
+            cols, cols, cols, fixed(512, 128), fixed(512, 128), later,
+            fixed(8, 512), fixed(1, 2048), fixed(1536, 512), fixed(512, 128),
+        ],
+        out_specs=[later, fixed(PARTS, EARLY, 512)],
+        out_shape=[jax.ShapeDtypeStruct((slots, 512), F32), jax.ShapeDtypeStruct((PARTS, EARLY, 512), BF16)],
+        scratch_shapes=[pltpu.VMEM((1536, 512), F32), pltpu.VMEM((512, 128), F32)],
+        compiler_params=params(),
+        name="tail",
+    )(tokens, dq, dk, dv, dkm, dvm, gfirst, vec, bup, wt, memt)
 
 
 def unpack_kernel(sum_ref, wo, up, dn, wq, wk, wv, memory, b_up, *vectors):
@@ -1172,11 +1261,12 @@
     if n != PARTS:
         whole = pack_whole({k: lax.all_gather(v, "dp", axis=axis_of(k), tiled=True) for k, v in p.items()})
     found = projections(p, whole, tokens, segment, counts, mem_rows)
-    late, qa, ka, kn, vn, km, kmn, vmn, wt, memt, rows8, rbup, mixt, lse = found
+    late, qa, ka, va, km, kmn, vmn, wt, memt, rows8, rbup, mixt, lse = found
     seg2 = segment.reshape(slots // 128, 128)
     output, gfirst, mgrad, delta, early, vec, bup = middle(late, rows8, rbup, counts, mixt, tokens, cotangent)
-    dq, dk, dv, dkm, dvm = attend_backward(seg2, counts, qa, kn, ka, vn, kmn, km, vmn, mgrad, lse, delta)
-    gtok, sums = tail(early, tokens, dq, dk, dv, dkm, dvm, gfirst, vec, bup, wt, memt, n == PARTS)
+    gtok, sums = backward(
+        seg2, counts, early, tokens, qa, ka, va, kmn, km, vmn, mgrad, lse, delta, gfirst, vec, bup, wt, memt, n == PARTS
+    )
     if n == PARTS:
         grads = unpack(sums, mem_rows)
     else:

time: 241 us -> 232 us (0.963)
  Pallas kernels: 235 us -> 226 us
    pallas_call x2 -> x1, Pallas kernels: 108 us -> 100 us  [backward(): pl.pallas_call(functools.partial(scatter_kernel, blocks), grid=(blocks +...]
where the time goes in v6:
time: 232 us
  Pallas kernels  226 us (97%)
  local copies, waits for them, and re-layouts  4.64 us (2%)
    pallas_call x1, Pallas kernels, backward(): pl.pallas_call(functools.partial(scatter_kernel, blocks), grid=(blocks +...  100 us
    pallas_call x1, Pallas kernels, projections(): pl.pallas_call(functools.partial(gather_kernel, mem_rows, half), grid=(ha...  77.3 us
    pallas_call x1, Pallas kernels, middle(): pl.pallas_call(functools.partial(mid_kernel, rb), grid=(slots // rb,), in...  46.2 us
    unnamed x1, local copies, waits for them, and re-layouts  4.64 us

profile of v6, /device:TPU:0, one launch (start us, length us, event | category | flops | bytes accessed | tf_op | source)
XLA Modules:
  0.0 231.6 jit_solution(5381611878107339723)
XLA Ops:
  1.3 77.3 %gather_attend.1 = (bf16[4,2,2,2,144,512]{5,4,3,2,1,0:T(8,128)(2,1)}, bf16[8,80,2048]{2,1,0:T(8,128)(2,1)}, bf16[8,80,2048]{2,1,0:T(8,128)(2,1)}, bf16[8,80,2048...) custom-call(bf16[16,512]{1,0:T(8,128)(2,1)} %wq.1, ...), custom_call_target="tpu_custom_call" | custom-call | tf_op jit(solution)/shard_map/gather_attend/pallas_call | solution.py:404
  78.6 46.2 %middle.1 = (bf16[2048,512]{1,0:T(8,128)(2,1)}, f32[2048,512]{1,0:T(8,128)}, bf16[512,2048]{1,0:T(8,128)(2,1)}, f32[8,2048]{1,0:T(8,128)}, bf16[32,144,512]{2,1,...) custom-call(s32[1]{0:T(128)S(6)} %copy.39.cnt_ref, f32[8,512]{1,0:T(8,128)} %get-tuple-element.56.row_ref, ...), custom_call_target="tpu_custom_call" | custom-call | tf_op jit(solution)/shard_map/middle/pallas_call | solution.py:736
  124.7 100.4 %backward_scatter.1 = (f32[2048,512]{1,0:T(8,128)}, f32[208,512]{1,0:T(8,128)}) custom-call(bf16[8,80,2048]{2,1,0:T(8,128)(2,1)} %get-tuple-element.61.qa_ref, bf16[8,80,2048]{2,1,0:T(8,128)(2,1)} %get-tuple-element.62.ka_ref, bf16[8,80,2048]{2,1,0:T(8,128)(2,1)} %get-tuple-element.63.va_ref, bf16[8,32,128]{2,1,0:T(8,128)(2,1)} %get-tuple-element.64.kmn_ref, ...), custom_call_target="tpu_custom_call" | custom-call | tf_op jit(solution)/shard_map/backward_scatter/pallas_call | solution.py:1090
  225.1 1.8 unpack.1
  226.9 4.6 %copy.40 = f32[2048,512]{1,0:T(8,128)} copy(f32[2048,512]{1,0:T(8,128)} %get-tuple-element.113) | data formatting | bytes 8388608

commit v7 on v6

--- a/solution.py
+++ b/solution.py
@@ -188,7 +188,7 @@
 VECTORS = ("b_query", "b_value", "b_out", "gain_attn", "shift_attn", "b_down", "gain_ffn", "shift_ffn")
 EARLY = 64
 LATE = 144
-EARLY_PARTS = ((slice(0, 32), "zxy"), (slice(32, 64), "zyx"))
+EARLY_PARTS = ((slice(0, 16), "zxy"), (slice(16, 32), "zyx"), (slice(32, 48), "zxy"), (slice(48, 64), "zyx"))
 LATE_PARTS = (
     (slice(0, 48), "zxy"),
     (slice(48, 96), "zyx"),
@@ -917,9 +917,11 @@
     sum_ref[:, 1:2] += jnp.sum(dv.astype(F32), axis=1, keepdims=True)
 
 
-def late_grads(dkm_ref, dvm_ref, vec_ref, bup_ref, wt_ref, acc_ref, sum_ref, late):
-    for j in range(3):
-        late(slice(16 * j, 16 * j + 16), slice(0, 512), acc_ref[512 * j : 512 * j + 512, :].T.astype(BF16))
+def matrix_grad(j, acc_ref):
+    return acc_ref[512 * j : 512 * j + 512, :].T.astype(BF16)
+
+
+def small_grads(dkm_ref, dvm_ref, vec_ref, bup_ref, wt_ref, sum_ref, late):
     gmem = dot(wt_ref[512:1024, :], dkm_ref[...], 0, 0) + dot(wt_ref[1024:1536, :], dvm_ref[...], 0, 0)
     late(slice(48, 64), slice(0, 128), gmem.astype(BF16))
     lane = lax.broadcasted_iota(jnp.int32, (512, 128), 1)
@@ -1020,27 +1022,46 @@
     def _():
         advance(firsts)
 
+    def put(rows, lanes, value):
+        late[:, :, :, :, rows, lanes] = value.reshape(4, 2, 2, 2, 16, value.shape[1])
+
+    def depart(index):
+        cross(late, LATE, SUM_LATE[index][0], crossing[len(SUM_EARLY) + index])
+
+    def onward(index):
+        rows = SUM_LATE[index][0]
+        old = slice(rows.start - LATE, rows.stop - LATE)
+        join(
+            place, copies, parts_sum, lambda z: late[z, :, :, place.core, old], other, rows,
+            crossing[len(SUM_EARLY) + index],
+        )
+        next(lasts[index])
+
     @pl.when(step == blocks)
     def _():
-        for h in range(H):
-            s = slice(64 * h, 64 * h + 64)
-            dk_ref[s, :] = dka_ref[h].astype(BF16)
-            dv_ref[s, :] = dva_ref[h].astype(BF16)
-            dkm_ref[s, :] = dkma_ref[h].astype(BF16)
-            dvm_ref[s, :] = dvma_ref[h].astype(BF16)
-        tok, dv, dvm = tok_ref[...], dv_ref[...], dvm_ref[...]
-        acc_ref[512:1024, :] = dot(dk_ref[...], tok, 1, 0) + dot(dkm_ref[...], memt_ref[...], 1, 1)
-        acc_ref[1024:1536, :] = dot(dv, tok, 1, 0) + dot(dvm, memt_ref[...], 1, 1)
-        sum_ref[:, 1:2] = jnp.sum(dv.astype(F32), axis=1, keepdims=True) + jnp.sum(
-            dvm.astype(F32), axis=1, keepdims=True
+        put(slice(0, 16), slice(0, 512), matrix_grad(0, acc_ref))
+        depart(0)
+        tok = tok_ref[...]
+        for j, whole, part, memory, memory_part in (
+            (1, dka_ref, dk_ref, dkma_ref, dkm_ref),
+            (2, dva_ref, dv_ref, dvma_ref, dvm_ref),
+        ):
+            for h in range(H):
+                s = slice(64 * h, 64 * h + 64)
+                part[s, :] = whole[h].astype(BF16)
+                memory_part[s, :] = memory[h].astype(BF16)
+            acc_ref[512 * j : 512 * j + 512, :] = dot(part[...], tok, 1, 0) + dot(
+                memory_part[...], memt_ref[...], 1, 1
+            )
+            put(slice(16 * j, 16 * j + 16), slice(0, 512), matrix_grad(j, acc_ref))
+            depart(j)
+            onward(j - 1)
+        sum_ref[:, 1:2] = jnp.sum(dv_ref[...].astype(F32), axis=1, keepdims=True) + jnp.sum(
+            dvm_ref[...].astype(F32), axis=1, keepdims=True
         )
-
-        def put(rows, lanes, value):
-            late[:, :, :, :, rows, lanes] = value.reshape(4, 2, 2, 2, 16, value.shape[1])
-
-        late_grads(dkm_ref, dvm_ref, vec_ref, bup_ref, wt_ref, acc_ref, sum_ref, put)
-        for number, (rows, _) in zip(crossing[len(SUM_EARLY) :], SUM_LATE):
-            cross(late, LATE, rows, number)
+        small_grads(dkm_ref, dvm_ref, vec_ref, bup_ref, wt_ref, sum_ref, put)
+        depart(3)
+        onward(2)
 
     @pl.when(step > blocks)
     def _():
@@ -1050,17 +1071,15 @@
 
     @pl.when(step == blocks + 1)
     def _():
-        for index, (rows, _) in enumerate(SUM_LATE):
-            join(
-                place, copies, parts_sum,
-                lambda z, old=slice(rows.start - LATE, rows.stop - LATE): late[z, :, :, place.core, old],
-                other, rows, crossing[len(SUM_EARLY) + index],
-            )
-            next(lasts[index])
+        onward(3)
+
+    @pl.when(step == blocks + 2)
+    def _():
+        advance(lasts[0:2])
 
     @pl.when(step == blocks + 3)
     def _():
-        advance(lasts)
+        advance(lasts[2:4])
 
     @pl.when(step == pl.num_programs(0) - 1)
     def _():
@@ -1146,7 +1165,9 @@
         def put(rows, lanes, value):
             late_ref[:, rows, lanes] = value.reshape(PARTS, 16, value.shape[1])
 
-        late_grads(dkm_ref, dvm_ref, vec_ref, bup_ref, wt_ref, acc_ref, sum_ref, put)
+        for j in range(3):
+            put(slice(16 * j, 16 * j + 16), slice(0, 512), matrix_grad(j, acc_ref))
+        small_grads(dkm_ref, dvm_ref, vec_ref, bup_ref, wt_ref, sum_ref, put)
 
     @pl.when(step >= half)
     def _():
@@ -1175,7 +1196,15 @@
     )(tokens, dq, dk, dv, dkm, dvm, gfirst, vec, bup, wt, memt)
 
 
-def unpack_kernel(sum_ref, wo, up, dn, wq, wk, wv, memory, b_up, *vectors):
+def unpack_kernel(sum_ref, part_ref, gtok_ref, wo, up, dn, wq, wk, wv, memory, b_up, *rest):
+    vectors, (block, arrive, leave) = rest[:8], rest[8:]
+    count = arrive.shape[0]
+    rows = block.shape[0] // count
+    spans = [slice(rows * k, rows * k + rows) for k in range(count)]
+    loads = [pltpu.make_async_copy(part_ref.at[s], block.at[s], arrive.at[k]) for k, s in enumerate(spans)]
+    stores = [pltpu.make_async_copy(block.at[s], gtok_ref.at[s], leave.at[k]) for k, s in enumerate(spans)]
+    for load in loads:
+        load.start()
     me = lax.axis_index("dp")
     wo[...] = sum_ref[0:16]
     for c in range(4):
@@ -1192,22 +1221,35 @@
     lane = lax.broadcasted_iota(jnp.int32, (16, 256), 1)
     own = jnp.sum(jnp.where(row * 4 + lane // 64 == me, sum_ref[192:208, 256:512], 0.0), axis=0, keepdims=True)
     b_up[...] = own[:, 0:64] + own[:, 64:128] + own[:, 128:192] + own[:, 192:256]
-
-
-def unpack(sums, mem_rows):
+    for load, store in zip(loads, stores):
+        load.wait()
+        store.start()
+    for store in stores:
+        store.wait()
+
+
+def unpack(sums, part, mem_rows):
     shapes = [(16, 512), (16, 2048), (64, 512), (16, 512), (16, 512), (16, 512), (16, mem_rows), (1, 64)] + [(1, 16)] * 8
     found = pl.pallas_call(
         unpack_kernel,
-        out_shape=[jax.ShapeDtypeStruct(s, F32) for s in shapes],
+        in_specs=[pl.BlockSpec(memory_space=pltpu.VMEM), pl.BlockSpec(memory_space=pl.ANY)],
+        out_specs=[pl.BlockSpec(memory_space=pl.ANY)] + [pl.BlockSpec(memory_space=pltpu.VMEM)] * len(shapes),
+        out_shape=[jax.ShapeDtypeStruct(s, F32) for s in [part.shape] + shapes],
+        scratch_shapes=[
+            pltpu.VMEM(part.shape, F32),
+            pltpu.SemaphoreType.DMA((4,)),
+            pltpu.SemaphoreType.DMA((4,)),
+        ],
         compiler_params=params(),
         name="unpack",
-    )(sums)
+    )(sums, part)
+    gtok, found = found[0], found[1:]
     out = dict(zip(("w_out", "w_up", "w_down", "w_query", "w_key", "w_value", "memory"), found[:7]))
     out["memory"] = out["memory"].T
     out["b_up"] = found[7].reshape(64)
     for name, value in zip(VECTORS, found[8:]):
         out[name] = value.reshape(16)
-    return out
+    return gtok, out
 
 
 NAMES = (
@@ -1268,7 +1310,7 @@
         seg2, counts, early, tokens, qa, ka, va, kmn, km, vmn, mgrad, lse, delta, gfirst, vec, bup, wt, memt, n == PARTS
     )
     if n == PARTS:
-        grads = unpack(sums, mem_rows)
+        gtok, grads = unpack(sums, gtok, mem_rows)
     else:
         full = unpack_whole(early.astype(F32), sums.astype(F32), mem_rows)
         grads = {

time: 232 us -> 227 us (0.978)
  local copies, waits for them, and re-layouts: 4.64 us -> 0 us
    unnamed x1 -> x0, local copies, waits for them, and re-layouts: 4.64 us -> none
    pallas_call x1, Pallas kernels: 1.77 us -> 5.09 us  [unpack(): pl.pallas_call(unpack_kernel, in_specs=[pl.BlockSpec(memory_space=pltpu.V...]
where the time goes in v7:
time: 227 us
  Pallas kernels  225 us (99%)
    pallas_call x1, Pallas kernels, backward(): pl.pallas_call(functools.partial(scatter_kernel, blocks), grid=(blocks +...  98.7 us
    pallas_call x1, Pallas kernels, projections(): pl.pallas_call(functools.partial(gather_kernel, mem_rows, half), grid=(ha...  75.2 us
    pallas_call x1, Pallas kernels, middle(): pl.pallas_call(functools.partial(mid_kernel, rb), grid=(slots // rb,), in...  46.2 us
    pallas_call x1, Pallas kernels, unpack(): pl.pallas_call(unpack_kernel, in_specs=[pl.BlockSpec(memory_space=pltpu.V...  5.09 us

profile of v7, /device:TPU:0, one launch (start us, length us, event | category | flops | bytes accessed | tf_op | source)
XLA Modules:
  0.0 226.6 jit_solution(10173625415619669512)
XLA Ops:
  1.3 75.2 %gather_attend.1 = (bf16[4,2,2,2,144,512]{5,4,3,2,1,0:T(8,128)(2,1)}, bf16[8,80,2048]{2,1,0:T(8,128)(2,1)}, bf16[8,80,2048]{2,1,0:T(8,128)(2,1)}, bf16[8,80,2048...) custom-call(bf16[16,512]{1,0:T(8,128)(2,1)} %wq.1, ...), custom_call_target="tpu_custom_call" | custom-call | tf_op jit(solution)/shard_map/gather_attend/pallas_call | solution.py:404
  76.5 46.2 %middle.1 = (bf16[2048,512]{1,0:T(8,128)(2,1)}, f32[2048,512]{1,0:T(8,128)}, bf16[512,2048]{1,0:T(8,128)(2,1)}, f32[8,2048]{1,0:T(8,128)}, bf16[32,144,512]{2,1,...) custom-call(s32[1]{0:T(128)S(6)} %copy.38.cnt_ref, f32[8,512]{1,0:T(8,128)} %get-tuple-element.57.row_ref, ...), custom_call_target="tpu_custom_call" | custom-call | tf_op jit(solution)/shard_map/middle/pallas_call | solution.py:736
  122.7 98.7 %backward_scatter.1 = (f32[2048,512]{1,0:T(8,128)}, f32[208,512]{1,0:T(8,128)}) custom-call(bf16[8,80,2048]{2,1,0:T(8,128)(2,1)} %get-tuple-element.62.qa_ref, bf16[8,80,2048]{2,1,0:T(8,128)(2,1)} %get-tuple-element.63.ka_ref, bf16[8,80,2048]{2,1,0:T(8,128)(2,1)} %get-tuple-element.64.va_ref, bf16[8,32,128]{2,1,0:T(8,128)(2,1)} %get-tuple-element.65.kmn_ref, ...), custom_call_target="tpu_custom_call" | custom-call | tf_op jit(solution)/shard_map/backward_scatter/pallas_call | solution.py:1109
  221.3 5.1 %unpack.1 = (f32[2048,512]{1,0:T(8,128)}, f32[16,512]{1,0:T(8,128)}, f32[16,2048]{1,0:T(8,128)}, f32[64,512]{1,0:T(8,128)}, f32[16,512]{1,0:T(8,128)}, /*index=5...) custom-call(f32[208,512]{1,0:T(8,128)} %get-tuple-element.77.sum_ref, ...), custom_call_target="tpu_custom_call" | custom-call | tf_op jit(solution)/shard_map/unpack/pallas_call | solution.py:1233

commit v8 on v7

--- a/solution.py
+++ b/solution.py
@@ -326,7 +326,7 @@
         end = jnp.minimum(block + reach + 1, slots // BQ)
         queries = qa_all.at[:, :, pl.ds(pl.multiple_of(block * BQ, BQ), BQ)]
         attend(
-            begin * (BQ // 128), (end - begin) * (BQ // BK), queries, ka_all, va_all, kmn_ref, vm_ref, mix_ref, lse_ref,
+            True, begin * (BQ // 128), (end - begin) * (BQ // BK), queries, ka_all, va_all, kmn_ref, vm_ref, mix_ref, lse_ref,
             acc_ref, m_ref, sa_ref, sb_ref,
         )
 
@@ -460,10 +460,12 @@
     return pl.ds(pl.multiple_of((begin + block * (BK // 128)) * 128, 128), BK)
 
 
-def pipelined(blocks, work, first, second):
-    @pl.when(blocks > 0)
-    def _():
-        work((0, first), None)
+def pipelined(blocks, work, first, second, started):
+    if not started:
+
+        @pl.when(blocks > 0)
+        def _():
+            work((0, first), None)
 
     pairs = jnp.maximum(blocks - 1, 0) // 2
 
@@ -484,7 +486,9 @@
         work(None, (j, first))
 
 
-def attend(begin, blocks, qa_ref, ka_ref, va_ref, kmn_ref, vm_ref, mix_ref, lse_ref, acc_ref, m_ref, sa_ref, sb_ref):
+def attend(
+    sure, begin, blocks, qa_ref, ka_ref, va_ref, kmn_ref, vm_ref, mix_ref, lse_ref, acc_ref, m_ref, sa_ref, sb_ref
+):
     def weights(h, s):
         old = m_ref[h : h + 1, :]
         top = jnp.maximum(old, jnp.max(s, axis=0, keepdims=True))
@@ -503,12 +507,14 @@
                 m_ref[h - 1 : h, :] = top
 
     scores = [dot(kmn_ref[h, :, 0:HA], qa_ref[h], 1, 0) for h in range(H)]
+    if sure:
+        work((0, sa_ref), None)
     for h in range(H):
         top = jnp.max(scores[h], axis=0, keepdims=True)
         p = jnp.exp(scores[h] - top).astype(BF16)
         acc_ref[h] = dot(vm_ref[h, :, 0:MP], p, 1, 0)
         m_ref[h : h + 1, :] = top
-    pipelined(blocks, work, sa_ref, sb_ref)
+    pipelined(blocks, work, sa_ref, sb_ref, sure)
     for h in range(H):
         total = acc_ref[h, 64:65, :]
         mix_ref[64 * h : 64 * h + 64, :] = (acc_ref[h, 0:64, :] * (1.0 / total)).astype(BF16)
@@ -526,7 +532,7 @@
         key_ranges(seg_ref[...], cnt_ref[0], slots, range_ref)
 
     attend(
-        range_ref[0, step], range_ref[1, step], qa_ref, ka_ref, va_ref, kmn_ref, vm_ref, mix_ref, lse_ref,
+        False, range_ref[0, step], range_ref[1, step], qa_ref, ka_ref, va_ref, kmn_ref, vm_ref, mix_ref, lse_ref,
         acc_ref, m_ref, sa_ref, sb_ref,
     )
 
@@ -778,7 +784,7 @@
 
 
 def attend_back(
-    begin, blocks, qa_ref, ka_ref, va_ref, kmn_ref, km_ref, vmn_ref, do_ref, lse_ref, delta_ref,
+    sure, begin, blocks, qa_ref, ka_ref, va_ref, kmn_ref, km_ref, vmn_ref, do_ref, lse_ref, delta_ref,
     q2_ref, do2_ref, dqa_ref, dka_ref, dva_ref, dkma_ref, dvma_ref, sa_ref, ga_ref, sb_ref, gb_ref,
 ):
     frow = lax.broadcasted_iota(jnp.int32, (16, BQ), 0)
@@ -810,13 +816,17 @@
                 dka_ref[h - 1, :, ks] += dot(q2_ref[h - 1, 0:64, :], ds, 1, 1)
                 dqa_ref[h - 1] += dot(ka_ref[h - 1, 0:64, ks], ds, 1, 0)
 
-    ps = [jnp.exp(dot(kmn_ref[h, :, 0:HA], q2_ref[h], 1, 0)) for h in range(H)]
-    dss = [(ps[h] * dot(vmn_ref[h, :, 0:HA], do2_ref[h], 1, 0)).astype(BF16) for h in range(H)]
+    ps = [dot(kmn_ref[h, :, 0:HA], q2_ref[h], 1, 0) for h in range(H)]
+    dps = [dot(vmn_ref[h, :, 0:HA], do2_ref[h], 1, 0) for h in range(H)]
+    if sure:
+        work((0, (sa_ref, ga_ref)), None)
+    ps = [jnp.exp(p) for p in ps]
+    dss = [(p * dp).astype(BF16) for p, dp in zip(ps, dps)]
     for h in range(H):
         dvma_ref[h, :, 0:MP] += dot(do2_ref[h, 0:64, :], ps[h].astype(BF16), 1, 1)
         dkma_ref[h, :, 0:MP] += dot(q2_ref[h, 0:64, :], dss[h], 1, 1)
         dqa_ref[h] = dot(km_ref[h, 0:64, 0:MP], dss[h], 1, 0)
-    pipelined(blocks, work, (sa_ref, ga_ref), (sb_ref, gb_ref))
+    pipelined(blocks, work, (sa_ref, ga_ref), (sb_ref, gb_ref), sure)
 
 
 def bwd_kernel(
@@ -833,7 +843,7 @@
             ref[...] = jnp.zeros_like(ref)
 
     attend_back(
-        range_ref[0, step], range_ref[1, step], qa_ref, ka_ref, va_ref, kmn_ref, km_ref, vmn_ref, do_ref, lse_ref,
+        False, range_ref[0, step], range_ref[1, step], qa_ref, ka_ref, va_ref, kmn_ref, km_ref, vmn_ref, do_ref, lse_ref,
         delta_ref, q2_ref, do2_ref, dqa_ref, dka_ref, dva_ref, dkma_ref, dvma_ref, sa_ref, ga_ref, sb_ref, gb_ref,
     )
     for h in range(H):
@@ -943,10 +953,10 @@
 
 def scatter_kernel(
     blocks, qa_ref, ka_ref, va_ref, kmn_ref, km_ref, vmn_ref, do_ref, lse_ref, delta_ref,
-    tok_ref, gfirst_ref, vec_ref, bup_ref, wt_ref, memt_ref, early_ref, gtok_ref, out_ref,
+    tok_hbm, gfirst_ref, vec_ref, bup_ref, wt_hbm, memt_ref, early_ref, gtok_ref, out_ref,
     q2_ref, do2_ref, dqa_ref, dka_ref, dva_ref, dkma_ref, dvma_ref, sa_ref, ga_ref, sb_ref, gb_ref,
     dq_ref, dk_ref, dv_ref, dkm_ref, dvm_ref,
-    acc_ref, sum_ref, late, parts_sum, other, send, recv, local, *landing,
+    tok_ref, wt_ref, acc_ref, sum_ref, late, parts_sum, other, send, recv, local, fetch, *landing,
 ):
     step = pl.program_id(0)
     place = Place()
@@ -965,6 +975,12 @@
             early_ref.at[:, :, :, place.core, rows], parts_sum.at[:, :, :, rows], local.at[index]
         )
 
+    def fetches():
+        return (
+            pltpu.make_async_copy(tok_hbm, tok_ref, fetch.at[0]),
+            pltpu.make_async_copy(wt_hbm, wt_ref, fetch.at[1]),
+        )
+
     def cross(source, base, rows, number):
         old = slice(rows.start - base, rows.stop - base)
         copies.start(
@@ -974,11 +990,12 @@
     @pl.when(step == 0)
     def _():
         place.greet()
+        for copy in fetches():
+            copy.start()
         for index in range(len(SUM_EARLY)):
             load(index).start()
         for ref in (dka_ref, dva_ref, dkma_ref, dvma_ref, sum_ref):
             ref[...] = jnp.zeros_like(ref)
-        acc_ref[0:512, :] = jnp.zeros((512, 512), F32)
 
     @pl.when(step < blocks)
     def _():
@@ -986,19 +1003,18 @@
         begin = jnp.maximum(step - reach, 0)
         end = jnp.minimum(step + reach + 1, blocks)
         attend_back(
-            begin * (BQ // 128), (end - begin) * (BQ // BK), qa_ref, ka_ref, va_ref, kmn_ref, km_ref, vmn_ref,
+            True, begin * (BQ // 128), (end - begin) * (BQ // BK), qa_ref, ka_ref, va_ref, kmn_ref, km_ref, vmn_ref,
             do_ref, lse_ref, delta_ref, q2_ref, do2_ref, dqa_ref, dka_ref, dva_ref, dkma_ref, dvma_ref,
             sa_ref, ga_ref, sb_ref, gb_ref,
         )
         here = pl.ds(pl.multiple_of(step * BQ, BQ), BQ)
         for h in range(H):
             dq_ref[64 * h : 64 * h + 64, here] = (dqa_ref[h] * HD ** -0.5).astype(BF16)
-        dq = dq_ref[:, here]
-        acc_ref[0:512, :] += dot(dq, tok_ref[here, :], 1, 0)
-        sum_ref[:, 0:1] += jnp.sum(dq.astype(F32), axis=1, keepdims=True)
 
     @pl.when(step == 0)
     def _():
+        for copy in fetches():
+            copy.wait()
         place.met()
         for number, (rows, _) in zip(crossing, SUM_EARLY):
             cross(early_ref, 0, rows, number)
@@ -1039,9 +1055,10 @@
 
     @pl.when(step == blocks)
     def _():
+        tok = tok_ref[...]
+        acc_ref[0:512, :] = dot(dq_ref[...], tok, 1, 0)
         put(slice(0, 16), slice(0, 512), matrix_grad(0, acc_ref))
         depart(0)
-        tok = tok_ref[...]
         for j, whole, part, memory, memory_part in (
             (1, dka_ref, dk_ref, dkma_ref, dkm_ref),
             (2, dva_ref, dv_ref, dvma_ref, dvm_ref),
@@ -1056,6 +1073,7 @@
             put(slice(16 * j, 16 * j + 16), slice(0, 512), matrix_grad(j, acc_ref))
             depart(j)
             onward(j - 1)
+        sum_ref[:, 0:1] = jnp.sum(dq_ref[...].astype(F32), axis=1, keepdims=True)
         sum_ref[:, 1:2] = jnp.sum(dv_ref[...].astype(F32), axis=1, keepdims=True) + jnp.sum(
             dvm_ref[...].astype(F32), axis=1, keepdims=True
         )
@@ -1106,6 +1124,7 @@
     later = pl.BlockSpec((rb, 512), lambda i: (jnp.maximum(i - blocks - 1, 0), 0))
     stat = pl.BlockSpec((H, BQ), lambda i: (0, at(i)))
     score = pltpu.VMEM((H, BK, BQ), F32)
+    hbm = pl.BlockSpec(memory_space=pl.ANY)
     return pl.pallas_call(
         functools.partial(scatter_kernel, blocks),
         grid=(blocks + 1 + slots // rb,),
@@ -1113,8 +1132,8 @@
             pl.BlockSpec((H, HA, BQ), lambda i: (0, 0, at(i))),
             full(ka), full(va), full(kmn), full(km), full(vmn),
             pl.BlockSpec((512, BQ), lambda i: (0, at(i))), stat, stat,
-            full(tokens), later, full(vec), full(bup), full(wt), full(memt),
-            pl.BlockSpec(memory_space=pl.ANY),
+            hbm, later, full(vec), full(bup), hbm, full(memt),
+            hbm,
         ],
         out_specs=[later, fixed(ROWS, 512)],
         out_shape=[jax.ShapeDtypeStruct((slots, 512), F32), jax.ShapeDtypeStruct((ROWS, 512), F32)],
@@ -1132,6 +1151,8 @@
             pltpu.VMEM((512, slots), BF16),
             pltpu.VMEM((512, 128), BF16),
             pltpu.VMEM((512, 128), BF16),
+            pltpu.VMEM(tokens.shape, BF16),
+            pltpu.VMEM(wt.shape, BF16),
             pltpu.VMEM((1536, 512), F32),
             pltpu.VMEM((512, 128), F32),
             pltpu.VMEM((4, 2, 2, 2, EARLY, 512), BF16),
@@ -1140,6 +1161,7 @@
             pltpu.SemaphoreType.DMA((SUM_COPIES,)),
             pltpu.SemaphoreType.DMA((SUM_COPIES,)),
             pltpu.SemaphoreType.DMA((len(SUM_EARLY),)),
+            pltpu.SemaphoreType.DMA((2,)),
         ]
         + [pltpu.VMEM(shape, BF16) for shape in slot_shapes(SUM_PARTS).values()],
         compiler_params=params(collective_id=1, has_side_effects=True),
@@ -1196,16 +1218,19 @@
     )(tokens, dq, dk, dv, dkm, dvm, gfirst, vec, bup, wt, memt)
 
 
-def unpack_kernel(sum_ref, part_ref, gtok_ref, wo, up, dn, wq, wk, wv, memory, b_up, *rest):
-    vectors, (block, arrive, leave) = rest[:8], rest[8:]
+def unpack_kernel(sum_hbm, part_ref, gtok_ref, wo, up, dn, wq, wk, wv, memory, b_up, *rest):
+    vectors, (sum_ref, block, ready, arrive, leave) = rest[:8], rest[8:]
     count = arrive.shape[0]
     rows = block.shape[0] // count
     spans = [slice(rows * k, rows * k + rows) for k in range(count)]
     loads = [pltpu.make_async_copy(part_ref.at[s], block.at[s], arrive.at[k]) for k, s in enumerate(spans)]
     stores = [pltpu.make_async_copy(block.at[s], gtok_ref.at[s], leave.at[k]) for k, s in enumerate(spans)]
+    sums = pltpu.make_async_copy(sum_hbm, sum_ref, ready)
+    sums.start()
     for load in loads:
         load.start()
     me = lax.axis_index("dp")
+    sums.wait()
     wo[...] = sum_ref[0:16]
     for c in range(4):
         up[:, 512 * c : 512 * c + 512] = sum_ref[16 + 16 * c : 32 + 16 * c]
@@ -1232,11 +1257,13 @@
     shapes = [(16, 512), (16, 2048), (64, 512), (16, 512), (16, 512), (16, 512), (16, mem_rows), (1, 64)] + [(1, 16)] * 8
     found = pl.pallas_call(
         unpack_kernel,
-        in_specs=[pl.BlockSpec(memory_space=pltpu.VMEM), pl.BlockSpec(memory_space=pl.ANY)],
+        in_specs=[pl.BlockSpec(memory_space=pl.ANY)] * 2,
         out_specs=[pl.BlockSpec(memory_space=pl.ANY)] + [pl.BlockSpec(memory_space=pltpu.VMEM)] * len(shapes),
         out_shape=[jax.ShapeDtypeStruct(s, F32) for s in [part.shape] + shapes],
         scratch_shapes=[
+            pltpu.VMEM(sums.shape, F32),
             pltpu.VMEM(part.shape, F32),
+            pltpu.SemaphoreType.DMA,
             pltpu.SemaphoreType.DMA((4,)),
             pltpu.SemaphoreType.DMA((4,)),
         ],

time: 227 us -> 220 us (0.969)
  Pallas kernels: 225 us -> 219 us
    pallas_call x1, Pallas kernels: 98.7 us -> 94.4 us  [backward(): pl.pallas_call(functools.partial(scatter_kernel, blocks), grid=(blocks +...]
    pallas_call x1, Pallas kernels: 75.2 us -> 72.8 us  [projections(): pl.pallas_call(functools.partial(gather_kernel, mem_rows, half), grid=(ha...]
where the time goes in v8:
time: 220 us
  Pallas kernels  219 us (100%)
    pallas_call x1, Pallas kernels, backward(): pl.pallas_call(functools.partial(scatter_kernel, blocks), grid=(blocks +...  94.4 us
    pallas_call x1, Pallas kernels, projections(): pl.pallas_call(functools.partial(gather_kernel, mem_rows, half), grid=(ha...  72.8 us
    pallas_call x1, Pallas kernels, middle(): pl.pallas_call(functools.partial(mid_kernel, rb), grid=(slots // rb,), in...  46.2 us
    pallas_call x1, Pallas kernels, unpack(): pl.pallas_call(unpack_kernel, in_specs=[pl.BlockSpec(memory_space=pl.ANY)...  5.23 us

profile of v8, /device:TPU:0, one launch (start us, length us, event | category | flops | bytes accessed | tf_op | source)
XLA Modules:
  0.0 220.1 jit_solution(11963010385639809412)
XLA Ops:
  1.3 72.8 %gather_attend.1 = (bf16[4,2,2,2,144,512]{5,4,3,2,1,0:T(8,128)(2,1)}, bf16[8,80,2048]{2,1,0:T(8,128)(2,1)}, bf16[8,80,2048]{2,1,0:T(8,128)(2,1)}, bf16[8,80,2048...) custom-call(bf16[16,512]{1,0:T(8,128)(2,1)} %wq.1, ...), custom_call_target="tpu_custom_call" | custom-call | tf_op jit(solution)/shard_map/gather_attend/pallas_call | solution.py:404
  74.1 46.2 %middle.1 = (bf16[2048,512]{1,0:T(8,128)(2,1)}, f32[2048,512]{1,0:T(8,128)}, bf16[512,2048]{1,0:T(8,128)(2,1)}, f32[8,2048]{1,0:T(8,128)}, bf16[32,144,512]{2,1,...) custom-call(s32[1]{0:T(128)S(6)} %copy.38.cnt_ref, f32[8,512]{1,0:T(8,128)} %get-tuple-element.57.row_ref, ...), custom_call_target="tpu_custom_call" | custom-call | tf_op jit(solution)/shard_map/middle/pallas_call | solution.py:742
  120.3 94.4 %backward_scatter.1 = (f32[2048,512]{1,0:T(8,128)}, f32[208,512]{1,0:T(8,128)}) custom-call(bf16[8,80,2048]{2,1,0:T(8,128)(2,1)} %get-tuple-element.62.qa_ref, bf16[8,80,2048]{2,1,0:T(8,128)(2,1)} %get-tuple-element.63.ka_ref, bf16[8,80,2048]{2,1,0:T(8,128)(2,1)} %get-tuple-element.64.va_ref, bf16[8,32,128]{2,1,0:T(8,128)(2,1)} %get-tuple-element.65.kmn_ref, ...), custom_call_target="tpu_custom_call" | custom-call | tf_op jit(solution)/shard_map/backward_scatter/pallas_call | solution.py:1128
  214.7 5.2 %unpack.1 = (f32[2048,512]{1,0:T(8,128)}, f32[16,512]{1,0:T(8,128)}, f32[16,2048]{1,0:T(8,128)}, f32[64,512]{1,0:T(8,128)}, f32[16,512]{1,0:T(8,128)}, /*index=5...) custom-call(f32[208,512]{1,0:T(8,128)} %get-tuple-element.77.sum_hbm, ...), custom_call_target="tpu_custom_call" | custom-call | tf_op jit(solution)/shard_map/unpack/pallas_call | solution.py:1258

commit v9 on v8

--- a/solution.py
+++ b/solution.py
@@ -460,19 +460,29 @@
     return pl.ds(pl.multiple_of((begin + block * (BK // 128)) * 128, 128), BK)
 
 
-def pipelined(blocks, work, first, second, started):
+def pipelined(blocks, work, first, second, started, finish):
     if not started:
 
         @pl.when(blocks > 0)
         def _():
             work((0, first), None)
 
+        pl.when(blocks == 0)(finish)
+
     pairs = jnp.maximum(blocks - 1, 0) // 2
 
-    @pl.loop(0, pairs)
+    def two(j):
+        work((j + 1, second), (j, first))
+        work((j + 2, first), (j + 1, second))
+
+    @pl.loop(0, pairs // 2)
     def _(i):
-        work((2 * i + 1, second), (2 * i, first))
-        work((2 * i + 2, first), (2 * i + 1, second))
+        two(4 * i)
+        two(4 * i + 2)
+
+    @pl.when(pairs % 2 == 1)
+    def _():
+        two(2 * pairs - 2)
 
     j = 2 * pairs
 
@@ -480,10 +490,12 @@
     def _():
         work((j + 1, second), (j, first))
         work(None, (j + 1, second))
+        finish()
 
     @pl.when(blocks - j == 1)
     def _():
         work(None, (j, first))
+        finish()
 
 
 def attend(
@@ -514,11 +526,14 @@
         p = jnp.exp(scores[h] - top).astype(BF16)
         acc_ref[h] = dot(vm_ref[h, :, 0:MP], p, 1, 0)
         m_ref[h : h + 1, :] = top
-    pipelined(blocks, work, sa_ref, sb_ref, sure)
-    for h in range(H):
-        total = acc_ref[h, 64:65, :]
-        mix_ref[64 * h : 64 * h + 64, :] = (acc_ref[h, 0:64, :] * (1.0 / total)).astype(BF16)
-        lse_ref[h : h + 1, :] = m_ref[h : h + 1, :] + jnp.log(total)
+
+    def finish():
+        for h in range(H):
+            total = acc_ref[h, 64:65, :]
+            mix_ref[64 * h : 64 * h + 64, :] = (acc_ref[h, 0:64, :] * (1.0 / total)).astype(BF16)
+            lse_ref[h : h + 1, :] = m_ref[h : h + 1, :] + jnp.log(total)
+
+    pipelined(blocks, work, sa_ref, sb_ref, sure, finish)
 
 
 def fwd_kernel(
@@ -784,7 +799,7 @@
 
 
 def attend_back(
-    sure, begin, blocks, qa_ref, ka_ref, va_ref, kmn_ref, km_ref, vmn_ref, do_ref, lse_ref, delta_ref,
+    sure, finish, begin, blocks, qa_ref, ka_ref, va_ref, kmn_ref, km_ref, vmn_ref, do_ref, lse_ref, delta_ref,
     q2_ref, do2_ref, dqa_ref, dka_ref, dva_ref, dkma_ref, dvma_ref, sa_ref, ga_ref, sb_ref, gb_ref,
 ):
     frow = lax.broadcasted_iota(jnp.int32, (16, BQ), 0)
@@ -826,7 +841,7 @@
         dvma_ref[h, :, 0:MP] += dot(do2_ref[h, 0:64, :], ps[h].astype(BF16), 1, 1)
         dkma_ref[h, :, 0:MP] += dot(q2_ref[h, 0:64, :], dss[h], 1, 1)
         dqa_ref[h] = dot(km_ref[h, 0:64, 0:MP], dss[h], 1, 0)
-    pipelined(blocks, work, (sa_ref, ga_ref), (sb_ref, gb_ref), sure)
+    pipelined(blocks, work, (sa_ref, ga_ref), (sb_ref, gb_ref), sure, finish)
 
 
 def bwd_kernel(
@@ -842,12 +857,14 @@
         for ref in (dka_ref, dva_ref, dkma_ref, dvma_ref):
             ref[...] = jnp.zeros_like(ref)
 
+    def finish():
+        for h in range(H):
+            dq_ref[64 * h : 64 * h + 64, :] = (dqa_ref[h] * HD ** -0.5).astype(BF16)
+
     attend_back(
-        False, range_ref[0, step], range_ref[1, step], qa_ref, ka_ref, va_ref, kmn_ref, km_ref, vmn_ref, do_ref, lse_ref,
+        False, finish, range_ref[0, step], range_ref[1, step], qa_ref, ka_ref, va_ref, kmn_ref, km_ref, vmn_ref, do_ref, lse_ref,
         delta_ref, q2_ref, do2_ref, dqa_ref, dka_ref, dva_ref, dkma_ref, dvma_ref, sa_ref, ga_ref, sb_ref, gb_ref,
     )
-    for h in range(H):
-        dq_ref[64 * h : 64 * h + 64, :] = (dqa_ref[h] * HD ** -0.5).astype(BF16)
 
     @pl.when(step == pl.num_programs(0) - 1)
     def _():
@@ -1002,14 +1019,17 @@
         reach = LONGEST // BQ
         begin = jnp.maximum(step - reach, 0)
         end = jnp.minimum(step + reach + 1, blocks)
+        here = pl.ds(pl.multiple_of(step * BQ, BQ), BQ)
+
+        def finish():
+            for h in range(H):
+                dq_ref[64 * h : 64 * h + 64, here] = (dqa_ref[h] * HD ** -0.5).astype(BF16)
+
         attend_back(
-            True, begin * (BQ // 128), (end - begin) * (BQ // BK), qa_ref, ka_ref, va_ref, kmn_ref, km_ref, vmn_ref,
+            True, finish, begin * (BQ // 128), (end - begin) * (BQ // BK), qa_ref, ka_ref, va_ref, kmn_ref, km_ref, vmn_ref,
             do_ref, lse_ref, delta_ref, q2_ref, do2_ref, dqa_ref, dka_ref, dva_ref, dkma_ref, dvma_ref,
             sa_ref, ga_ref, sb_ref, gb_ref,
         )
-        here = pl.ds(pl.multiple_of(step * BQ, BQ), BQ)
-        for h in range(H):
-            dq_ref[64 * h : 64 * h + 64, here] = (dqa_ref[h] * HD ** -0.5).astype(BF16)
 
     @pl.when(step == 0)
     def _():

time: 220 us -> 218 us (level)
  Pallas kernels: 219 us -> 216 us
where the time goes in v9:
time: 218 us; the launch traced here: 217 us
  Pallas kernels  216 us (99%)
    pallas_call x1, Pallas kernels, backward(): pl.pallas_call(functools.partial(scatter_kernel, blocks), grid=(blocks +...  93.2 us
    pallas_call x1, Pallas kernels, projections(): pl.pallas_call(functools.partial(gather_kernel, mem_rows, half), grid=(ha...  71.4 us
    pallas_call x1, Pallas kernels, middle(): pl.pallas_call(functools.partial(mid_kernel, rb), grid=(slots // rb,), in...  46.2 us
    pallas_call x1, Pallas kernels, unpack(): pl.pallas_call(unpack_kernel, in_specs=[pl.BlockSpec(memory_space=pl.ANY)...  5.23 us

profile of v9, /device:TPU:0, one launch (start us, length us, event | category | flops | bytes accessed | tf_op | source)
XLA Modules:
  0.0 217.5 jit_solution(9081374805249747041)
XLA Ops:
  1.3 71.4 %gather_attend.1 = (bf16[4,2,2,2,144,512]{5,4,3,2,1,0:T(8,128)(2,1)}, bf16[8,80,2048]{2,1,0:T(8,128)(2,1)}, bf16[8,80,2048]{2,1,0:T(8,128)(2,1)}, bf16[8,80,2048...) custom-call(bf16[16,512]{1,0:T(8,128)(2,1)} %wq.1, ...), custom_call_target="tpu_custom_call" | custom-call | tf_op jit(solution)/shard_map/gather_attend/pallas_call | solution.py:404
  72.7 46.2 %middle.1 = (bf16[2048,512]{1,0:T(8,128)(2,1)}, f32[2048,512]{1,0:T(8,128)}, bf16[512,2048]{1,0:T(8,128)(2,1)}, f32[8,2048]{1,0:T(8,128)}, bf16[32,144,512]{2,1,...) custom-call(s32[1]{0:T(128)S(6)} %copy.38.cnt_ref, f32[8,512]{1,0:T(8,128)} %get-tuple-element.57.row_ref, ...), custom_call_target="tpu_custom_call" | custom-call | tf_op jit(solution)/shard_map/middle/pallas_call | solution.py:757
  118.8 93.2 %backward_scatter.1 = (f32[2048,512]{1,0:T(8,128)}, f32[208,512]{1,0:T(8,128)}) custom-call(bf16[8,80,2048]{2,1,0:T(8,128)(2,1)} %get-tuple-element.62.qa_ref, bf16[8,80,2048]{2,1,0:T(8,128)(2,1)} %get-tuple-element.63.ka_ref, bf16[8,80,2048]{2,1,0:T(8,128)(2,1)} %get-tuple-element.64.va_ref, bf16[8,32,128]{2,1,0:T(8,128)(2,1)} %get-tuple-element.65.kmn_ref, ...), custom_call_target="tpu_custom_call" | custom-call | tf_op jit(solution)/shard_map/backward_scatter/pallas_call | solution.py:1148
  212.1 5.2 %unpack.1 = (f32[2048,512]{1,0:T(8,128)}, f32[16,512]{1,0:T(8,128)}, f32[16,2048]{1,0:T(8,128)}, f32[64,512]{1,0:T(8,128)}, f32[16,512]{1,0:T(8,128)}, /*index=5...) custom-call(f32[208,512]{1,0:T(8,128)} %get-tuple-element.77.sum_hbm, ...), custom_call_target="tpu_custom_call" | custom-call | tf_op jit(solution)/shard_map/unpack/pallas_call | solution.py:1278

commit v10 on v9

--- a/solution.py
+++ b/solution.py
@@ -509,14 +509,14 @@
     def work(new, old):
         kept = {}
         for h in range(H + 1):
+            if h > 0 and old:
+                p, fade, top = kept.pop(h - 1)
+                acc_ref[h - 1] = acc_ref[h - 1] * fade + dot(va_ref[h - 1, :, key_slots(begin, old[0])], p, 1, 0)
+                m_ref[h - 1 : h, :] = top
             if h < H and new:
                 new[1][h] = dot(ka_ref[h, :, key_slots(begin, new[0])], qa_ref[h], 0, 0)
             if h < H and old:
                 kept[h] = weights(h, old[1][h])
-            if h > 0 and old:
-                p, fade, top = kept.pop(h - 1)
-                acc_ref[h - 1] = acc_ref[h - 1] * fade + dot(va_ref[h - 1, :, key_slots(begin, old[0])], p, 1, 0)
-                m_ref[h - 1 : h, :] = top
 
     scores = [dot(kmn_ref[h, :, 0:HA], qa_ref[h], 1, 0) for h in range(H)]
     if sure:
@@ -817,6 +817,12 @@
     def work(new, old):
         kept = {}
         for h in range(H + 1):
+            if h > 0 and old:
+                ks = key_slots(begin, old[0])
+                p, ds = kept.pop(h - 1)
+                dva_ref[h - 1, :, ks] += dot(do2_ref[h - 1, 0:64, :], p, 1, 1)
+                dka_ref[h - 1, :, ks] += dot(q2_ref[h - 1, 0:64, :], ds, 1, 1)
+                dqa_ref[h - 1] += dot(ka_ref[h - 1, 0:64, ks], ds, 1, 0)
             if h < H and new:
                 ks = key_slots(begin, new[0])
                 new[1][0][h] = dot(ka_ref[h, :, ks], q2_ref[h], 0, 0)
@@ -824,12 +830,6 @@
             if h < H and old:
                 p = jnp.exp(old[1][0][h])
                 kept[h] = p.astype(BF16), (p * old[1][1][h]).astype(BF16)
-            if h > 0 and old:
-                ks = key_slots(begin, old[0])
-                p, ds = kept.pop(h - 1)
-                dva_ref[h - 1, :, ks] += dot(do2_ref[h - 1, 0:64, :], p, 1, 1)
-                dka_ref[h - 1, :, ks] += dot(q2_ref[h - 1, 0:64, :], ds, 1, 1)
-                dqa_ref[h - 1] += dot(ka_ref[h - 1, 0:64, ks], ds, 1, 0)
 
     ps = [dot(kmn_ref[h, :, 0:HA], q2_ref[h], 1, 0) for h in range(H)]
     dps = [dot(vmn_ref[h, :, 0:HA], do2_ref[h], 1, 0) for h in range(H)]

time: 218 us -> 217 us (level)
  no operation moved by 1% of the time
where the time goes in v10:
time: 217 us; the launch traced here: 216 us
  Pallas kernels  215 us (99%)
    pallas_call x1, Pallas kernels, backward(): pl.pallas_call(functools.partial(scatter_kernel, blocks), grid=(blocks +...  92.1 us
    pallas_call x1, Pallas kernels, projections(): pl.pallas_call(functools.partial(gather_kernel, mem_rows, half), grid=(ha...  71.2 us
    pallas_call x1, Pallas kernels, middle(): pl.pallas_call(functools.partial(mid_kernel, rb), grid=(slots // rb,), in...  46.2 us
    pallas_call x1, Pallas kernels, unpack(): pl.pallas_call(unpack_kernel, in_specs=[pl.BlockSpec(memory_space=pl.ANY)...  5.23 us

profile of v10, /device:TPU:0, one launch (start us, length us, event | category | flops | bytes accessed | tf_op | source)
XLA Modules:
  0.0 216.3 jit_solution(9480539859022254736)
XLA Ops:
  1.3 71.2 %gather_attend.1 = (bf16[4,2,2,2,144,512]{5,4,3,2,1,0:T(8,128)(2,1)}, bf16[8,80,2048]{2,1,0:T(8,128)(2,1)}, bf16[8,80,2048]{2,1,0:T(8,128)(2,1)}, bf16[8,80,2048...) custom-call(bf16[16,512]{1,0:T(8,128)(2,1)} %wq.1, ...), custom_call_target="tpu_custom_call" | custom-call | tf_op jit(solution)/shard_map/gather_attend/pallas_call | solution.py:404
  72.6 46.2 %middle.1 = (bf16[2048,512]{1,0:T(8,128)(2,1)}, f32[2048,512]{1,0:T(8,128)}, bf16[512,2048]{1,0:T(8,128)(2,1)}, f32[8,2048]{1,0:T(8,128)}, bf16[32,144,512]{2,1,...) custom-call(s32[1]{0:T(128)S(6)} %copy.38.cnt_ref, f32[8,512]{1,0:T(8,128)} %get-tuple-element.57.row_ref, ...), custom_call_target="tpu_custom_call" | custom-call | tf_op jit(solution)/shard_map/middle/pallas_call | solution.py:757
  118.7 92.1 %backward_scatter.1 = (f32[2048,512]{1,0:T(8,128)}, f32[208,512]{1,0:T(8,128)}) custom-call(bf16[8,80,2048]{2,1,0:T(8,128)(2,1)} %get-tuple-element.62.qa_ref, bf16[8,80,2048]{2,1,0:T(8,128)(2,1)} %get-tuple-element.63.ka_ref, bf16[8,80,2048]{2,1,0:T(8,128)(2,1)} %get-tuple-element.64.va_ref, bf16[8,32,128]{2,1,0:T(8,128)(2,1)} %get-tuple-element.65.kmn_ref, ...), custom_call_target="tpu_custom_call" | custom-call | tf_op jit(solution)/shard_map/backward_scatter/pallas_call | solution.py:1148
  210.8 5.2 %unpack.1 = (f32[2048,512]{1,0:T(8,128)}, f32[16,512]{1,0:T(8,128)}, f32[16,2048]{1,0:T(8,128)}, f32[64,512]{1,0:T(8,128)}, f32[16,512]{1,0:T(8,128)}, /*index=5...) custom-call(f32[208,512]{1,0:T(8,128)} %get-tuple-element.77.sum_hbm, ...), custom_call_target="tpu_custom_call" | custom-call | tf_op jit(solution)/shard_map/unpack/pallas_call | solution.py:1278
